TPU v7x, 32 devices: a whole 2x2x4 slice. The times are simulated.
32 devices in a mesh: dp: 8 (over z, x), mp: 4 (over y, core).
Axes of the slice: x: 2, y: 2, z: 4, core: 2. Of those that a mesh axis runs over, the one named last changes fastest.
Arguments:
- big_copy: bfloat16 [4, 62208, 128], P('mp', 'dp')
- big_master: float32 [4, 62208, 128], P('mp', 'dp'), may hold values from -0.18 to 0.18
- big_first: float32 [4, 62208, 128], P('mp', 'dp'), may hold values from -9e-07 to 9e-07
- big_second: float32 [4, 62208, 128], P('mp', 'dp'), may hold values from 9.4e-16 to 1.5e-14
- ada_copy: bfloat16 [18579456], P(('dp', 'mp')), may hold values from -0.1875 to 0.1875
- ada_master: float32 [18579456], P(('dp', 'mp')), may hold values from -0.18 to 0.18
- ada_first: float32 [18579456], P(('dp', 'mp')), may hold values from -9e-07 to 9e-07
- ada_second: float32 [18579456], P(('dp', 'mp')), may hold values from 9.4e-16 to 1.5e-14
- rest_copy: bfloat16 [2813184], P(('dp', 'mp'))
- rest_master: float32 [2813184], P(('dp', 'mp')), may hold values from -0.18 to 0.18
- rest_first: float32 [2813184], P(('dp', 'mp')), may hold values from -9e-07 to 9e-07
- rest_second: float32 [2813184], P(('dp', 'mp')), may hold values from 9.4e-16 to 1.5e-14
- owner_tiles: int32 [62208], replicated, may hold values from 0 to 62207, as said below
- kept_patches: float32 [2, 32, 128, 16], P(None, ('dp', 'mp')), may hold values from -6 to 6
- kept_pos: int32 [2, 32, 128], P(None, ('dp', 'mp')), may hold values from 0 to 255, as said below
- timestep: int32 [2, 32], P(None, ('dp', 'mp')), may hold values from 0 to 999
- label: int32 [2, 32], P(None, ('dp', 'mp')), may hold values from 0 to 1000
- owner: int32 [2, 32], P(None, ('dp', 'mp')), may hold values from 0 to 7, as said below
- target: float32 [2, 32, 256, 16], P(None, ('dp', 'mp')), may hold values from -6 to 6
- step: int32 [1], replicated, may hold values from 1 to 20
Outputs:
- loss: float32 [1], replicated
- grad_norm: float32 [1], replicated
- big_master_new: float32 [4, 62208, 128], P('mp', 'dp')
- big_first_new: float32 [4, 62208, 128], P('mp', 'dp')
- big_second_new: float32 [4, 62208, 128], P('mp', 'dp')
- big_copy_new: bfloat16 [4, 62208, 128], P('mp', 'dp')
- ada_master_new: float32 [18579456], P(('dp', 'mp'))
- ada_first_new: float32 [18579456], P(('dp', 'mp'))
- ada_second_new: float32 [18579456], P(('dp', 'mp'))
- ada_copy_new: bfloat16 [18579456], P(('dp', 'mp'))
- rest_master_new: float32 [2813184], P(('dp', 'mp'))
- rest_first_new: float32 [2813184], P(('dp', 'mp'))
- rest_second_new: float32 [2813184], P(('dp', 'mp'))
- rest_copy_new: bfloat16 [2813184], P(('dp', 'mp'))
Inputs may be any that keep to these rules, and one draw needn't show every extreme that they name: `owner_tiles`: a permutation of 0 .. 62207. `kept_pos`: the 128 positions of one image are distinct. For each micro-batch b and each m there is one r in 0 .. 8 - 1 with owner[b, d * 4 + m] = d XOR r for every d.
All inputs are finite; a program needn't handle non-finite values.
Results may differ from a plain program's by a relative error of at most 0.007.
Values may be sent and summed in bfloat16 or wider, within the bound.
A program may use at most 512 MiB of HBM per device.

v0:
```python
import math

import jax
import jax.numpy as jnp
from jax import lax
from jax.sharding import PartitionSpec as P

D = 1152
HEADS = 16
HD = 72
FF = 4608
PD = 16
FREQ = 256
CLASSES = 1001
GRID = 16
SEQ = 256
KEEP = 128


EPS_NORM = 1e-06
MAX_NORM = 0.01
RATE = 0.02
DECAY = 0.1
BETA_ONE = 0.9
BETA_TWO = 0.999
ADAM_EPS = 1e-08
MASKED_WEIGHT = 0.1
highest = lax.Precision.HIGHEST


def partner_2(value, axis, stride):
    mask = 2**stride
    pairs = [(source, source ^ mask) for source in range(lax.axis_size(axis))]
    return lax.ppermute(value, axis, pairs)


def product(left, right):
    return jnp.dot(left, right, preferred_element_type=jnp.float32)


def normalize(values):
    center = values - jnp.mean(values, axis=-1, keepdims=True)
    spread = lax.rsqrt(jnp.mean(center * center, axis=-1, keepdims=True) + EPS_NORM)
    return (center * spread, spread)


def normalize_back(grad_normed, normed, spread):
    adjusted = grad_normed - jnp.mean(grad_normed, axis=-1, keepdims=True)
    adjusted = adjusted - normed * jnp.mean(grad_normed * normed, axis=-1, keepdims=True)
    return spread * adjusted


def position_table(columns):
    quarter = columns // 4
    omegas = 1.0 / 10000.0 ** (jnp.arange(quarter, dtype=jnp.float32) / quarter)
    places = jnp.arange(GRID * GRID, dtype=jnp.int32)

    def half_table(coords):
        angles = coords.astype(jnp.float32)[:, None] * omegas[None, :]
        return jnp.concatenate([jnp.sin(angles), jnp.cos(angles)], axis=1)

    return jnp.concatenate([half_table(places % GRID), half_table(places // GRID)], axis=1)


def time_features(stamp):
    halves = FREQ // 2
    frequency = jnp.exp(-math.log(10000.0) * jnp.arange(halves, dtype=jnp.float32) / halves)
    angles = stamp.astype(jnp.float32) * frequency
    return jnp.concatenate([jnp.cos(angles), jnp.sin(angles)])


def row_gather(values):
    return lax.all_gather(values, "mp", axis=0, tiled=True)


def row_sum(values):
    return lax.psum_scatter(values, "mp", scatter_dimension=0, tiled=True)


def route_bit(route, bit):
    return jnp.bitwise_and(jnp.right_shift(route, bit), 1) == 1


def route_ids(values, route, levels):
    for bit in range(levels):
        partner = partner_2(values, "dp", bit)
        values = jnp.where(route_bit(route, bit), partner, values)
    return values


def route_rows(values, route, levels):
    for bit in range(levels):
        partner = partner_2(values, "dp", bit)
        values = jnp.where(route_bit(route, bit), partner, values)
    return values


def route_back(values, route, levels):
    for bit in range(levels):
        partner = partner_2(values, "dp", bit)
        values = jnp.where(route_bit(route, bit), partner, values)
    return values


def unpack_big(flat, columns, groups):
    head_width = HEADS * HD // groups
    hidden_width = FF // groups
    shapes = [
        (columns, 3 * head_width),
        (head_width, columns),
        (columns, hidden_width),
        (hidden_width, columns),
    ]
    levels = []
    offset = 0
    for level_index in range(2):
        pieces = []
        for dims in shapes:
            length = dims[0] * dims[1]
            pieces.append(flat[offset : offset + length].reshape(dims))
            offset += length
        levels.append(tuple(pieces))
    return levels


def unpack_rest(flat, columns):
    matrix = flat.reshape(columns, -1).T
    counts = [PD, FREQ, columns, CLASSES, 1, PD]
    pieces = []
    offset = 0
    for count in counts:
        pieces.append(matrix[offset : offset + count])
        offset += count
    return (pieces[0], pieces[1], pieces[2], pieces[3], pieces[4][0], pieces[5].T)


def split_heads(packed, groups, rows):
    third = packed.shape[1] // 3
    return [
        packed[:, index * third : (index + 1) * third].reshape(groups, rows, third // HD, HD)
        for index in range(3)
    ]


def attention_probs(queries, key_rows):
    scores = jnp.einsum("gqhe,gkhe->ghqk", queries, key_rows, preferred_element_type=jnp.float32)
    return jax.nn.softmax(scores * HD ** (-0.5), axis=-1)


def block_forward(state, weights, modulate):
    qkv_weight, proj_weight, up_weight, down_weight = weights
    shift_one, scale_one, gate_one, shift_two, scale_two, gate_two = jnp.split(modulate, 6)
    rows = state.shape[0]
    normed_one, spread_one = normalize(state)
    full_one = row_gather((normed_one * (1.0 + scale_one) + shift_one).astype(jnp.bfloat16))
    groups = full_one.shape[0] // rows
    packed = product(full_one, qkv_weight).astype(jnp.bfloat16)
    queries, key_rows, value_rows = split_heads(packed, groups, rows)
    probs = attention_probs(queries, key_rows)
    mixed = jnp.einsum(
        "ghqk,gkhe->gqhe",
        probs.astype(jnp.bfloat16),
        value_rows,
        preferred_element_type=jnp.float32,
    )
    attended = mixed.astype(jnp.bfloat16).reshape(groups * rows, -1)
    branch_one = row_sum(product(attended, proj_weight))
    middle = state + gate_one * branch_one
    normed_two, spread_two = normalize(middle)
    full_two = row_gather((normed_two * (1.0 + scale_two) + shift_two).astype(jnp.bfloat16))
    hidden_pre = product(full_two, up_weight)
    activated = jax.nn.gelu(hidden_pre, approximate=True).astype(jnp.bfloat16)
    branch_two = row_sum(product(activated, down_weight))
    result = middle + gate_two * branch_two
    saved = (
        normed_one,
        spread_one,
        full_one,
        packed,
        attended,
        branch_one,
        normed_two,
        spread_two,
        full_two,
        hidden_pre,
        activated,
        branch_two,
    )
    return (result, saved)


def block_backward(grad_out, saved, weights, modulate):
    (
        normed_one,
        spread_one,
        full_one,
        packed,
        attended,
        branch_one,
        normed_two,
        spread_two,
        full_two,
        hidden_pre,
        activated,
        branch_two,
    ) = saved
    qkv_weight, proj_weight, up_weight, down_weight = weights
    shift_one, scale_one, gate_one, shift_two, scale_two, gate_two = jnp.split(modulate, 6)
    rows = grad_out.shape[0]
    groups = full_one.shape[0] // rows
    grad_gate_two = jnp.sum(grad_out * branch_two, axis=0)
    back_two = row_gather((gate_two * grad_out).astype(jnp.bfloat16))
    grad_down = product(activated.T, back_two)
    grad_act = product(back_two, down_weight.T)
    unused, gelu_back = jax.vjp(lambda pre: jax.nn.gelu(pre, approximate=True), hidden_pre)
    grad_pre = gelu_back(grad_act)[0].astype(jnp.bfloat16)
    grad_up = product(full_two.T, grad_pre)
    grad_hidden_two = row_sum(product(grad_pre, up_weight.T))
    grad_shift_two = jnp.sum(grad_hidden_two, axis=0)
    grad_scale_two = jnp.sum(grad_hidden_two * normed_two, axis=0)
    grad_middle = grad_out + normalize_back(
        grad_hidden_two * (1.0 + scale_two), normed_two, spread_two
    )
    grad_gate_one = jnp.sum(grad_middle * branch_one, axis=0)
    back_one = row_gather((gate_one * grad_middle).astype(jnp.bfloat16))
    grad_proj = product(attended.T, back_one)
    grad_attended = product(back_one, proj_weight.T).astype(jnp.bfloat16)
    queries, key_rows, value_rows = split_heads(packed, groups, rows)
    probs = attention_probs(queries, key_rows)
    grad_mixed = grad_attended.reshape(queries.shape)
    grad_probs = jnp.einsum(
        "gqhe,gkhe->ghqk", grad_mixed, value_rows, preferred_element_type=jnp.float32
    )
    grad_values = jnp.einsum(
        "ghqk,gqhe->gkhe",
        probs.astype(jnp.bfloat16),
        grad_mixed,
        preferred_element_type=jnp.float32,
    )
    grad_scores = (
        probs * (grad_probs - jnp.sum(grad_probs * probs, axis=-1, keepdims=True)) * HD ** (-0.5)
    )
    grad_scores = grad_scores.astype(jnp.bfloat16)
    grad_queries = jnp.einsum(
        "ghqk,gkhe->gqhe", grad_scores, key_rows, preferred_element_type=jnp.float32
    )
    grad_keys = jnp.einsum(
        "ghqk,gqhe->gkhe", grad_scores, queries, preferred_element_type=jnp.float32
    )
    grad_packed = jnp.concatenate(
        [
            grad_part.reshape(groups * rows, -1)
            for grad_part in (grad_queries, grad_keys, grad_values)
        ],
        axis=1,
    ).astype(jnp.bfloat16)
    grad_qkv = product(full_one.T, grad_packed)
    grad_hidden_one = row_sum(product(grad_packed, qkv_weight.T))
    grad_shift_one = jnp.sum(grad_hidden_one, axis=0)
    grad_scale_one = jnp.sum(grad_hidden_one * normed_one, axis=0)
    grad_state = grad_middle + normalize_back(
        grad_hidden_one * (1.0 + scale_one), normed_one, spread_one
    )
    grad_mod = jnp.concatenate(
        [
            grad_shift_one,
            grad_scale_one,
            grad_gate_one,
            grad_shift_two,
            grad_scale_two,
            grad_gate_two,
        ]
    )
    return (grad_state, grad_mod, (grad_qkv, grad_proj, grad_up, grad_down))


def condition(stamp, tag, time_one, time_two, table):
    features = time_features(stamp).astype(jnp.bfloat16)[None, :]
    pre_time = product(features, time_one)
    hidden_time = jax.nn.silu(pre_time).astype(jnp.bfloat16)
    cond_value = product(hidden_time, time_two)[0] + table[tag].astype(jnp.float32)
    signal = jax.nn.silu(cond_value).astype(jnp.bfloat16)
    return (signal, (features, pre_time, hidden_time, cond_value))


def condition_back(grad_signal, saved, time_two, tag, table_rows):
    features, pre_time, hidden_time, cond_value = saved
    unused, silu_back = jax.vjp(jax.nn.silu, cond_value)
    grad_cond = silu_back(grad_signal)[0]
    grad_time_two = hidden_time.astype(jnp.float32).T * grad_cond[None, :]
    grad_hidden = jnp.dot(time_two.astype(jnp.float32), grad_cond, precision=highest)
    unused_pre, pre_back = jax.vjp(jax.nn.silu, pre_time)
    grad_pre = pre_back(grad_hidden[None, :])[0]
    grad_time_one = features.astype(jnp.float32).T * grad_pre
    grad_table = (jnp.arange(table_rows, dtype=jnp.int32)[:, None] == tag) * grad_cond[None, :]
    return (grad_time_one, grad_time_two, grad_table)


def adam_update(grad, master, first, second, clip, count):
    scaled = grad * clip
    first = BETA_ONE * first + (1.0 - BETA_ONE) * scaled
    second = BETA_TWO * second + (1.0 - BETA_TWO) * scaled * scaled
    fix_one = 1.0 - BETA_ONE**count
    fix_two = 1.0 - BETA_TWO**count
    master = master - RATE * (
        first / fix_one / (jnp.sqrt(second / fix_two) + ADAM_EPS) + DECAY * master
    )
    return (master, first, second, master.astype(jnp.bfloat16))


def local(
    big_copy,
    big_master,
    big_first,
    big_second,
    ada_copy,
    ada_master,
    ada_first,
    ada_second,
    rest_copy,
    rest_master,
    rest_first,
    rest_second,
    owner_tiles,
    kept_patches,
    kept_pos,
    timestep,
    label,
    owner,
    target,
    step,
):
    groups = lax.axis_size("mp")
    ranks = lax.axis_size("dp")
    levels_dp = ranks.bit_length() - 1
    my_rank = lax.axis_index("dp")
    tiles = owner_tiles.shape[0]
    columns = D
    gathered = lax.all_gather(big_copy, "dp", axis=1, tiled=True)[0]
    inverse = jnp.zeros((tiles,), jnp.int32).at[owner_tiles].set(jnp.arange(tiles, dtype=jnp.int32))
    big_flat = jnp.take(gathered, inverse, axis=0).reshape(-1)
    ada_flat, rest_flat = (
        lax.all_gather(ada_copy, ("dp", "mp"), axis=0, tiled=True),
        lax.all_gather(rest_copy, ("dp", "mp"), axis=0, tiled=True),
    )
    levels = unpack_big(big_flat, columns, groups)
    ada_matrix = ada_flat.reshape(columns, 14 * columns)
    embed_weight, time_one, time_two, table, mask_token, head_weight = unpack_rest(
        rest_flat, columns
    )
    positions = position_table(columns)
    images = ranks * groups
    inv_count = 1.0 / (PD * kept_patches.shape[0] * images * KEEP)
    zeros_six = jnp.zeros((6 * columns,), jnp.bfloat16)
    zeros_eight = jnp.zeros((8 * columns,), jnp.bfloat16)

    def micro_step(carry, inputs):
        grads_big, grads_rest, loss_sum = carry
        patches, place, stamp, tag, dest, goal = inputs
        route = jnp.bitwise_xor(dest, my_rank)
        signal_enc, saved_enc = condition(stamp, tag, time_one, time_two, table)
        mod_enc = product(signal_enc[None, :], ada_matrix[:, : 6 * columns])[0]
        embedded = product(patches.astype(jnp.bfloat16), embed_weight) + jnp.take(
            positions, place, axis=0
        )
        enc_out, enc_saved = block_forward(embedded, levels[0], mod_enc)
        sent = enc_out.astype(jnp.bfloat16)
        meta = jnp.concatenate([place, stamp[None], tag[None]])
        got_meta = route_ids(meta, route, levels_dp)
        arrived = route_rows(sent, route, levels_dp)
        keep_rows = place.shape[0]
        dec_place = got_meta[:keep_rows]
        dec_tag = got_meta[keep_rows + 1]
        signal_dec, saved_dec = condition(got_meta[keep_rows], dec_tag, time_one, time_two, table)
        mod_dec = product(signal_dec[None, :], ada_matrix[:, 6 * columns :])[0]
        hits = jnp.arange(SEQ, dtype=jnp.int32)[:, None] == dec_place[None, :]
        kept = jnp.sum(hits.astype(jnp.float32), axis=1, keepdims=True)
        dec_in = (
            product(hits.astype(jnp.bfloat16), arrived)
            + (1.0 - kept) * mask_token.astype(jnp.float32)[None, :]
            + positions
        )
        dec_out, dec_saved = block_forward(dec_in, levels[1], mod_dec[: 6 * columns])
        final_shift = mod_dec[6 * columns : 7 * columns]
        final_scale = mod_dec[7 * columns :]
        normed_final, spread_final = normalize(dec_out)
        head_in = (normed_final * (1.0 + final_scale) + final_shift).astype(jnp.bfloat16)
        output = product(head_in, head_weight)
        error = output - goal
        weight = kept + MASKED_WEIGHT * (1.0 - kept)
        loss_part = jnp.sum(weight * error * error) * inv_count
        grad_output = (2.0 * inv_count * weight * error).astype(jnp.bfloat16)
        grad_head = product(head_in.T, grad_output)
        grad_head_in = product(grad_output, head_weight.T)
        grad_final = jnp.concatenate(
            [jnp.sum(grad_head_in, axis=0), jnp.sum(grad_head_in * normed_final, axis=0)]
        )
        grad_dec_out = normalize_back(
            grad_head_in * (1.0 + final_scale), normed_final, spread_final
        )
        grad_dec_in, grad_mod_dec, dec_grads = block_backward(
            grad_dec_out, dec_saved, levels[1], mod_dec[: 6 * columns]
        )
        grad_mask = jnp.sum((1.0 - kept) * grad_dec_in, axis=0)
        grad_arrived = jnp.take(grad_dec_in, dec_place, axis=0).astype(jnp.bfloat16)
        grad_sent = route_back(grad_arrived, route, levels_dp)
        grad_embedded, grad_mod_enc, enc_grads = block_backward(
            grad_sent.astype(jnp.float32), enc_saved, levels[0], mod_enc
        )
        grad_embed = jnp.dot(
            patches.astype(jnp.bfloat16).astype(jnp.float32).T, grad_embedded, precision=highest
        )
        vector_enc = grad_mod_enc.astype(jnp.bfloat16)
        vector_dec = jnp.concatenate([grad_mod_dec, grad_final]).astype(jnp.bfloat16)
        grad_signal_enc = product(ada_matrix[:, : 6 * columns], vector_enc)
        grad_signal_dec = product(ada_matrix[:, 6 * columns :], vector_dec)
        time_enc = condition_back(grad_signal_enc, saved_enc, time_two, tag, table.shape[0])
        time_dec = condition_back(grad_signal_dec, saved_dec, time_two, dec_tag, table.shape[0])
        rest_terms = [
            grad_embed,
            time_enc[0] + time_dec[0],
            time_enc[1] + time_dec[1],
            time_enc[2] + time_dec[2],
            grad_mask[None, :],
            grad_head.T,
        ]
        grads_rest = grads_rest + jnp.concatenate(rest_terms, axis=0)
        big_terms = [
            term.reshape(-1) for level_grads in (enc_grads, dec_grads) for term in level_grads
        ]
        grads_big = grads_big + jnp.concatenate(big_terms)
        signal_pair = jnp.stack([signal_enc, signal_dec])
        vector_pair = jnp.stack(
            [jnp.concatenate([vector_enc, zeros_eight]), jnp.concatenate([zeros_six, vector_dec])]
        )
        return ((grads_big, grads_rest, loss_sum + loss_part), (signal_pair, vector_pair))

    inputs = (
        kept_patches[:, 0],
        kept_pos[:, 0],
        timestep[:, 0],
        label[:, 0],
        owner[:, 0],
        target[:, 0],
    )
    start_carry = (
        jnp.zeros(big_flat.shape, jnp.float32),
        jnp.zeros((rest_flat.shape[0] // columns, columns), jnp.float32),
        jnp.zeros((), jnp.float32),
    )
    finals, factors = lax.scan(micro_step, start_carry, inputs)
    grads_big, grads_matrix, loss_sum = finals
    grads_rest = grads_matrix.T.reshape(-1)
    signal_rows = factors[0].reshape(-1, columns)
    vector_rows = factors[1].reshape(-1, 14 * columns)
    tile_part = jnp.take(grads_big.reshape(tiles, 128), owner_tiles, axis=0)
    owned_big = lax.psum_scatter(tile_part, "dp", scatter_dimension=0, tiled=True)
    local_ada = product(signal_rows.T, vector_rows).reshape(-1)
    owned_ada, owned_rest = (
        lax.psum_scatter(local_ada, ("dp", "mp"), scatter_dimension=0, tiled=True),
        lax.psum_scatter(grads_rest, ("dp", "mp"), scatter_dimension=0, tiled=True),
    )
    squares = (
        jnp.sum(owned_big * owned_big)
        + jnp.sum(owned_ada * owned_ada)
        + jnp.sum(owned_rest * owned_rest)
    )
    loss_total, square_total = lax.psum((loss_sum, squares), ("dp", "mp"))
    grad_norm = jnp.sqrt(square_total)
    clip = jnp.minimum(1.0, MAX_NORM / (grad_norm + 1e-06))
    count = step[0].astype(jnp.float32)
    big_out = adam_update(
        owned_big.reshape(big_master.shape), big_master, big_first, big_second, clip, count
    )
    ada_out = adam_update(owned_ada, ada_master, ada_first, ada_second, clip, count)
    rest_out = adam_update(owned_rest, rest_master, rest_first, rest_second, clip, count)
    return (
        loss_total.reshape(1),
        grad_norm.reshape(1),
        big_out[0],
        big_out[1],
        big_out[2],
        big_out[3],
        ada_out[0],
        ada_out[1],
        ada_out[2],
        ada_out[3],
        rest_out[0],
        rest_out[1],
        rest_out[2],
        rest_out[3],
    )


def solution(mesh):
    in_specs = (
        P("mp", "dp", None),
        P("mp", "dp", None),
        P("mp", "dp", None),
        P("mp", "dp", None),
        P(("dp", "mp")),
        P(("dp", "mp")),
        P(("dp", "mp")),
        P(("dp", "mp")),
        P(("dp", "mp")),
        P(("dp", "mp")),
        P(("dp", "mp")),
        P(("dp", "mp")),
        P(),
        P(None, ("dp", "mp"), None, None),
        P(None, ("dp", "mp"), None),
        P(None, ("dp", "mp")),
        P(None, ("dp", "mp")),
        P(None, ("dp", "mp")),
        P(None, ("dp", "mp"), None, None),
        P(),
    )
    out_specs = (
        P(),
        P(),
        P("mp", "dp", None),
        P("mp", "dp", None),
        P("mp", "dp", None),
        P("mp", "dp", None),
        P(("dp", "mp")),
        P(("dp", "mp")),
        P(("dp", "mp")),
        P(("dp", "mp")),
        P(("dp", "mp")),
        P(("dp", "mp")),
        P(("dp", "mp")),
        P(("dp", "mp")),
    )
    return jax.shard_map(local, mesh=mesh, in_specs=in_specs, out_specs=out_specs, check_vma=False)
```

profile of v0, /device:TPU:0, one launch (start us, length us, event | category | flops | bytes accessed | tf_op | source)
XLA Modules:
  0.0 4550.4 jit_solution(6090198136656134866)
XLA Ops:
  16.0 227.5 %scatter_custom_fusion = s32[62208]{0:T(1024)S(1)} fusion(s32[62208]{0:T(1024)S(1)} %compare_select_fusion.3, s32[62208]{0:T(1024)S(1)} %iota.68, s32[]{:T(128)} %constant.304.clone.1), kind=kCustom, calls=%fused_computation.350 | custom fusion | bytes 248836 | tf_op jit(solution)/shard_map/scatter | solution.py:340
  249.5 239.8 %all-reduce.10.cloned.1.call-done = bf16[2813184]{0:T(1024)(128)(2,1)} async-done(((bf16[2813184]{0:T(1024)(128)(2,1)}), bf16[2813184]{0:T(1024)(128)(2,1)}) %all-reduce.10.cloned.1.call-update) | async-done | bytes 5626384
  526.3 132.9 %gather_fusion.2 = bf16[62208,128]{1,0:T(8,128)(2,1)} fusion(bf16[62208,128]{1,0:T(8,128)(2,1)} %bitcast.394, s32[62464]{0:T(1024)} %pad_clamp_fusion.3), kind=kCustom, calls=%fused_computation.2 | custom fusion | bytes 32099328 | tf_op jit(solution)/shard_map/jit(_take)/gather | solution.py:341
  659.2 32.4 broadcast_select_fusion.9
  751.0 56.8 %reshape.644 = bf16[1152,16128]{1,0:T(8,128)(2,1)} reshape(bf16[18579456]{0:T(1024)(128)(2,1)} %all-gather.11.cloned.1.call-done) | data formatting | bytes 74317824 | tf_op jit(solution)/shard_map/reshape | solution.py:347
  807.8 1827.0 %while.22 = (s32[]{:T(128)}, f32[7962624]{0:T(1024)}, f32[2442,1152]{1,0:T(8,128)}, f32[]{:T(128)}, bf16[2,2,1152]{2,1,0:T(2,128)(2,1)}, /*index=5*/bf16[2,2,161...) while((s32[]{:T(128)}, f32[7962624]{0:T(1024)}, ...), condition=%wide.region_53.55_spmd.clone, body=%wide.region_1.54_spmd.clone.sunk | while | flops 38242885632 | bytes 1207063040 | solution.py:451
  875.4 33.2 reduce-scatter.12.cloned.1.call-done
  938.0 32.9 reduce-scatter.14.cloned.1.call-done
  1048.9 47.9 %reduce-scatter.16.cloned.1.call-done = f32[256,1152]{1,0:T(8,128)} async-done(((f32[1024,1152]{1,0:T(8,128)}), f32[256,1152]{1,0:T(8,128)}) %reduce-scatter.16.cloned.1.call-update) | async-done | bytes 1179664 | tf_op jit(solution)/shard_map/while/body/eval_jaxpr/reduce_scatter | solution.py:77
  1138.2 48.0 %reduce-scatter.18.cloned.1.call-done = f32[256,1152]{1,0:T(8,128)} async-done(((f32[1024,1152]{1,0:T(8,128)}), f32[256,1152]{1,0:T(8,128)}) %reduce-scatter.18.cloned.1.call-update) | async-done | bytes 1179664 | tf_op jit(solution)/shard_map/while/body/eval_jaxpr/reduce_scatter | solution.py:77
  1193.8 24.2 all-gather.23.cloned.1.call-done
  1233.8 47.9 %reduce-scatter.20.cloned.1.call-done = f32[256,1152]{1,0:T(8,128)} async-done(((f32[1024,1152]{1,0:T(8,128)}), f32[256,1152]{1,0:T(8,128)}) %reduce-scatter.20.cloned.1.call-update) | async-done | bytes 1179664 | tf_op jit(solution)/shard_map/while/body/eval_jaxpr/reduce_scatter | solution.py:77
  1287.7 24.0 all-gather.25.cloned.1.call-done
  1351.4 47.9 %reduce-scatter.22.cloned.1.call-done = f32[256,1152]{1,0:T(8,128)} async-done(((f32[1024,1152]{1,0:T(8,128)}), f32[256,1152]{1,0:T(8,128)}) %reduce-scatter.22.cloned.1.call-update) | async-done | bytes 1179664 | tf_op jit(solution)/shard_map/while/body/eval_jaxpr/reduce_scatter | solution.py:77
  1667.6 31.7 concatenate.111
  1778.5 33.2 reduce-scatter.12.cloned.1.call-done
  1841.1 33.0 reduce-scatter.14.cloned.1.call-done
  1952.0 47.9 %reduce-scatter.16.cloned.1.call-done = f32[256,1152]{1,0:T(8,128)} async-done(((f32[1024,1152]{1,0:T(8,128)}), f32[256,1152]{1,0:T(8,128)}) %reduce-scatter.16.cloned.1.call-update) | async-done | bytes 1179664 | tf_op jit(solution)/shard_map/while/body/eval_jaxpr/reduce_scatter | solution.py:77
  2003.1 24.0 all-gather.21.cloned.1.call-done
  2041.3 48.0 %reduce-scatter.18.cloned.1.call-done = f32[256,1152]{1,0:T(8,128)} async-done(((f32[1024,1152]{1,0:T(8,128)}), f32[256,1152]{1,0:T(8,128)}) %reduce-scatter.18.cloned.1.call-update) | async-done | bytes 1179664 | tf_op jit(solution)/shard_map/while/body/eval_jaxpr/reduce_scatter | solution.py:77
  2096.9 24.2 all-gather.23.cloned.1.call-done
  2137.0 48.0 %reduce-scatter.20.cloned.1.call-done = f32[256,1152]{1,0:T(8,128)} async-done(((f32[1024,1152]{1,0:T(8,128)}), f32[256,1152]{1,0:T(8,128)}) %reduce-scatter.20.cloned.1.call-update) | async-done | bytes 1179664 | tf_op jit(solution)/shard_map/while/body/eval_jaxpr/reduce_scatter | solution.py:77
  2254.6 47.9 %reduce-scatter.22.cloned.1.call-done = f32[256,1152]{1,0:T(8,128)} async-done(((f32[1024,1152]{1,0:T(8,128)}), f32[256,1152]{1,0:T(8,128)}) %reduce-scatter.22.cloned.1.call-update) | async-done | bytes 1179664 | tf_op jit(solution)/shard_map/while/body/eval_jaxpr/reduce_scatter | solution.py:77
  2527.0 31.9 select_add_fusion.4
  2580.6 31.7 concatenate.111
  2669.8 27.2 convolution_bitcast_fusion
  2697.1 65.2 %reshape.655 = f32[18579456]{0:T(1024)} reshape(f32[1152,16128]{1,0:T(8,128)} %convolution_bitcast_fusion) | data formatting | bytes 148635648 | tf_op jit(solution)/shard_map/reshape | solution.py:458
  2763.4 125.8 %gather_fusion.3 = f32[62208,128]{1,0:T(8,128)} fusion(f32[62208,128]{1,0:T(8,128)} %bitcast.393, s32[62464]{0:T(1024)S(1)} %pad_clamp_fusion.2), kind=kCustom, calls=%fused_computation.3 | custom fusion | bytes 63949824 | tf_op jit(solution)/shard_map/jit(_take)/gather | solution.py:456
  2889.1 33.5 broadcast_select_fusion.8
  2923.5 1040.8 %all-reduce.12.cloned.1.call-done = (f32[18579456]{0:T(1024)}, f32[2813184]{0:T(1024)}) async-done(((f32[18579456]{0:T(1024)}, f32[2813184]{0:T(1024)}), (f32[18579456]{0:T(1024)}, f32[2813184]{0:T(1024)})) %all-reduce.12.cloned.1.call-update) | async-done | bytes 85570576
  3968.8 508.5 %reduce-scatter.10.cloned.1.call-done = f32[7776,128]{1,0:T(8,128)} async-done(((f32[62208,128]{1,0:T(8,128)}), f32[7776,128]{1,0:T(8,128)}) %reduce-scatter.10.cloned.1.call-update) | async-done | bytes 3981328 | tf_op jit(solution)/shard_map/reduce_scatter | solution.py:457
  4483.0 40.3 all-reduce.5
  (1126 shorter events, 1266.1 us)
Async XLA Ops:
  8.0 481.4 %all-reduce.10.cloned.1.call-start = ((), (), s32[]{:S(2)}) async-start(), calls=%async_computation.12 | async-start | bytes 11255808
  14.7 511.7 %all-gather.13.cloned.1.call-start = ((), (), s32[]{:S(2)}) async-start(), calls=%async_computation.10 | async-start | bytes 17915904 | tf_op jit(solution)/shard_map/all_gather | solution.py:339
  15.3 735.7 %all-gather.11.cloned.1.call-start = ((), (), s32[]{:S(2)}) async-start(), calls=%async_computation.9 | async-start | bytes 38320128 | tf_op jit(solution)/shard_map/all_gather | solution.py:343
  910.9 60.0 %reduce-scatter.14.cloned.1.call-start = ((), (), s32[]{:S(2)}) async-start(), calls=%async_computation.17 | async-start | bytes 2949120 | tf_op jit(solution)/shard_map/while/body/eval_jaxpr/reduce_scatter | solution.py:77
  937.7 93.2 %all-gather.19.cloned.1.call-start = ((), (), s32[]{:S(2)}) async-start(), calls=%async_computation.18 | async-start | bytes 2949120 | tf_op jit(solution)/shard_map/while/body/eval_jaxpr/all_gather | solution.py:73
  1007.7 89.1 %reduce-scatter.16.cloned.1.call-start = ((), (), s32[]{:S(2)}) async-start(), calls=%async_computation.19 | async-start | bytes 5898240 | tf_op jit(solution)/shard_map/while/body/eval_jaxpr/reduce_scatter | solution.py:77
  1048.8 75.1 %all-gather.21.cloned.1.call-start = ((), (), s32[]{:S(2)}) async-start(), calls=%async_computation.20 | async-start | bytes 2949120 | tf_op jit(solution)/shard_map/while/body/eval_jaxpr/all_gather | solution.py:73
  1099.7 86.4 %reduce-scatter.18.cloned.1.call-start = ((), (), s32[]{:S(2)}) async-start(), calls=%async_computation.21 | async-start | bytes 5898240 | tf_op jit(solution)/shard_map/while/body/eval_jaxpr/reduce_scatter | solution.py:77
  1138.1 79.8 %all-gather.23.cloned.1.call-start = ((), (), s32[]{:S(2)}) async-start(), calls=%async_computation.22 | async-start | bytes 2949120 | tf_op jit(solution)/shard_map/while/body/eval_jaxpr/all_gather | solution.py:73
  1193.7 88.0 %reduce-scatter.20.cloned.1.call-start = ((), (), s32[]{:S(2)}) async-start(), calls=%async_computation.23 | async-start | bytes 5898240 | tf_op jit(solution)/shard_map/while/body/eval_jaxpr/reduce_scatter | solution.py:77
  1233.8 77.9 %all-gather.25.cloned.1.call-start = ((), (), s32[]{:S(2)}) async-start(), calls=%async_computation.24 | async-start | bytes 2949120 | tf_op jit(solution)/shard_map/while/body/eval_jaxpr/all_gather | solution.py:73
  1287.5 111.9 %reduce-scatter.22.cloned.1.call-start = ((), (), s32[]{:S(2)}) async-start(), calls=%async_computation.25 | async-start | bytes 5898240 | tf_op jit(solution)/shard_map/while/body/eval_jaxpr/reduce_scatter | solution.py:77
  1351.3 103.0 %all-gather.27.cloned.1.call-start = ((), (), s32[]{:S(2)}) async-start(), calls=%async_computation.26 | async-start | bytes 1474560 | tf_op jit(solution)/shard_map/while/body/eval_jaxpr/all_gather | solution.py:73
  1436.7 85.3 %reduce-scatter.24.cloned.1.call-start = ((), (), s32[]{:S(2)}) async-start(), calls=%async_computation.27 | async-start | bytes 2949120 | tf_op jit(solution)/shard_map/while/body/eval_jaxpr/reduce_scatter | solution.py:77
  1465.2 98.8 %all-gather.29.cloned.1.call-start = ((), (), s32[]{:S(2)}) async-start(), calls=%async_computation.28 | async-start | bytes 1474560 | tf_op jit(solution)/shard_map/while/body/eval_jaxpr/all_gather | solution.py:73
  1526.8 119.1 %reduce-scatter.26.cloned.1.call-start = ((), (), s32[]{:S(2)}) async-start(), calls=%async_computation.29 | async-start | bytes 2949120 | tf_op jit(solution)/shard_map/while/body/eval_jaxpr/reduce_scatter | solution.py:77
  1751.2 60.5 %reduce-scatter.12.cloned.1.call-start = ((), (), s32[]{:S(2)}) async-start(), calls=%async_computation.15 | async-start | bytes 2949120 | tf_op jit(solution)/shard_map/while/body/eval_jaxpr/reduce_scatter | solution.py:77
  1814.0 60.0 %reduce-scatter.14.cloned.1.call-start = ((), (), s32[]{:S(2)}) async-start(), calls=%async_computation.17 | async-start | bytes 2949120 | tf_op jit(solution)/shard_map/while/body/eval_jaxpr/reduce_scatter | solution.py:77
  1840.9 93.3 %all-gather.19.cloned.1.call-start = ((), (), s32[]{:S(2)}) async-start(), calls=%async_computation.18 | async-start | bytes 2949120 | tf_op jit(solution)/shard_map/while/body/eval_jaxpr/all_gather | solution.py:73
  1910.8 89.1 %reduce-scatter.16.cloned.1.call-start = ((), (), s32[]{:S(2)}) async-start(), calls=%async_computation.19 | async-start | bytes 5898240 | tf_op jit(solution)/shard_map/while/body/eval_jaxpr/reduce_scatter | solution.py:77
  1951.9 75.1 %all-gather.21.cloned.1.call-start = ((), (), s32[]{:S(2)}) async-start(), calls=%async_computation.20 | async-start | bytes 2949120 | tf_op jit(solution)/shard_map/while/body/eval_jaxpr/all_gather | solution.py:73
  2002.8 86.4 %reduce-scatter.18.cloned.1.call-start = ((), (), s32[]{:S(2)}) async-start(), calls=%async_computation.21 | async-start | bytes 5898240 | tf_op jit(solution)/shard_map/while/body/eval_jaxpr/reduce_scatter | solution.py:77
  2041.3 79.9 %all-gather.23.cloned.1.call-start = ((), (), s32[]{:S(2)}) async-start(), calls=%async_computation.22 | async-start | bytes 2949120 | tf_op jit(solution)/shard_map/while/body/eval_jaxpr/all_gather | solution.py:73
  2096.9 88.1 %reduce-scatter.20.cloned.1.call-start = ((), (), s32[]{:S(2)}) async-start(), calls=%async_computation.23 | async-start | bytes 5898240 | tf_op jit(solution)/shard_map/while/body/eval_jaxpr/reduce_scatter | solution.py:77
  2136.9 78.0 %all-gather.25.cloned.1.call-start = ((), (), s32[]{:S(2)}) async-start(), calls=%async_computation.24 | async-start | bytes 2949120 | tf_op jit(solution)/shard_map/while/body/eval_jaxpr/all_gather | solution.py:73
  2190.7 111.8 %reduce-scatter.22.cloned.1.call-start = ((), (), s32[]{:S(2)}) async-start(), calls=%async_computation.25 | async-start | bytes 5898240 | tf_op jit(solution)/shard_map/while/body/eval_jaxpr/reduce_scatter | solution.py:77
  2254.5 103.0 %all-gather.27.cloned.1.call-start = ((), (), s32[]{:S(2)}) async-start(), calls=%async_computation.26 | async-start | bytes 1474560 | tf_op jit(solution)/shard_map/while/body/eval_jaxpr/all_gather | solution.py:73
  2339.9 85.1 %reduce-scatter.24.cloned.1.call-start = ((), (), s32[]{:S(2)}) async-start(), calls=%async_computation.27 | async-start | bytes 2949120 | tf_op jit(solution)/shard_map/while/body/eval_jaxpr/reduce_scatter | solution.py:77
  2368.4 99.0 %all-gather.29.cloned.1.call-start = ((), (), s32[]{:S(2)}) async-start(), calls=%async_computation.28 | async-start | bytes 1474560 | tf_op jit(solution)/shard_map/while/body/eval_jaxpr/all_gather | solution.py:73
  2429.8 129.1 %reduce-scatter.26.cloned.1.call-start = ((), (), s32[]{:S(2)}) async-start(), calls=%async_computation.29 | async-start | bytes 2949120 | tf_op jit(solution)/shard_map/while/body/eval_jaxpr/reduce_scatter | solution.py:77
  2634.8 1329.4 %all-reduce.12.cloned.1.call-start = ((), (), s32[]{:S(2)}) async-start(), calls=%async_computation.13 | async-start | bytes 171147264
  2762.2 1715.1 %reduce-scatter.10.cloned.1.call-start = ((), (), s32[]{:S(2)}) async-start(), calls=%async_computation.11 | async-start | bytes 35831808 | tf_op jit(solution)/shard_map/reduce_scatter | solution.py:457
  (273 other events, 5165.4 us)
Sparse Core Ops, SparseCore 0:
  14.8 474.5 all-reduce.9
  875.4 33.0 reduce-scatter.11
  911.1 17.4 all-gather.16
  937.9 33.0 reduce-scatter.13
  1007.8 23.1 all-gather.18
  1048.9 47.8 reduce-scatter.15
  1099.8 24.0 all-gather.20
  1138.2 47.8 reduce-scatter.17
  1193.9 24.0 all-gather.22
  1233.9 47.8 reduce-scatter.19
  1287.6 24.0 all-gather.24
  1351.5 47.8 reduce-scatter.21
  1436.8 17.4 all-gather.26
  1465.3 33.0 reduce-scatter.23
  1526.9 17.2 all-gather.28
  1587.8 32.8 reduce-scatter.25
  1751.3 16.5 all-gather.14
  1778.6 33.0 reduce-scatter.11
  1814.2 17.4 all-gather.16
  1841.0 33.0 reduce-scatter.13
  1911.0 23.1 all-gather.18
  1952.1 47.8 reduce-scatter.15
  2002.9 24.0 all-gather.20
  2041.4 47.8 reduce-scatter.17
  2097.0 24.0 all-gather.22
  2137.0 47.8 reduce-scatter.19
  2190.8 24.0 all-gather.24
  2254.6 47.8 reduce-scatter.21
  2340.0 17.4 all-gather.26
  2368.5 33.0 reduce-scatter.23
  2429.9 17.3 all-gather.28
  2491.2 32.7 reduce-scatter.25
  (1 shorter events, 15.9 us)
Sparse Core Ops, SparseCore 1:
  17.3 233.7 all-gather.12
  253.9 220.3 all-gather.10
  2762.3 1201.8 all-reduce.11
  3968.6 508.6 reduce-scatter.9
where the time goes:
time: 4570 us; the launch traced here: 4550 us
  waiting for transfers between devices  2690 us (59%)
  local copies, waits for them, and re-layouts  1030 us (23%)
  matrix products  438 us (10%)
  other arithmetic  272 us (6%)
    unnamed x7, waiting for transfers between devices  1280 us
    reduce_scatter x16, waiting for transfers between devices, row_sum(): return lax.psum_scatter(values, 'mp', scatter_dimension=0, tiled=True)  516 us
    reduce_scatter x1, waiting for transfers between devices, local(): lax.psum_scatter(tile_part, 'dp', scatter_dimension=0, tiled=True)  509 us
    dot_general x75, matrix products, product(): return jnp.dot(left, right, preferred_element_type=jnp.float32)  350 us
    all_gather x16, waiting for transfers between devices, row_gather(): return lax.all_gather(values, 'mp', axis=0, tiled=True)  293 us
    scatter x1, local copies, waits for them, and re-layouts, local(): jnp.zeros((tiles,), jnp.int32).at[owner_tiles]  228 us
    gather x1, local copies, waits for them, and re-layouts, local(): big_flat = jnp.take(gathered, inverse, axis=0).reshape(-1)  133 us
    gather x1, local copies, waits for them, and re-layouts, local(): tile_part = jnp.take(grads_big.reshape(tiles, 128), owner_tiles, axis=0)  126 us
  transfers between devices with their start and end apart: 55, of which 43 were waited for; matrix products, arithmetic and copies ran while one was open for 22% of the time, Pallas kernels for 0%

commit v1 on v0

--- a/solution.py
+++ b/solution.py
@@ -1,8 +1,11 @@
+import functools
 import math
 
 import jax
 import jax.numpy as jnp
 from jax import lax
+from jax.experimental import pallas as pl
+from jax.experimental.pallas import tpu as pltpu
 from jax.sharding import PartitionSpec as P
 
 D = 1152
@@ -308,7 +311,7 @@
     return (master, first, second, master.astype(jnp.bfloat16))
 
 
-def local(
+def local_general(
     big_copy,
     big_master,
     big_first,
@@ -492,7 +495,638 @@
     )
 
 
+WORLD_AXES = ("dp", "mp")
+CHUNK_ROWS = 1136
+REST_ROWS = 2 * PD + FREQ + D + CLASSES + 1
+
+
+def tile_place(tiles, ranks):
+    counts = [count // ranks for count in matrix_tiles()]
+    layer_tiles = sum(matrix_tiles())
+    level = tiles // layer_tiles
+    inside = tiles % layer_tiles
+    dest = jnp.zeros_like(tiles)
+    slot = jnp.zeros_like(tiles)
+    start = 0
+    base = 0
+    for count, total in zip(counts, matrix_tiles()):
+        local_tile = inside - start
+        here = (local_tile >= 0) & (local_tile < total)
+        dest = jnp.where(here, local_tile // count, dest)
+        slot = jnp.where(here, base + level * count + local_tile % count, slot)
+        start += total
+        base += 2 * count
+    return dest, slot
+
+
+def matrix_tiles():
+    groups = 4
+    head_width = HEADS * HD // groups
+    hidden_width = FF // groups
+    sizes = [D * 3 * head_width, head_width * D, D * hidden_width, hidden_width * D]
+    return [size // 128 for size in sizes]
+
+
+def rank_within(dest, ranks):
+    n = dest.shape[0]
+    inner = 96
+    outer = n // inner
+    hot = (dest.reshape(outer, inner)[None] == jnp.arange(ranks)[:, None, None]).astype(jnp.bfloat16)
+    upto = (jnp.arange(inner)[:, None] < jnp.arange(inner)[None, :]).astype(jnp.bfloat16)
+    before = jnp.einsum("roi,ij->roj", hot, upto, preferred_element_type=jnp.float32)
+    totals = jnp.sum(hot.astype(jnp.float32), axis=2)
+    over = (jnp.arange(outer)[:, None] < jnp.arange(outer)[None, :]).astype(jnp.float32)
+    prior = jnp.dot(totals, over, precision=highest)
+    rank = jnp.sum(hot.astype(jnp.float32) * (before + prior[:, :, None]), axis=0)
+    return rank.astype(jnp.int32).reshape(n), jnp.sum(totals, axis=1).astype(jnp.int32)
+
+
+def widen(source, dest, rows):
+    step = 16
+    whole = rows // step
+
+    def body(i, unused):
+        at = pl.ds(pl.multiple_of(i * step, step), step)
+        dest[at, :] = source[at, :].astype(dest.dtype)
+        return unused
+
+    lax.fori_loop(0, whole, body, 0)
+
+
+def pack_kernel(n, capacity, pos_ref, slot_ref, fill_ref, x_ref, buf_ref, tag_ref, wide, sorted_rows):
+    ranks = fill_ref.shape[0]
+    total = ranks * capacity
+    widen(x_ref, wide, n)
+
+    def fill(r, unused):
+        def one(i, carry):
+            tag_ref[r * capacity + i] = n
+            return carry
+
+        return lax.fori_loop(fill_ref[r], capacity, one, unused)
+
+    lax.fori_loop(0, ranks, fill, 0)
+
+    def move(i, unused):
+        for j in range(16):
+            k = i * 16 + j
+            p = pos_ref[k]
+            sorted_rows[pl.ds(p, 1), :] = wide[pl.ds(k, 1), :]
+            tag_ref[p] = slot_ref[k]
+        return unused
+
+    lax.fori_loop(0, n // 16, move, 0)
+    widen(sorted_rows, buf_ref, total)
+
+
+def scatter_kernel(n, total, tag_ref, buf_ref, out_ref, wide):
+    widen(buf_ref, wide, total)
+
+    def move(i, unused):
+        for j in range(16):
+            k = i * 16 + j
+            out_ref[pl.ds(tag_ref[k], 1), :] = wide[pl.ds(k, 1), :]
+        return unused
+
+    lax.fori_loop(0, total // 16, move, 0)
+
+
+def gather_kernel(total, index_ref, x_ref, out_ref, wide_out):
+    def move(i, unused):
+        for j in range(16):
+            k = i * 16 + j
+            wide_out[pl.ds(k, 1), :] = x_ref[pl.ds(index_ref[k], 1), :]
+        return unused
+
+    lax.fori_loop(0, total // 16, move, 0)
+    widen(wide_out, out_ref, total)
+
+
+SMEM = pl.BlockSpec(memory_space=pltpu.SMEM)
+VMEM = pl.BlockSpec(memory_space=pltpu.VMEM)
+PARAMS = pltpu.CompilerParams(vmem_limit_bytes=48 * 1024 * 1024)
+
+
+def pack_rows(rows, pos, slot, fill, capacity):
+    n = rows.shape[0]
+    ranks = fill.shape[0]
+    total = ranks * capacity
+    return pl.pallas_call(
+        functools.partial(pack_kernel, n, capacity),
+        out_shape=(
+            jax.ShapeDtypeStruct((total, 128), jnp.bfloat16),
+            jax.ShapeDtypeStruct((total + 16,), jnp.int32),
+        ),
+        in_specs=[SMEM, SMEM, SMEM, VMEM],
+        out_specs=(VMEM, SMEM),
+        scratch_shapes=[
+            pltpu.VMEM((n, 128), jnp.float32),
+            pltpu.VMEM((total + 16, 128), jnp.float32),
+        ],
+        compiler_params=PARAMS,
+        name="pack_rows",
+    )(pos, slot, fill, rows)
+
+
+def scatter_rows(rows, tags, n):
+    total = rows.shape[0]
+    return pl.pallas_call(
+        functools.partial(scatter_kernel, n, total),
+        out_shape=jax.ShapeDtypeStruct((n + 16, 128), jnp.float32),
+        in_specs=[SMEM, VMEM],
+        out_specs=VMEM,
+        scratch_shapes=[pltpu.VMEM((total, 128), jnp.float32)],
+        compiler_params=PARAMS,
+        name="scatter_rows",
+    )(tags, rows)
+
+
+def gather_rows(rows, index, dtype):
+    total = index.shape[0]
+    return pl.pallas_call(
+        functools.partial(gather_kernel, total),
+        out_shape=jax.ShapeDtypeStruct((total, 128), dtype),
+        in_specs=[SMEM, VMEM],
+        out_specs=VMEM,
+        scratch_shapes=[pltpu.VMEM((total, 128), jnp.float32)],
+        compiler_params=PARAMS,
+        name="gather_rows",
+    )(index, rows)
+
+
+def swap_ranks(buf, ranks):
+    rest = buf.shape[1:]
+    split = buf.reshape((ranks, buf.shape[0] // ranks) + rest)
+    return lax.all_to_all(split, "dp", 0, 0).reshape(buf.shape)
+
+
+def round_positions(dest, rank, counts, capacity, turn):
+    ranks = counts.shape[0]
+    low = turn * capacity
+    inside = (rank >= low) & (rank < low + capacity)
+    pos = jnp.where(inside, dest * capacity + rank - low, ranks * capacity)
+    fill = jnp.clip(counts - low, 0, capacity)
+    return pos, fill, inside
+
+
+def tiles_to_slots(rows, dest, slot, rank, counts, rounds):
+    n = rows.shape[0]
+    ranks = counts.shape[0]
+
+    def turn_of(turn):
+        pos, fill, unused = round_positions(dest, rank, counts, CHUNK_ROWS, turn)
+        buf, tags = pack_rows(rows, pos, slot, fill, CHUNK_ROWS)
+        got = swap_ranks(buf, ranks)
+        got_tags = swap_ranks(tags[: ranks * CHUNK_ROWS], ranks)
+        return scatter_rows(got, got_tags, n), got_tags
+
+    first, tags = turn_of(0)
+
+    def more(carry):
+        turn, slots = carry
+        added, more_tags = turn_of(turn)
+        fresh = jnp.zeros((n + 16,), jnp.bool_).at[more_tags].set(True)
+        return turn + 1, jnp.where(fresh[:, None], added, slots)
+
+    unused, slots = lax.while_loop(lambda carry: carry[0] < rounds, more, (1, first))
+    return slots[:n], tags
+
+
+def slots_to_tiles(slots, tags, dest, slot, rank, counts, rounds):
+    n = dest.shape[0]
+    ranks = counts.shape[0]
+    padded = jnp.concatenate([slots, jnp.zeros((16, 128), slots.dtype)])
+
+    def turn_of(turn, turn_tags):
+        pos, unused, inside = round_positions(dest, rank, counts, CHUNK_ROWS, turn)
+        buf = gather_rows(padded, turn_tags, jnp.bfloat16)
+        got = swap_ranks(buf, ranks).astype(jnp.float32)
+        return gather_rows(got, jnp.minimum(pos, ranks * CHUNK_ROWS - 1), jnp.float32), inside
+
+    first, unused = turn_of(0, tags)
+
+    def more(carry):
+        turn, rows = carry
+        pos, fill, unused = round_positions(dest, rank, counts, CHUNK_ROWS, turn)
+        empty = jnp.full((ranks * CHUNK_ROWS + 1,), n, jnp.int32)
+        turn_tags = swap_ranks(empty.at[pos].set(slot)[:-1].at[:].get(), ranks)
+        added, inside = turn_of(turn, turn_tags)
+        return turn + 1, jnp.where(inside[:, None], added, rows)
+
+    unused, rows = lax.while_loop(lambda carry: carry[0] < rounds, more, (1, first))
+    return rows
+
+
+def slot_matrices(slots, ranks):
+    widths = [3 * HEADS * HD // 4, D, FF // 4, D]
+    levels = [[], []]
+    base = 0
+    for total, width in zip(matrix_tiles(), widths):
+        count = total // ranks
+        for level in range(2):
+            part = slots[base : base + count]
+            levels[level].append(part.reshape(count * 128 // width, width))
+            base += count
+    return levels
+
+
+def matrices_slots(levels):
+    parts = []
+    for index in range(4):
+        for level in range(2):
+            parts.append(levels[level][index].reshape(-1, 128))
+    return jnp.concatenate(parts)
+
+
+def gather_matrix(part):
+    whole = lax.all_gather(part, ("mp", "dp"), axis=0, tiled=False)
+    groups = lax.axis_size("mp")
+    return whole.reshape(groups, -1, part.shape[1])
+
+
+def scatter_matrix(parts):
+    ranks = lax.axis_size("dp")
+    stacked = jnp.stack([part.reshape(ranks, -1, part.shape[1]) for part in parts])
+    merged = stacked.reshape((-1,) + stacked.shape[2:])
+    return lax.psum_scatter(merged, ("mp", "dp"), scatter_dimension=0, tiled=False)
+
+
+def heads_of(packed, images):
+    third = packed[0].shape[1] // 3
+    pieces = []
+    for index in range(3):
+        cols = [
+            part[:, index * third : (index + 1) * third].reshape(images, -1, third // HD, HD)
+            for part in packed
+        ]
+        pieces.append(jnp.concatenate(cols, axis=2).transpose(0, 2, 1, 3))
+    return pieces
+
+
+def own_forward(state, weights, modulate):
+    qkv_weight, proj_weight, up_weight, down_weight = weights
+    groups = qkv_weight.shape[0]
+    images, rows, columns = state.shape
+    shift_one, scale_one, gate_one, shift_two, scale_two, gate_two = [
+        modulate[:, index, None, :] for index in range(6)
+    ]
+    normed_one, spread_one = normalize(state)
+    full_one = (normed_one * (1.0 + scale_one) + shift_one).astype(jnp.bfloat16)
+    flat_one = full_one.reshape(-1, columns)
+    packed = [product(flat_one, qkv_weight[m]).astype(jnp.bfloat16) for m in range(groups)]
+    queries, key_rows, value_rows = heads_of(packed, images)
+    scores = jnp.einsum(
+        "ghqe,ghke->ghqk", queries, key_rows, preferred_element_type=jnp.float32
+    )
+    probs = jax.nn.softmax(scores * HD ** (-0.5), axis=-1)
+    mixed = jnp.einsum(
+        "ghqk,ghke->ghqe",
+        probs.astype(jnp.bfloat16),
+        value_rows,
+        preferred_element_type=jnp.float32,
+    ).astype(jnp.bfloat16)
+    attended = mixed.transpose(0, 2, 1, 3).reshape(-1, columns)
+    branch_one = product(attended, proj_weight.reshape(-1, columns)).reshape(state.shape)
+    middle = state + gate_one * branch_one
+    normed_two, spread_two = normalize(middle)
+    full_two = (normed_two * (1.0 + scale_two) + shift_two).astype(jnp.bfloat16)
+    flat_two = full_two.reshape(-1, columns)
+    hidden_pre = [product(flat_two, up_weight[m]) for m in range(groups)]
+    activated = [jax.nn.gelu(pre, approximate=True).astype(jnp.bfloat16) for pre in hidden_pre]
+    branch_two = sum(product(activated[m], down_weight[m]) for m in range(groups))
+    branch_two = branch_two.reshape(state.shape)
+    result = middle + gate_two * branch_two
+    saved = (
+        normed_one,
+        spread_one,
+        flat_one,
+        queries,
+        key_rows,
+        value_rows,
+        attended,
+        branch_one,
+        normed_two,
+        spread_two,
+        flat_two,
+        hidden_pre,
+        activated,
+        branch_two,
+    )
+    return (result, saved)
+
+
+def own_backward(grad_out, saved, weights, modulate):
+    (
+        normed_one,
+        spread_one,
+        flat_one,
+        queries,
+        key_rows,
+        value_rows,
+        attended,
+        branch_one,
+        normed_two,
+        spread_two,
+        flat_two,
+        hidden_pre,
+        activated,
+        branch_two,
+    ) = saved
+    qkv_weight, proj_weight, up_weight, down_weight = weights
+    groups = qkv_weight.shape[0]
+    images, rows, columns = grad_out.shape
+    shift_one, scale_one, gate_one, shift_two, scale_two, gate_two = [
+        modulate[:, index, None, :] for index in range(6)
+    ]
+    grad_gate_two = jnp.sum(grad_out * branch_two, axis=1)
+    back_two = (gate_two * grad_out).astype(jnp.bfloat16).reshape(-1, columns)
+    grad_down = []
+    grad_up = []
+    grad_pres = []
+    for m in range(groups):
+        grad_down.append(product(activated[m].T, back_two).astype(jnp.bfloat16))
+        grad_act = product(back_two, down_weight[m].T)
+        unused, gelu_back = jax.vjp(lambda pre: jax.nn.gelu(pre, approximate=True), hidden_pre[m])
+        grad_pre = gelu_back(grad_act)[0].astype(jnp.bfloat16)
+        grad_up.append(product(flat_two.T, grad_pre).astype(jnp.bfloat16))
+        grad_pres.append(grad_pre)
+    grad_hidden_two = sum(product(grad_pres[m], up_weight[m].T) for m in range(groups))
+    grad_hidden_two = grad_hidden_two.reshape(grad_out.shape)
+    grad_shift_two = jnp.sum(grad_hidden_two, axis=1)
+    grad_scale_two = jnp.sum(grad_hidden_two * normed_two, axis=1)
+    grad_middle = grad_out + normalize_back(
+        grad_hidden_two * (1.0 + scale_two), normed_two, spread_two
+    )
+    grad_gate_one = jnp.sum(grad_middle * branch_one, axis=1)
+    back_one = (gate_one * grad_middle).astype(jnp.bfloat16).reshape(-1, columns)
+    grad_proj = product(attended.T, back_one).astype(jnp.bfloat16).reshape(groups, -1, columns)
+    grad_attended = product(back_one, proj_weight.reshape(-1, columns).T).astype(jnp.bfloat16)
+    grad_mixed = grad_attended.reshape(images, rows, HEADS, HD).transpose(0, 2, 1, 3)
+    scores = jnp.einsum(
+        "ghqe,ghke->ghqk", queries, key_rows, preferred_element_type=jnp.float32
+    )
+    probs = jax.nn.softmax(scores * HD ** (-0.5), axis=-1)
+    grad_probs = jnp.einsum(
+        "ghqe,ghke->ghqk", grad_mixed, value_rows, preferred_element_type=jnp.float32
+    )
+    grad_values = jnp.einsum(
+        "ghqk,ghqe->ghke",
+        probs.astype(jnp.bfloat16),
+        grad_mixed,
+        preferred_element_type=jnp.float32,
+    )
+    grad_scores = (
+        probs * (grad_probs - jnp.sum(grad_probs * probs, axis=-1, keepdims=True)) * HD ** (-0.5)
+    ).astype(jnp.bfloat16)
+    grad_queries = jnp.einsum(
+        "ghqk,ghke->ghqe", grad_scores, key_rows, preferred_element_type=jnp.float32
+    )
+    grad_keys = jnp.einsum(
+        "ghqk,ghqe->ghke", grad_scores, queries, preferred_element_type=jnp.float32
+    )
+    parts = [
+        part.astype(jnp.bfloat16).transpose(0, 2, 1, 3).reshape(images * rows, groups, -1)
+        for part in (grad_queries, grad_keys, grad_values)
+    ]
+    grad_qkv = []
+    grad_hidden_one = 0.0
+    for m in range(groups):
+        grad_packed = jnp.concatenate([part[:, m] for part in parts], axis=1)
+        grad_qkv.append(product(flat_one.T, grad_packed).astype(jnp.bfloat16))
+        grad_hidden_one = grad_hidden_one + product(grad_packed, qkv_weight[m].T)
+    grad_hidden_one = grad_hidden_one.reshape(grad_out.shape)
+    grad_shift_one = jnp.sum(grad_hidden_one, axis=1)
+    grad_scale_one = jnp.sum(grad_hidden_one * normed_one, axis=1)
+    grad_state = grad_middle + normalize_back(
+        grad_hidden_one * (1.0 + scale_one), normed_one, spread_one
+    )
+    grad_mod = jnp.concatenate(
+        [
+            grad_shift_one,
+            grad_scale_one,
+            grad_gate_one,
+            grad_shift_two,
+            grad_scale_two,
+            grad_gate_two,
+        ],
+        axis=1,
+    )
+    return (grad_state, grad_mod, (grad_qkv, [grad_proj[m] for m in range(groups)], grad_up, grad_down))
+
+
+def contract(left, right, left_axis, right_axis):
+    return lax.dot_general(
+        left,
+        right,
+        (((left_axis,), (right_axis,)), ((), ())),
+        preferred_element_type=jnp.float32,
+    )
+
+
+def contract_wide(left, right, left_axis, right_axis):
+    return lax.dot_general(
+        left.astype(jnp.float32),
+        right.astype(jnp.float32),
+        (((left_axis,), (right_axis,)), ((), ())),
+        precision=highest,
+        preferred_element_type=jnp.float32,
+    )
+
+
+def silu_back(values, grads):
+    unused, pull = jax.vjp(jax.nn.silu, values)
+    return pull(grads)[0]
+
+
+def local(
+    big_copy,
+    big_master,
+    big_first,
+    big_second,
+    ada_copy,
+    ada_master,
+    ada_first,
+    ada_second,
+    rest_copy,
+    rest_master,
+    rest_first,
+    rest_second,
+    owner_tiles,
+    kept_patches,
+    kept_pos,
+    timestep,
+    label,
+    owner,
+    target,
+    step,
+):
+    groups = lax.axis_size("mp")
+    ranks = lax.axis_size("dp")
+    world = groups * ranks
+    my_rank = lax.axis_index("dp")
+    micro = kept_patches.shape[0]
+    own_columns = D // world
+    columns = D
+
+    owned = big_copy.shape[1]
+    all_dest, unused_slot = tile_place(owner_tiles, ranks)
+    all_hot = all_dest.reshape(ranks, owned, 1) == jnp.arange(ranks)
+    rounds = (jnp.max(jnp.sum(all_hot.astype(jnp.int32), axis=1)) + CHUNK_ROWS - 1) // CHUNK_ROWS
+    own_tiles = lax.dynamic_slice(owner_tiles, (my_rank * owned,), (owned,))
+    dest, slot = tile_place(own_tiles, ranks)
+    rank, counts = rank_within(dest, ranks)
+    slots, tags = tiles_to_slots(big_copy[0], dest, slot, rank, counts, rounds)
+    slices = slot_matrices(slots.astype(jnp.bfloat16), ranks)
+    weights = [[gather_matrix(part) for part in level] for level in slices]
+
+    facts = jnp.concatenate([timestep[:, 0], label[:, 0]])
+    facts = lax.all_gather(facts, WORLD_AXES, axis=0, tiled=False)
+    stamps = facts[:, :micro].reshape(-1)
+    tags_all = facts[:, micro:].reshape(-1)
+    rest_own = rest_copy.reshape(own_columns, REST_ROWS)
+    edges = [0, PD, PD + FREQ, PD + FREQ + D, PD + FREQ + D + CLASSES, REST_ROWS]
+    win_t, one_t, two_t, table_t, tail_t = [
+        rest_own[:, edges[i] : edges[i + 1]] for i in range(5)
+    ]
+    ends = lax.all_gather(
+        jnp.concatenate([win_t, tail_t], axis=1), WORLD_AXES, axis=0, tiled=True
+    )
+    embed_weight = ends[:, :PD].T
+    mask_token = ends[:, PD].astype(jnp.float32)
+    head_weight = ends[:, PD + 1 :]
+    features = jax.vmap(time_features)(stamps).astype(jnp.bfloat16)
+    pre_time = contract(features, one_t, 1, 1)
+    hidden_own = jax.nn.silu(pre_time).astype(jnp.bfloat16)
+    hidden_all = lax.all_gather(hidden_own.T, WORLD_AXES, axis=0, tiled=True)
+    picks = (tags_all[:, None] == jnp.arange(CLASSES, dtype=jnp.int32)[None, :]).astype(
+        jnp.bfloat16
+    )
+    cond_own = contract(hidden_all, two_t, 0, 1) + contract(picks, table_t, 1, 1)
+    signal_own = jax.nn.silu(cond_own).astype(jnp.bfloat16)
+    ada_own = ada_copy.reshape(own_columns, 14 * columns)
+    mods = lax.psum_scatter(
+        product(signal_own, ada_own), WORLD_AXES, scatter_dimension=0, tiled=True
+    )
+    mod_enc = mods[:, : 6 * columns].reshape(micro, 6, columns)
+    mod_dec = mods[:, 6 * columns : 12 * columns].reshape(micro, 6, columns)
+    final_shift = mods[:, None, 12 * columns : 13 * columns]
+    final_scale = mods[:, None, 13 * columns :]
+
+    goals = lax.all_gather(target[:, 0], "dp", axis=0, tiled=False)
+    goal = jnp.stack([goals[owner[b, 0], b] for b in range(micro)])
+    positions = position_table(columns)
+    images = ranks * groups
+    inv_count = 1.0 / (PD * micro * images * KEEP)
+    place = kept_pos[:, 0]
+    patches = kept_patches[:, 0].astype(jnp.bfloat16)
+    hits = (
+        jnp.arange(SEQ, dtype=jnp.int32)[None, :, None] == place[:, None, :]
+    ).astype(jnp.float32)
+    hits_low = hits.astype(jnp.bfloat16)
+    kept = jnp.sum(hits, axis=2)[:, :, None]
+    embedded = product(patches.reshape(-1, PD), embed_weight).reshape(micro, KEEP, columns)
+    embedded = embedded + jnp.take(positions, place, axis=0)
+    enc_out, enc_saved = own_forward(embedded, weights[0], mod_enc)
+    sent = enc_out.astype(jnp.bfloat16)
+    dec_in = (
+        jnp.einsum("bpr,brd->bpd", hits_low, sent, preferred_element_type=jnp.float32)
+        + (1.0 - kept) * mask_token[None, None, :]
+        + positions[None]
+    )
+    dec_out, dec_saved = own_forward(dec_in, weights[1], mod_dec)
+    normed_final, spread_final = normalize(dec_out)
+    head_in = (normed_final * (1.0 + final_scale) + final_shift).astype(jnp.bfloat16)
+    flat_head = head_in.reshape(-1, columns)
+    output = product(flat_head, head_weight).reshape(micro, SEQ, PD)
+    error = output - goal
+    weight = kept + MASKED_WEIGHT * (1.0 - kept)
+    loss_sum = jnp.sum(weight * error * error) * inv_count
+
+    grad_output = (2.0 * inv_count * weight * error).astype(jnp.bfloat16).reshape(-1, PD)
+    grad_head = contract(grad_output, flat_head, 0, 0)
+    grad_head_in = product(grad_output, head_weight.T).reshape(dec_out.shape)
+    grad_final = jnp.concatenate(
+        [jnp.sum(grad_head_in, axis=1), jnp.sum(grad_head_in * normed_final, axis=1)], axis=1
+    )
+    grad_dec_out = normalize_back(grad_head_in * (1.0 + final_scale), normed_final, spread_final)
+    grad_dec_in, grad_mod_dec, dec_grads = own_backward(
+        grad_dec_out, dec_saved, weights[1], mod_dec
+    )
+    dec_sums = [scatter_matrix(parts) for parts in dec_grads]
+    grad_mask = jnp.sum((1.0 - kept) * grad_dec_in, axis=(0, 1))[None, :]
+    grad_sent = jnp.einsum(
+        "bpr,bpd->brd",
+        hits_low,
+        grad_dec_in.astype(jnp.bfloat16),
+        preferred_element_type=jnp.float32,
+    )
+    grad_embedded, grad_mod_enc, enc_grads = own_backward(
+        grad_sent, enc_saved, weights[0], mod_enc
+    )
+    enc_sums = [scatter_matrix(parts) for parts in enc_grads]
+    grad_embed = contract_wide(
+        patches.reshape(-1, PD), grad_embedded.reshape(-1, columns), 0, 0
+    )
+
+    vectors = jnp.concatenate([grad_mod_enc, grad_mod_dec, grad_final], axis=1)
+    vectors = lax.all_gather(vectors.astype(jnp.bfloat16), WORLD_AXES, axis=0, tiled=True)
+    owned_ada = contract(signal_own, vectors, 0, 0).reshape(-1)
+    grad_signal = contract(vectors, ada_own, 1, 1)
+    grad_cond = silu_back(cond_own, grad_signal)
+    grad_two_t = contract_wide(grad_cond, hidden_all, 0, 1)
+    grad_table_t = contract_wide(grad_cond, picks, 0, 0)
+    shared = jnp.concatenate(
+        [contract_wide(grad_cond, two_t, 1, 0), grad_embed, grad_mask, grad_head], axis=0
+    )
+    shared = shared.reshape(-1, world, own_columns).transpose(1, 0, 2)
+    shared = lax.psum_scatter(shared, WORLD_AXES, scatter_dimension=0, tiled=False)
+    count_all = micro * world
+    grad_pre = silu_back(pre_time, shared[:count_all])
+    grad_one_t = contract_wide(grad_pre, features, 0, 0)
+    ends_t = shared[count_all:].T
+    owned_rest = jnp.concatenate(
+        [ends_t[:, :PD], grad_one_t, grad_two_t, grad_table_t, ends_t[:, PD:]], axis=1
+    ).reshape(-1)
+
+    sums = matrices_slots(
+        [[part.astype(jnp.float32) for part in level] for level in (enc_sums, dec_sums)]
+    )
+    squares = jnp.sum(sums * sums) + jnp.sum(owned_ada * owned_ada) + jnp.sum(owned_rest * owned_rest)
+    totals = lax.psum(jnp.stack([loss_sum, squares]), WORLD_AXES)
+    owned_big = slots_to_tiles(sums, tags, dest, slot, rank, counts, rounds)
+    grad_norm = jnp.sqrt(totals[1])
+    clip = jnp.minimum(1.0, MAX_NORM / (grad_norm + 1e-06))
+    count = step[0].astype(jnp.float32)
+    big_out = adam_update(
+        owned_big.reshape(big_master.shape), big_master, big_first, big_second, clip, count
+    )
+    ada_out = adam_update(owned_ada, ada_master, ada_first, ada_second, clip, count)
+    rest_out = adam_update(owned_rest, rest_master, rest_first, rest_second, clip, count)
+    return (
+        totals[:1],
+        grad_norm.reshape(1),
+        big_out[0],
+        big_out[1],
+        big_out[2],
+        big_out[3],
+        ada_out[0],
+        ada_out[1],
+        ada_out[2],
+        ada_out[3],
+        rest_out[0],
+        rest_out[1],
+        rest_out[2],
+        rest_out[3],
+    )
+
+
+def whole_columns(mesh):
+    ranks, groups = mesh.shape["dp"], mesh.shape["mp"]
+    return groups == 4 and D % (ranks * groups) == 0 and ranks == 8
+
+
 def solution(mesh):
+    body = local if whole_columns(mesh) else local_general
     in_specs = (
         P("mp", "dp", None),
         P("mp", "dp", None),
@@ -531,4 +1165,4 @@
         P(("dp", "mp")),
         P(("dp", "mp")),
     )
-    return jax.shard_map(local, mesh=mesh, in_specs=in_specs, out_specs=out_specs, check_vma=False)
+    return jax.shard_map(body, mesh=mesh, in_specs=in_specs, out_specs=out_specs, check_vma=False)

time: 4570 us -> 2560 us (0.56)
  waiting for transfers between devices: 2690 us -> 1620 us
  local copies, waits for them, and re-layouts: 1030 us -> 224 us
  matrix products: 438 us -> 240 us
  blocking collectives: 40.3 us -> 232 us
  other arithmetic: 272 us -> 110 us
  Pallas kernels: 0 us -> 79.7 us
    unnamed x7 -> x23, waiting for transfers between devices: 1280 us -> 229 us
    reshape x44 -> x61, local copies, waits for them, and re-layouts: 296 us -> 19.6 us  [the longest x48 11.8 us: heads_of(): part[:, index * third:(index + 1) * third]]
    gather x6 -> x1, local copies, waits for them, and re-layouts: 267 us -> 2.2 us  [local(): embedded = embedded + jnp.take(positions, place, axis=0)]
    scatter x1 -> x0, local copies, waits for them, and re-layouts: 228 us -> none  [local(): jnp.zeros((tiles,), jnp.int32).at[owner_tiles]]
    all_gather x18 -> x9, waiting for transfers between devices: 293 us -> 501 us  [the longest x8 488 us: gather_matrix(): whole = lax.all_gather(part, ('mp', 'dp'), axis=0, tiled=False)]
    dot_general x75 -> x82, matrix products: 350 us -> 167 us  [product(): return jnp.dot(left, right, preferred_element_type=jnp.float32)]
    reduce_scatter x17 -> x6, waiting for transfers between devices: 1020 us -> 852 us  [scatter_matrix(): lax.psum_scatter(merged, ('mp', 'dp'), scatter_dimension=0, tiled=False)]
    all_gather x0 -> x3, blocking collectives: none -> 110 us  [the longest x1 41.1 us: local(): hidden_all = lax.all_gather(hidden_own.T, WORLD_AXES, axis=0, tiled=True)]
  transfers between devices with their start and end apart: 55 -> 21, of which waited for: 43 -> 19; matrix products, arithmetic and copies ran while one was open for 22% -> 14% of each run, Pallas kernels for 0% -> 1%
where the time goes in v1:
time: 2560 us; the launch traced here: 2550 us
  waiting for transfers between devices  1620 us (63%)
  matrix products  240 us (9%)
  blocking collectives  232 us (9%)
  local copies, waits for them, and re-layouts  224 us (9%)
  other arithmetic  110 us (4%)
  Pallas kernels  79.7 us (3%)
  between operations  28.5 us (1%)
    reduce_scatter x6, waiting for transfers between devices, scatter_matrix(): lax.psum_scatter(merged, ('mp', 'dp'), scatter_dimension=0, tiled=False)  852 us
    all_gather x8, waiting for transfers between devices, gather_matrix(): whole = lax.all_gather(part, ('mp', 'dp'), axis=0, tiled=False)  488 us
    unnamed x23, waiting for transfers between devices  229 us
    dot_general x82, matrix products, product(): return jnp.dot(left, right, preferred_element_type=jnp.float32)  167 us
    unnamed x1, blocking collectives  68.2 us
  transfers between devices with their start and end apart: 21, of which 19 were waited for; matrix products, arithmetic and copies ran while one was open for 14% of the time, Pallas kernels for 1%

profile of v1, /device:TPU:0, one launch (start us, length us, event | category | flops | bytes accessed | tf_op | source)
XLA Modules:
  0.0 2547.5 jit_solution(12335009530802995953)
XLA Ops:
  9.1 31.6 %pack_rows.2 = (bf16[9088,128]{1,0:T(8,128)(2,1)S(1)}, s32[9104]{0:T(1024)S(1)}) custom-call(s32[7776]{0:T(1024)S(1)} %get-tuple-element.187.pos_ref, s32[7776]{0:T(1024)S(1)} %get-tuple-element.516.slot_ref, s32[8]{0:T(128)S(1)} %broadcast_clamp_fusion.fill_ref, bf16[7776,128]{1,0:T(8,128)(2,1)} %bitcast.606), custom_call_target="tpu_custom_call" | custom-call | tf_op jit(solution)/shard_map/pack_rows/pallas_call | solution.py:614
  42.2 13.8 all_to_all.55
  63.7 68.2 %all-reduce = s32[128]{0:T(128)S(1)} all-reduce(s32[128]{0:T(128)S(1)} %add_dynamic-update-slice_fusion), channel_id=2, replica_groups=mesh['dp'=8,'mp'=4] {'dp','mp'}, use_global_device_ids=true, to_apply=%add | all-reduce | flops 128 | bytes 1024
  133.1 41.1 %all-gather.3 = bf16[32,36,64]{2,1,0:T(8,128)(2,1)S(1)} all-gather(bf16[1,36,64]{2,1,0:T(8,128)(2,1)S(1)} %fusion.250), channel_id=1, replica_groups=mesh['dp'=8,'mp'=4] {'dp','mp'}, dimensions={0}, use_global_device_ids=true | all-gather | bytes 152064 | tf_op jit(solution)/shard_map/all_gather | solution.py:1000
  182.9 16.5 scatter_rows.2
  218.1 38.1 %all-gather.2 = bf16[32,36,33]{2,1,0:T(8,128)(2,1)S(1)} all-gather(bf16[1,36,33]{2,1,0:T(8,128)(2,1)S(1)} %maximum_bitcast_fusion.15), channel_id=1, replica_groups=mesh['dp'=8,'mp'=4] {'dp','mp'}, dimensions={0}, use_global_device_ids=true | all-gather | bytes 78408 | tf_op jit(solution)/shard_map/all_gather | solution.py:991
  264.4 31.0 %all-gather.1 = f32[16,1,256,16]{2,3,1,0:T(8,128)S(1)} all-gather(f32[2,1,256,16]{2,3,1,0:T(8,128)S(1)} %copy-done.229), channel_id=3, replica_groups=mesh['dp'=8,'mp'=4] {'dp'}, dimensions={0}, use_global_device_ids=true | all-gather | bytes 294912 | tf_op jit(solution)/shard_map/all_gather | solution.py:1015
  300.8 16.4 all-reduce.8.cloned.1.call-done
  324.1 54.8 %all-gather.25.cloned.1.call-done = bf16[32,36,1152]{2,1,0:T(8,128)(2,1)} async-done(((bf16[1,36,1152]{2,1,0:T(8,128)(2,1)}), bf16[32,36,1152]{2,1,0:T(8,128)(2,1)}) %all-gather.25.cloned.1.call-update) | async-done | bytes 2654224 | tf_op jit(solution)/shard_map/all_gather | solution.py:742
  389.3 50.9 %all-gather.17.cloned.1.call-done = bf16[32,36,1152]{2,1,0:T(8,128)(2,1)} async-done(((bf16[1,36,1152]{2,1,0:T(8,128)(2,1)}), bf16[32,36,1152]{2,1,0:T(8,128)(2,1)}) %all-gather.17.cloned.1.call-update) | async-done | bytes 2654224 | tf_op jit(solution)/shard_map/all_gather | solution.py:742
  450.5 68.9 %all-gather.15.cloned.1.call-done = bf16[32,144,864]{2,1,0:T(8,128)(2,1)} async-done(((bf16[1,144,864]{2,1,0:T(8,128)(2,1)}), bf16[32,144,864]{2,1,0:T(8,128)(2,1)}) %all-gather.15.cloned.1.call-update) | async-done | bytes 7962640 | tf_op jit(solution)/shard_map/all_gather | solution.py:742
  548.8 49.0 %all-gather.23.cloned.1.call-done = bf16[32,144,864]{2,1,0:T(8,128)(2,1)} async-done(((bf16[1,144,864]{2,1,0:T(8,128)(2,1)}), bf16[32,144,864]{2,1,0:T(8,128)(2,1)}) %all-gather.23.cloned.1.call-update) | async-done | bytes 7962640 | tf_op jit(solution)/shard_map/all_gather | solution.py:742
  604.0 83.3 %all-gather.19.cloned.1.call-done = bf16[32,144,1152]{2,1,0:T(8,128)(2,1)} async-done(((bf16[1,144,1152]{2,1,0:T(8,128)(2,1)}), bf16[32,144,1152]{2,1,0:T(8,128)(2,1)}) %all-gather.19.cloned.1.call-update) | async-done | bytes 10616848 | tf_op jit(solution)/shard_map/all_gather | solution.py:742
  700.5 76.2 %all-gather.21.cloned.1.call-done = bf16[32,144,1152]{2,1,0:T(8,128)(2,1)} async-done(((bf16[1,144,1152]{2,1,0:T(8,128)(2,1)}), bf16[32,144,1152]{2,1,0:T(8,128)(2,1)}) %all-gather.21.cloned.1.call-update) | async-done | bytes 10616848 | tf_op jit(solution)/shard_map/all_gather | solution.py:742
  832.9 33.3 %all-gather.27.cloned.1.call-done = bf16[32,144,1152]{2,1,0:T(8,128)(2,1)} async-done(((bf16[1,144,1152]{2,1,0:T(8,128)(2,1)}), bf16[32,144,1152]{2,1,0:T(8,128)(2,1)}) %all-gather.27.cloned.1.call-update) | async-done | bytes 10616848 | tf_op jit(solution)/shard_map/all_gather | solution.py:742
  884.5 71.2 %all-gather.29.cloned.1.call-done = bf16[32,144,1152]{2,1,0:T(8,128)(2,1)} async-done(((bf16[1,144,1152]{2,1,0:T(8,128)(2,1)}), bf16[32,144,1152]{2,1,0:T(8,128)(2,1)}) %all-gather.29.cloned.1.call-update) | async-done | bytes 10616848 | tf_op jit(solution)/shard_map/all_gather | solution.py:742
  1017.4 13.7 fusion.88
  1031.1 14.5 fusion.91
  1160.6 13.4 all-gather.31.cloned.1.call-done
  1288.1 84.3 %reduce-scatter.27.cloned.1.call-done = bf16[1,36,1152]{2,1,0:T(8,128)(2,1)} async-done(((bf16[32,36,1152]{2,1,0:T(8,128)(2,1)}), bf16[1,36,1152]{2,1,0:T(8,128)(2,1)}) %reduce-scatter.27.cloned.1.call-update) | async-done | bytes 82960
  1377.7 127.6 %all-reduce.10.cloned.1.call-done = f32[32,97,36]{1,2,0:T(8,128)} async-done(((f32[32,97,36]{1,2,0:T(8,128)}), f32[32,97,36]{1,2,0:T(8,128)}) %all-reduce.10.cloned.1.call-update) | async-done | bytes 446992
  1508.1 133.2 %reduce-scatter.13.cloned.1.call-done = bf16[1,144,864]{2,1,0:T(8,128)(2,1)} async-done(((bf16[32,144,864]{2,1,0:T(8,128)(2,1)}), bf16[1,144,864]{2,1,0:T(8,128)(2,1)}) %reduce-scatter.13.cloned.1.call-update) | async-done | bytes 248848 | tf_op jit(solution)/shard_map/reduce_scatter | solution.py:751
  1642.7 133.8 %reduce-scatter.15.cloned.1.call-done = bf16[1,144,864]{2,1,0:T(8,128)(2,1)} async-done(((bf16[32,144,864]{2,1,0:T(8,128)(2,1)}), bf16[1,144,864]{2,1,0:T(8,128)(2,1)}) %reduce-scatter.15.cloned.1.call-update) | async-done | bytes 248848 | tf_op jit(solution)/shard_map/reduce_scatter | solution.py:751
  1778.6 146.0 %reduce-scatter.17.cloned.1.call-done = bf16[1,144,1152]{2,1,0:T(8,128)(2,1)} async-done(((bf16[32,144,1152]{2,1,0:T(8,128)(2,1)}), bf16[1,144,1152]{2,1,0:T(8,128)(2,1)}) %reduce-scatter.17.cloned.1.call-update) | async-done | bytes 331792 | tf_op jit(solution)/shard_map/reduce_scatter | solution.py:751
  1925.9 146.5 %reduce-scatter.19.cloned.1.call-done = bf16[1,144,1152]{2,1,0:T(8,128)(2,1)} async-done(((bf16[32,144,1152]{2,1,0:T(8,128)(2,1)}), bf16[1,144,1152]{2,1,0:T(8,128)(2,1)}) %reduce-scatter.19.cloned.1.call-update) | async-done | bytes 331792 | tf_op jit(solution)/shard_map/reduce_scatter | solution.py:751
  2073.7 146.5 %reduce-scatter.21.cloned.1.call-done = bf16[1,144,1152]{2,1,0:T(8,128)(2,1)} async-done(((bf16[32,144,1152]{2,1,0:T(8,128)(2,1)}), bf16[1,144,1152]{2,1,0:T(8,128)(2,1)}) %reduce-scatter.21.cloned.1.call-update) | async-done | bytes 331792 | tf_op jit(solution)/shard_map/reduce_scatter | solution.py:751
  2221.5 146.5 %reduce-scatter.23.cloned.1.call-done = bf16[1,144,1152]{2,1,0:T(8,128)(2,1)} async-done(((bf16[32,144,1152]{2,1,0:T(8,128)(2,1)}), bf16[1,144,1152]{2,1,0:T(8,128)(2,1)}) %reduce-scatter.23.cloned.1.call-update) | async-done | bytes 331792 | tf_op jit(solution)/shard_map/reduce_scatter | solution.py:751
  2385.9 39.8 %psum.7 = f32[2]{0:T(128)S(1)} all-reduce(f32[2]{0:T(128)S(1)} %pad_maximum_fusion.35), channel_id=1, replica_groups=mesh['dp'=8,'mp'=4] {'dp','mp'}, use_global_device_ids=true, to_apply=%region_64.65 | all-reduce | flops 2 | bytes 16 | tf_op jit(solution)/shard_map/psum | solution.py:1095
  2426.9 11.4 concatenate.107.x_ref
  2438.3 17.1 gather_rows.6
  2472.7 40.9 %all-to-all-done.6 = bf16[8,1136,128]{2,1,0:T(8,128)(2,1)S(1)} async-done(((bf16[8,1136,128]{2,1,0:T(8,128)(2,1)}), bf16[8,1136,128]{2,1,0:T(8,128)(2,1)S(1)}, u32[]{:S(2)}, u32[]{:S(2)}) %all-to-all-start.6) | async-done | bytes 2326560 | tf_op jit(solution)/shard_map/all_to_all | solution.py:660
  2513.9 14.5 gather_rows.7
  (1015 shorter events, 545.0 us)
Async XLA Ops:
  55.9 127.0 %all-to-all-start.5 = ((bf16[8,1136,128]{2,1,0:T(8,128)(2,1)}), bf16[8,1136,128]{2,1,0:T(8,128)(2,1)S(1)}, u32[]{:S(2)}, u32[]{:S(2)}) async-start(bf16[8,1136,128]{2,1,0:T(8,128)(2,1)} %bitcast.603), calls=%async_computation.5 | async-start | bytes 4653056 | tf_op jit(solution)/shard_map/all_to_all | solution.py:660
  59.7 257.5 %all-reduce.8.cloned.1.call-start = ((), (), s32[]{:S(2)}) async-start(), calls=%async_computation.30 | async-start | bytes 8257536
  60.0 119.0 %copy-start.147 = (bf16[36,2442]{1,0:T(8,128)(2,1)}, bf16[36,2442]{1,0:T(8,128)(2,1)S(1)}, u32[]{:S(2)}) copy-start(bf16[36,2442]{1,0:T(8,128)(2,1)S(1)} %reshape.791) | copy-start | bytes 527476
  179.0 199.9 %all-gather.25.cloned.1.call-start = ((), (), s32[]{:S(2)}) async-start(), calls=%async_computation.20 | async-start | bytes 3041280 | tf_op jit(solution)/shard_map/all_gather | solution.py:742
  205.4 234.8 %all-gather.17.cloned.1.call-start = ((), (), s32[]{:S(2)}) async-start(), calls=%async_computation.16 | async-start | bytes 3041280 | tf_op jit(solution)/shard_map/all_gather | solution.py:742
  206.2 313.2 %all-gather.15.cloned.1.call-start = ((), (), s32[]{:S(2)}) async-start(), calls=%async_computation.15 | async-start | bytes 8515584 | tf_op jit(solution)/shard_map/all_gather | solution.py:742
  208.5 389.3 %all-gather.23.cloned.1.call-start = ((), (), s32[]{:S(2)}) async-start(), calls=%async_computation.19 | async-start | bytes 8515584 | tf_op jit(solution)/shard_map/all_gather | solution.py:742
  209.7 477.5 %all-gather.19.cloned.1.call-start = ((), (), s32[]{:S(2)}) async-start(), calls=%async_computation.17 | async-start | bytes 10948608 | tf_op jit(solution)/shard_map/all_gather | solution.py:742
  211.8 565.0 %all-gather.21.cloned.1.call-start = ((), (), s32[]{:S(2)}) async-start(), calls=%async_computation.18 | async-start | bytes 10948608 | tf_op jit(solution)/shard_map/all_gather | solution.py:742
  213.0 653.2 %all-gather.27.cloned.1.call-start = ((), (), s32[]{:S(2)}) async-start(), calls=%async_computation.21 | async-start | bytes 10948608 | tf_op jit(solution)/shard_map/all_gather | solution.py:742
  214.2 741.5 %all-gather.29.cloned.1.call-start = ((), (), s32[]{:S(2)}) async-start(), calls=%async_computation.22 | async-start | bytes 10948608 | tf_op jit(solution)/shard_map/all_gather | solution.py:742
  318.5 226.7 %copy-start.211 = (f32[2,1,1152]{2,0,1:T(2,128)}, f32[2,1,1152]{2,0,1:T(2,128)S(1)}, u32[]{:S(2)}) copy-start(f32[2,1,1152]{2,0,1:T(2,128)S(1)} %copy.335) | copy-start | bytes 27652
  318.5 470.0 %copy-start.215 = (f32[2,1,1152]{2,0,1:T(2,128)}, f32[2,1,1152]{2,0,1:T(2,128)S(1)}, u32[]{:S(2)}) copy-start(f32[2,1,1152]{2,0,1:T(2,128)S(1)} %copy.334) | copy-start | bytes 27652
  318.6 471.3 %copy-start.193 = (f32[2,1,1152]{2,0,1:T(2,128)}, f32[2,1,1152]{2,0,1:T(2,128)S(1)}, u32[]{:S(2)}) copy-start(f32[2,1,1152]{2,0,1:T(2,128)S(1)} %copy.332) | copy-start | bytes 27652
  319.0 214.6 %copy-start.26 = (bf16[256,1152]{1,0:T(8,128)(2,1)}, bf16[256,1152]{1,0:T(8,128)(2,1)S(1)}, u32[]{:S(2)}) copy-start(bf16[256,1152]{1,0:T(8,128)(2,1)S(1)} %fusion.137) | copy-start | bytes 1769476
  320.6 283.1 %copy-start.191 = (f32[2,1152]{1,0:T(2,128)}, f32[2,1152]{1,0:T(2,128)S(1)}, u32[]{:S(2)}) copy-start(f32[2,1152]{1,0:T(2,128)S(1)} %get-tuple-element.361) | copy-start | bytes 27652
  323.9 850.1 %all-gather.31.cloned.1.call-start = ((), (), s32[]{:S(2)}) async-start(), calls=%async_computation.29 | async-start | bytes 2128896 | tf_op jit(solution)/shard_map/all_gather | solution.py:1072
  548.5 240.0 %copy-start.16 = (f32[2,128,1152]{2,1,0:T(8,128)}, f32[2,128,1152]{2,1,0:T(8,128)S(1)}, u32[]{:S(2)}) copy-start(f32[2,128,1152]{2,1,0:T(8,128)S(1)} %get-tuple-element.201) | copy-start | bytes 3538948
  1118.9 168.2 %reduce-scatter.25.cloned.1.call-start = ((), (), s32[]{:S(2)}) async-start(), calls=%async_computation.32 | async-start | bytes 3041280
  1125.1 247.3 %reduce-scatter.27.cloned.1.call-start = ((), (), s32[]{:S(2)}) async-start(), calls=%async_computation.33 | async-start | bytes 3041280
  1134.2 371.2 %all-reduce.10.cloned.1.call-start = ((), (), s32[]{:S(2)}) async-start(), calls=%async_computation.31 | async-start | bytes 1310720
  1184.8 456.5 %reduce-scatter.13.cloned.1.call-start = ((), (), s32[]{:S(2)}) async-start(), calls=%async_computation.23 | async-start | bytes 8515584 | tf_op jit(solution)/shard_map/reduce_scatter | solution.py:751
  1192.3 584.1 %reduce-scatter.15.cloned.1.call-start = ((), (), s32[]{:S(2)}) async-start(), calls=%async_computation.24 | async-start | bytes 8515584 | tf_op jit(solution)/shard_map/reduce_scatter | solution.py:751
  1233.0 691.6 %reduce-scatter.17.cloned.1.call-start = ((), (), s32[]{:S(2)}) async-start(), calls=%async_computation.25 | async-start | bytes 10948608 | tf_op jit(solution)/shard_map/reduce_scatter | solution.py:751
  1243.6 828.8 %reduce-scatter.19.cloned.1.call-start = ((), (), s32[]{:S(2)}) async-start(), calls=%async_computation.26 | async-start | bytes 10948608 | tf_op jit(solution)/shard_map/reduce_scatter | solution.py:751
  1258.0 962.2 %reduce-scatter.21.cloned.1.call-start = ((), (), s32[]{:S(2)}) async-start(), calls=%async_computation.27 | async-start | bytes 10948608 | tf_op jit(solution)/shard_map/reduce_scatter | solution.py:751
  1270.4 1097.6 %reduce-scatter.23.cloned.1.call-start = ((), (), s32[]{:S(2)}) async-start(), calls=%async_computation.28 | async-start | bytes 10948608 | tf_op jit(solution)/shard_map/reduce_scatter | solution.py:751
  1374.9 131.4 %copy-start.235 = (f32[64,36]{0,1:T(8,128)S(1)}, f32[64,36]{0,1:T(8,128)}, u32[]{:S(2)}) copy-start(f32[64,36]{0,1:T(8,128)} %copy-done.234) | copy-start | bytes 27652
  1374.9 131.4 %copy-start.250 = (bf16[64,128]{1,0:T(8,128)(2,1)S(1)}, bf16[64,128]{1,0:T(8,128)(2,1)}, u32[]{:S(2)}) copy-start(bf16[64,128]{1,0:T(8,128)(2,1)} %copy-done.249) | copy-start | bytes 49156
  1374.9 131.4 %copy-start.252 = (bf16[64,128]{1,0:T(8,128)(2,1)S(1)}, bf16[64,128]{1,0:T(8,128)(2,1)}, u32[]{:S(2)}) copy-start(bf16[64,128]{1,0:T(8,128)(2,1)} %copy-done.251) | copy-start | bytes 49156
  1507.4 271.2 %copy-start.61 = (f32[36,2442]{1,0:T(8,128)}, f32[36,2442]{1,0:T(8,128)S(1)}, u32[]{:S(2)}) copy-start(f32[36,2442]{1,0:T(8,128)S(1)} %concatenate.106) | copy-start | bytes 1054948
  2457.3 56.3 %all-to-all-start.6 = ((bf16[8,1136,128]{2,1,0:T(8,128)(2,1)}), bf16[8,1136,128]{2,1,0:T(8,128)(2,1)S(1)}, u32[]{:S(2)}, u32[]{:S(2)}) async-start(bf16[8,1136,128]{2,1,0:T(8,128)(2,1)} %bitcast.159), calls=%async_computation.12 | async-start | bytes 4653056 | tf_op jit(solution)/shard_map/all_to_all | solution.py:660
  (280 other events, 1669.1 us)
Sparse Core Ops, SparseCore 0:
  179.2 137.9 all-reduce.7
  320.7 58.2 all-gather.24
  382.5 57.6 all-gather.16
  443.6 75.7 all-gather.14
  522.2 75.5 all-gather.22
  601.2 85.9 all-gather.18
  690.8 85.8 all-gather.20
  780.3 85.8 all-gather.26
  869.7 85.8 all-gather.28
  1119.0 54.8 all-gather.30
  1180.0 92.8 reduce-scatter.24
  1279.6 92.8 reduce-scatter.26
  1377.7 127.6 all-reduce.9
  1512.1 129.1 reduce-scatter.12
  1647.1 129.3 reduce-scatter.14
  1783.4 141.1 reduce-scatter.16
  1931.6 140.7 reduce-scatter.18
  2079.4 140.7 reduce-scatter.20
  2227.3 140.6 reduce-scatter.22

commit v2 on v1

--- a/solution.py
+++ b/solution.py
@@ -495,7 +495,6 @@
     )
 
 
-WORLD_AXES = ("dp", "mp")
 CHUNK_ROWS = 1136
 REST_ROWS = 2 * PD + FREQ + D + CLASSES + 1
 
@@ -654,6 +653,389 @@
     )(index, rows)
 
 
+MESH = pl.DeviceIdType.MESH
+LAG = 2
+SLOTS = 4
+GATHER_SLOTS = 12
+
+
+def coordinates():
+    rank = lax.axis_index("dp")
+    group = lax.axis_index("mp")
+    return lax.div(rank, 2), lax.rem(rank, 2), lax.div(group, 2), lax.rem(group, 2)
+
+
+def device_at(z, x, y, core):
+    return (z * 2 + x, y * 2 + core)
+
+
+def neighbours():
+    z, x, y, core = coordinates()
+    along_x = device_at(z, 1 - x, y, core)
+    along_y = device_at(z, x, 1 - y, core)
+    first = tuple(jnp.where(core == 0, b, a) for a, b in zip(along_x, along_y))
+    second = tuple(jnp.where(core == 0, a, b) for a, b in zip(along_x, along_y))
+    others = [device_at(lax.rem(z + step, 4), x, y, core) for step in (1, 2, 3)]
+    return device_at(z, x, y, 1 - core), first, second, others
+
+
+def greet(peers):
+    barrier = pltpu.get_barrier_semaphore()
+    for peer in peers:
+        pl.semaphore_signal(barrier, inc=1, device_id=peer, device_id_type=MESH)
+    pl.semaphore_wait(barrier, len(peers))
+
+
+def block_of(ref, entry, group, at, side=None):
+    stacked, rows, width = entry
+    sides = slice(None) if side is None else side
+    if stacked:
+        return ref.at[group, :, sides, at, :]
+    return ref.at[:, sides, at, pl.ds(pl.multiple_of(group * width, 128), width)]
+
+
+def slice_of(ref, entry, group, z, x, at):
+    stacked, rows, width = entry
+    if stacked:
+        return ref.at[group, z, x, at, :]
+    return ref.at[z, x, at, pl.ds(pl.multiple_of(group * width, 128), width)]
+
+
+def chunk_ranges(plan, chunk):
+    ranges = []
+    start = 0
+    for stacked, rows, width in plan:
+        ranges.append((start, start + rows // chunk))
+        start += rows // chunk
+    return ranges, start
+
+
+def in_range(unit, low, high):
+    return (unit >= low) & (unit < high)
+
+
+def remote(source, target, send, receive, peer):
+    return pltpu.make_async_remote_copy(
+        src_ref=source,
+        dst_ref=target,
+        send_sem=send,
+        recv_sem=receive,
+        device_id=peer,
+        device_id_type=MESH,
+    )
+
+
+def gather_whole_kernel(plan, chunk, *refs):
+    count = len(plan)
+    slices, wholes = refs[:count], refs[count : 2 * count]
+    held, other_held, own_sem, out_sem, z_send, z_recv, a_send, a_recv, b_send, b_recv, c_send, c_recv = refs[2 * count :]
+    z, x, y, core = coordinates()
+    other, first, second, others = neighbours()
+    mine_first = jnp.where(core == 0, y, x)
+    mine_second = jnp.where(core == 0, x, y)
+    ranges, total = chunk_ranges(plan, chunk)
+    greet([other, first, second] + others)
+
+    def copies(stage, k, unit):
+        entry = plan[k]
+        slot = lax.rem(unit, GATHER_SLOTS)
+        at = pl.ds(pl.multiple_of((unit - ranges[k][0]) * chunk, chunk), chunk)
+        cols = pl.ds(0, entry[2])
+        own = held.at[slot, mine_first, mine_second, z, :, cols]
+        if stage == 0:
+            source = slices[k].at[at, :]
+            return [pltpu.make_async_copy(source, own, own_sem.at[slot])] + [
+                remote(source, own, z_send.at[i, slot], z_recv.at[i, slot], others[i])
+                for i in range(3)
+            ]
+        if stage == 1:
+            part = held.at[slot, mine_first, mine_second, :, :, cols]
+            return [remote(part, part, a_send.at[slot], a_recv.at[slot], second)]
+        if stage == 2:
+            part = held.at[slot, mine_first, :, :, :, cols]
+            return [remote(part, part, b_send.at[slot], b_recv.at[slot], first)]
+        if stage == 3:
+            source = held.at[slot, :, :, :, :, cols]
+            target = other_held.at[slot, :, :, :, :, cols]
+            return [remote(source, target, c_send.at[slot], c_recv.at[slot], other)]
+        made = []
+        from_other = stage == 5
+        ref, owner = (other_held, 1 - core) if from_other else (held, core)
+        for i in range(2):
+            for j in range(2):
+                side = jnp.where(owner == 0, j, i)
+                group = 2 * jnp.where(owner == 0, i, j) + owner
+                made.append(
+                    pltpu.make_async_copy(
+                        ref.at[slot, i, j, :, :, cols],
+                        block_of(wholes[k], entry, group, at, side),
+                        out_sem.at[int(from_other), 2 * i + j, slot],
+                    )
+                )
+        return made
+
+    def go(unit, waits, starts):
+        for k in range(count):
+
+            @pl.when(in_range(unit, *ranges[k]))
+            def _(k=k):
+                for stage in waits:
+                    for copy in copies(stage, k, unit):
+                        copy.wait()
+                for stage in starts:
+                    for copy in copies(stage, k, unit):
+                        copy.start()
+
+    def step(t, unused):
+        go(t - 1 - 4 * LAG, (4, 5), ())
+        go(t - 4 * LAG, (3,), (5,))
+        go(t - 3 * LAG, (2,), (3, 4))
+        go(t - 2 * LAG, (1,), (2,))
+        go(t - LAG, (0,), (1,))
+        go(t, (), (0,))
+        return unused
+
+    lax.fori_loop(0, total + 1 + 4 * LAG, step, 0)
+
+
+def whole_shape(entry):
+    stacked, rows, width = entry
+    return (4, 4, 2, rows, width) if stacked else (4, 2, rows, 4 * width)
+
+
+def gather_whole(plan, slices, chunk, number, name):
+    ANY = pl.BlockSpec(memory_space=pl.ANY)
+    count = len(plan)
+    dma = pltpu.SemaphoreType.DMA
+    kind = slices[0].dtype
+    size = sum(math.prod(whole_shape(entry)) for entry in plan) * kind.itemsize
+    held = pltpu.VMEM((GATHER_SLOTS, 2, 2, 4, chunk, max(entry[2] for entry in plan)), kind)
+    each = dma((GATHER_SLOTS,))
+    three = dma((3, GATHER_SLOTS))
+    return pl.pallas_call(
+        functools.partial(gather_whole_kernel, plan, chunk),
+        out_shape=[jax.ShapeDtypeStruct(whole_shape(entry), kind) for entry in plan],
+        in_specs=[ANY] * count,
+        out_specs=[ANY] * count,
+        scratch_shapes=[held, held, each, dma((2, 4, GATHER_SLOTS)), three, three] + [each] * 6,
+        compiler_params=pltpu.CompilerParams(
+            collective_id=number, has_side_effects=True, vmem_limit_bytes=48 * 1024 * 1024
+        ),
+        cost_estimate=pl.CostEstimate(flops=0, bytes_accessed=2 * size, transcendentals=0),
+        name=name,
+    )(*slices)
+
+
+def sum_slices_kernel(plan, chunk, *refs):
+    count = len(plan)
+    parts, outs = refs[:count], refs[count : 2 * count]
+    (own, from_core, from_first, from_second, from_z, half, quarter, eighth) = refs[
+        2 * count : 2 * count + 8
+    ]
+    own_sem, core_send, core_recv, a_send, a_recv, b_send, b_recv, z_send, z_recv = refs[
+        2 * count + 8 :
+    ]
+    z, x, y, core = coordinates()
+    other, first, second, others = neighbours()
+    mine_first = jnp.where(core == 0, y, x)
+    mine_second = jnp.where(core == 0, x, y)
+    ranges, total = chunk_ranges(plan, chunk)
+    greet([other, first, second] + others)
+
+    def copies(stage, width, unit, k=None):
+        slot = lax.rem(unit, SLOTS)
+        pair = lax.rem(unit, 2)
+        cols = pl.ds(0, width)
+        if stage == 0:
+            made = []
+            for j in range(2):
+                mine = own.at[pair, j, :, :, :, cols]
+                theirs = from_core.at[pair, j, :, :, :, cols]
+                if k is None:
+                    made.append(pltpu.make_async_copy(mine, mine, own_sem.at[j, pair]))
+                    made.append(remote(mine, theirs, core_send.at[j, pair], core_recv.at[j, pair], other))
+                else:
+                    at = pl.ds(pl.multiple_of((unit - ranges[k][0]) * chunk, chunk), chunk)
+                    kept = block_of(parts[k], plan[k], 2 * j + core, at)
+                    sent = block_of(parts[k], plan[k], 2 * j + 1 - core, at)
+                    made.append(pltpu.make_async_copy(kept, mine, own_sem.at[j, pair]))
+                    made.append(remote(sent, theirs, core_send.at[j, pair], core_recv.at[j, pair], other))
+            return made
+        if stage == 1:
+            source = half.at[slot, 1 - mine_first, :, :, :, cols]
+            target = from_first.at[slot, :, :, :, cols]
+            return [remote(source, target, a_send.at[slot], a_recv.at[slot], first)]
+        if stage == 2:
+            source = quarter.at[slot, 1 - mine_second, :, :, cols]
+            target = from_second.at[slot, :, :, cols]
+            return [remote(source, target, b_send.at[slot], b_recv.at[slot], second)]
+        made = []
+        for i in range(3):
+            source = eighth.at[slot, lax.rem(z + i + 1, 4), :, cols]
+            target = from_z.at[slot, i, :, cols]
+            made.append(remote(source, target, z_send.at[i, slot], z_recv.at[i, slot], others[i]))
+        return made
+
+    def wide(ref, index, cols):
+        return ref[(*index, slice(None), cols)].astype(jnp.float32)
+
+    def add(stage, width, unit):
+        slot = lax.rem(unit, SLOTS)
+        pair = lax.rem(unit, 2)
+        cols = slice(0, width)
+        if stage == 0:
+            for i in range(2):
+                for j in range(2):
+                    lead = jnp.where(core == 0, i, j)
+                    last = jnp.where(core == 0, j, i)
+                    for k in range(4):
+                        value = wide(own, (pair, i, k, j), cols) + wide(from_core, (pair, i, k, j), cols)
+                        half[slot, lead, last, k, :, cols] = value.astype(half.dtype)
+        elif stage == 1:
+            for j in range(2):
+                for k in range(4):
+                    value = wide(half, (slot, mine_first, j, k), cols) + wide(
+                        from_first, (slot, j, k), cols
+                    )
+                    quarter[slot, j, k, :, cols] = value.astype(quarter.dtype)
+        else:
+            for k in range(4):
+                value = wide(quarter, (slot, mine_second, k), cols) + wide(
+                    from_second, (slot, k), cols
+                )
+                eighth[slot, k, :, cols] = value.astype(eighth.dtype)
+
+    widths = sorted({entry[2] for entry in plan})
+
+    def go(unit, stage):
+        for width in widths:
+            inside = functools.reduce(
+                jnp.logical_or,
+                [in_range(unit, *ranges[k]) for k in range(count) if plan[k][2] == width],
+            )
+
+            @pl.when(inside)
+            def _(width=width):
+                for copy in copies(stage, width, unit):
+                    copy.wait()
+                add(stage, width, unit)
+                for copy in copies(stage + 1, width, unit):
+                    copy.start()
+
+    def finish(unit):
+        for k in range(count):
+
+            @pl.when(in_range(unit, *ranges[k]))
+            def _(k=k):
+                width = plan[k][2]
+                slot = lax.rem(unit, SLOTS)
+                cols = slice(0, width)
+                for copy in copies(3, width, unit):
+                    copy.wait()
+                at = pl.ds(pl.multiple_of((unit - ranges[k][0]) * chunk, chunk), chunk)
+                value = wide(eighth, (slot, z), cols)
+                for i in range(3):
+                    value = value + wide(from_z, (slot, i), cols)
+                outs[k][at, :] = value
+
+    def begin(unit):
+        for k in range(count):
+
+            @pl.when(in_range(unit, *ranges[k]))
+            def _(k=k):
+                for copy in copies(0, plan[k][2], unit, k):
+                    copy.start()
+
+    def step(t, unused):
+        finish(t - 1 - 3 * LAG)
+        go(t - 1 - 2 * LAG, 2)
+        go(t - 1 - LAG, 1)
+        go(t - 1, 0)
+        begin(t)
+        return unused
+
+    lax.fori_loop(0, total + 1 + 3 * LAG, step, 0)
+
+
+def sum_slices(plan, parts, chunk, number, name):
+    count = len(plan)
+    dma = pltpu.SemaphoreType.DMA
+    kind = parts[0].dtype
+    width = max(entry[2] for entry in plan)
+    size = sum(math.prod(whole_shape(entry)) for entry in plan) * kind.itemsize
+    buffers = [
+        (2, 2, 4, 2, chunk, width),
+        (2, 2, 4, 2, chunk, width),
+        (SLOTS, 2, 4, chunk, width),
+        (SLOTS, 4, chunk, width),
+        (SLOTS, 3, chunk, width),
+        (SLOTS, 2, 2, 4, chunk, width),
+        (SLOTS, 2, 4, chunk, width),
+        (SLOTS, 4, chunk, width),
+    ]
+    return pl.pallas_call(
+        functools.partial(sum_slices_kernel, plan, chunk),
+        out_shape=[jax.ShapeDtypeStruct((entry[1], entry[2]), jnp.float32) for entry in plan],
+        in_specs=[pl.BlockSpec(memory_space=pl.ANY)] * count,
+        out_specs=[VMEM] * count,
+        scratch_shapes=[pltpu.VMEM(shape, kind) for shape in buffers]
+        + [dma((2, 2))] * 3
+        + [dma((SLOTS,))] * 4
+        + [dma((3, SLOTS))] * 2,
+        compiler_params=pltpu.CompilerParams(
+            collective_id=number, has_side_effects=True, vmem_limit_bytes=48 * 1024 * 1024
+        ),
+        cost_estimate=pl.CostEstimate(flops=0, bytes_accessed=2 * size, transcendentals=0),
+        name=name,
+    )(*parts)
+
+
+def push_kernel(world, x_ref, out_ref, send_sem, recv_sem):
+    groups = lax.axis_size("mp")
+    me = lax.axis_index("dp") * groups + lax.axis_index("mp")
+
+    def peer(i):
+        to = lax.rem(me + i, world)
+        return (lax.div(to, groups), lax.rem(to, groups))
+
+    barrier = pltpu.get_barrier_semaphore()
+
+    def hail(i, unused):
+        pl.semaphore_signal(barrier, inc=1, device_id=peer(i), device_id_type=MESH)
+        return unused
+
+    lax.fori_loop(1, world, hail, 0)
+    out_ref[me] = x_ref[...]
+    pl.semaphore_wait(barrier, world - 1)
+
+    def copy(i):
+        return remote(x_ref, out_ref.at[me], send_sem.at[i], recv_sem.at[i], peer(i))
+
+    def start(i, unused):
+        copy(i).start()
+        return unused
+
+    def finish(i, unused):
+        copy(i).wait()
+        return unused
+
+    lax.fori_loop(1, world, start, 0)
+    lax.fori_loop(1, world, finish, 0)
+
+
+def push_all(value, world, number, name):
+    dma = pltpu.SemaphoreType.DMA
+    return pl.pallas_call(
+        functools.partial(push_kernel, world),
+        out_shape=jax.ShapeDtypeStruct((world,) + value.shape, value.dtype),
+        in_specs=[VMEM],
+        out_specs=VMEM,
+        scratch_shapes=[dma((world,)), dma((world,))],
+        compiler_params=pltpu.CompilerParams(collective_id=number, has_side_effects=True),
+        name=name,
+    )(value)
+
+
 def swap_ranks(buf, ranks):
     rest = buf.shape[1:]
     split = buf.reshape((ranks, buf.shape[0] // ranks) + rest)
@@ -738,34 +1120,62 @@
     return jnp.concatenate(parts)
 
 
-def gather_matrix(part):
-    whole = lax.all_gather(part, ("mp", "dp"), axis=0, tiled=False)
-    groups = lax.axis_size("mp")
-    return whole.reshape(groups, -1, part.shape[1])
-
-
-def scatter_matrix(parts):
-    ranks = lax.axis_size("dp")
-    stacked = jnp.stack([part.reshape(ranks, -1, part.shape[1]) for part in parts])
-    merged = stacked.reshape((-1,) + stacked.shape[2:])
-    return lax.psum_scatter(merged, ("mp", "dp"), scatter_dimension=0, tiled=False)
+QKV_WIDTH = 896
+PROJ_ROWS = 48
+
+
+def layer_plan(ranks):
+    return (
+        (False, D // ranks, QKV_WIDTH),
+        (True, PROJ_ROWS, D),
+        (False, D // ranks, FF // 4),
+        (True, FF // 4 // ranks, D),
+    )
+
+
+def pad_to(values, axis, size):
+    widths = [(0, 0)] * values.ndim
+    widths[axis] = (0, size - values.shape[axis])
+    return jnp.pad(values, widths)
+
+
+def pad_slices(level):
+    return [pad_to(level[0], 1, QKV_WIDTH), pad_to(level[1], 0, PROJ_ROWS), level[2], level[3]]
+
+
+def trim_slices(level, ranks):
+    return [level[0][:, : 3 * HEADS * HD // 4], level[1][: HEADS * HD // 4 // ranks], level[2], level[3]]
+
+
+def whole_weights(wholes, ranks):
+    qkv, proj, up, down = wholes
+    own_rows = HEADS * HD // 4 // ranks
+    proj = proj.reshape(4, ranks, PROJ_ROWS, D)[:, :, :own_rows].reshape(-1, D)
+    return (qkv.reshape(D, -1), proj, up.reshape(D, -1), down.reshape(-1, D))
+
+
+def whole_parts(grads, ranks):
+    qkv, proj, up, down = grads
+    shapes = [whole_shape(entry) for entry in layer_plan(ranks)]
+    proj = pad_to(proj.reshape(4, ranks, -1, D), 2, PROJ_ROWS)
+    return [part.reshape(shape) for part, shape in zip((qkv, proj, up, down), shapes)]
 
 
 def heads_of(packed, images):
-    third = packed[0].shape[1] // 3
-    pieces = []
-    for index in range(3):
-        cols = [
-            part[:, index * third : (index + 1) * third].reshape(images, -1, third // HD, HD)
-            for part in packed
-        ]
-        pieces.append(jnp.concatenate(cols, axis=2).transpose(0, 2, 1, 3))
-    return pieces
+    split = packed.reshape(images, -1, 4, QKV_WIDTH)[..., : 3 * HEADS * HD // 4]
+    split = split.reshape(images, -1, 4, 3, HEADS // 4, HD).transpose(3, 0, 2, 4, 1, 5)
+    split = split.reshape(3, images, HEADS, -1, HD)
+    return split[0], split[1], split[2]
+
+
+def columns_of(parts, images):
+    stacked = jnp.stack(parts).reshape(3, images, 4, HEADS // 4, -1, HD)
+    flat = stacked.transpose(1, 4, 2, 0, 3, 5).reshape(-1, 4, 3 * HEADS * HD // 4)
+    return pad_to(flat, 2, QKV_WIDTH).reshape(-1, 4 * QKV_WIDTH)
 
 
 def own_forward(state, weights, modulate):
     qkv_weight, proj_weight, up_weight, down_weight = weights
-    groups = qkv_weight.shape[0]
     images, rows, columns = state.shape
     shift_one, scale_one, gate_one, shift_two, scale_two, gate_two = [
         modulate[:, index, None, :] for index in range(6)
@@ -773,7 +1183,7 @@
     normed_one, spread_one = normalize(state)
     full_one = (normed_one * (1.0 + scale_one) + shift_one).astype(jnp.bfloat16)
     flat_one = full_one.reshape(-1, columns)
-    packed = [product(flat_one, qkv_weight[m]).astype(jnp.bfloat16) for m in range(groups)]
+    packed = product(flat_one, qkv_weight).astype(jnp.bfloat16)
     queries, key_rows, value_rows = heads_of(packed, images)
     scores = jnp.einsum(
         "ghqe,ghke->ghqk", queries, key_rows, preferred_element_type=jnp.float32
@@ -786,15 +1196,14 @@
         preferred_element_type=jnp.float32,
     ).astype(jnp.bfloat16)
     attended = mixed.transpose(0, 2, 1, 3).reshape(-1, columns)
-    branch_one = product(attended, proj_weight.reshape(-1, columns)).reshape(state.shape)
+    branch_one = product(attended, proj_weight).reshape(state.shape)
     middle = state + gate_one * branch_one
     normed_two, spread_two = normalize(middle)
     full_two = (normed_two * (1.0 + scale_two) + shift_two).astype(jnp.bfloat16)
     flat_two = full_two.reshape(-1, columns)
-    hidden_pre = [product(flat_two, up_weight[m]) for m in range(groups)]
-    activated = [jax.nn.gelu(pre, approximate=True).astype(jnp.bfloat16) for pre in hidden_pre]
-    branch_two = sum(product(activated[m], down_weight[m]) for m in range(groups))
-    branch_two = branch_two.reshape(state.shape)
+    hidden_pre = product(flat_two, up_weight)
+    activated = jax.nn.gelu(hidden_pre, approximate=True).astype(jnp.bfloat16)
+    branch_two = product(activated, down_weight).reshape(state.shape)
     result = middle + gate_two * branch_two
     saved = (
         normed_one,
@@ -833,24 +1242,18 @@
         branch_two,
     ) = saved
     qkv_weight, proj_weight, up_weight, down_weight = weights
-    groups = qkv_weight.shape[0]
     images, rows, columns = grad_out.shape
     shift_one, scale_one, gate_one, shift_two, scale_two, gate_two = [
         modulate[:, index, None, :] for index in range(6)
     ]
     grad_gate_two = jnp.sum(grad_out * branch_two, axis=1)
     back_two = (gate_two * grad_out).astype(jnp.bfloat16).reshape(-1, columns)
-    grad_down = []
-    grad_up = []
-    grad_pres = []
-    for m in range(groups):
-        grad_down.append(product(activated[m].T, back_two).astype(jnp.bfloat16))
-        grad_act = product(back_two, down_weight[m].T)
-        unused, gelu_back = jax.vjp(lambda pre: jax.nn.gelu(pre, approximate=True), hidden_pre[m])
-        grad_pre = gelu_back(grad_act)[0].astype(jnp.bfloat16)
-        grad_up.append(product(flat_two.T, grad_pre).astype(jnp.bfloat16))
-        grad_pres.append(grad_pre)
-    grad_hidden_two = sum(product(grad_pres[m], up_weight[m].T) for m in range(groups))
+    grad_down = product(activated.T, back_two).astype(jnp.bfloat16)
+    grad_act = product(back_two, down_weight.T)
+    unused, gelu_back = jax.vjp(lambda pre: jax.nn.gelu(pre, approximate=True), hidden_pre)
+    grad_pre = gelu_back(grad_act)[0].astype(jnp.bfloat16)
+    grad_up = product(flat_two.T, grad_pre).astype(jnp.bfloat16)
+    grad_hidden_two = product(grad_pre, up_weight.T)
     grad_hidden_two = grad_hidden_two.reshape(grad_out.shape)
     grad_shift_two = jnp.sum(grad_hidden_two, axis=1)
     grad_scale_two = jnp.sum(grad_hidden_two * normed_two, axis=1)
@@ -859,8 +1262,8 @@
     )
     grad_gate_one = jnp.sum(grad_middle * branch_one, axis=1)
     back_one = (gate_one * grad_middle).astype(jnp.bfloat16).reshape(-1, columns)
-    grad_proj = product(attended.T, back_one).astype(jnp.bfloat16).reshape(groups, -1, columns)
-    grad_attended = product(back_one, proj_weight.reshape(-1, columns).T).astype(jnp.bfloat16)
+    grad_proj = product(attended.T, back_one).astype(jnp.bfloat16)
+    grad_attended = product(back_one, proj_weight.T).astype(jnp.bfloat16)
     grad_mixed = grad_attended.reshape(images, rows, HEADS, HD).transpose(0, 2, 1, 3)
     scores = jnp.einsum(
         "ghqe,ghke->ghqk", queries, key_rows, preferred_element_type=jnp.float32
@@ -884,16 +1287,10 @@
     grad_keys = jnp.einsum(
         "ghqk,ghqe->ghke", grad_scores, queries, preferred_element_type=jnp.float32
     )
-    parts = [
-        part.astype(jnp.bfloat16).transpose(0, 2, 1, 3).reshape(images * rows, groups, -1)
-        for part in (grad_queries, grad_keys, grad_values)
-    ]
-    grad_qkv = []
-    grad_hidden_one = 0.0
-    for m in range(groups):
-        grad_packed = jnp.concatenate([part[:, m] for part in parts], axis=1)
-        grad_qkv.append(product(flat_one.T, grad_packed).astype(jnp.bfloat16))
-        grad_hidden_one = grad_hidden_one + product(grad_packed, qkv_weight[m].T)
+    parts = [part.astype(jnp.bfloat16) for part in (grad_queries, grad_keys, grad_values)]
+    grad_packed = columns_of(parts, images)
+    grad_qkv = product(flat_one.T, grad_packed).astype(jnp.bfloat16)
+    grad_hidden_one = product(grad_packed, qkv_weight.T)
     grad_hidden_one = grad_hidden_one.reshape(grad_out.shape)
     grad_shift_one = jnp.sum(grad_hidden_one, axis=1)
     grad_scale_one = jnp.sum(grad_hidden_one * normed_one, axis=1)
@@ -911,7 +1308,7 @@
         ],
         axis=1,
     )
-    return (grad_state, grad_mod, (grad_qkv, [grad_proj[m] for m in range(groups)], grad_up, grad_down))
+    return (grad_state, grad_mod, (grad_qkv, grad_proj, grad_up, grad_down))
 
 
 def contract(left, right, left_axis, right_axis):
@@ -977,40 +1374,60 @@
     rank, counts = rank_within(dest, ranks)
     slots, tags = tiles_to_slots(big_copy[0], dest, slot, rank, counts, rounds)
     slices = slot_matrices(slots.astype(jnp.bfloat16), ranks)
-    weights = [[gather_matrix(part) for part in level] for level in slices]
-
-    facts = jnp.concatenate([timestep[:, 0], label[:, 0]])
-    facts = lax.all_gather(facts, WORLD_AXES, axis=0, tiled=False)
-    stamps = facts[:, :micro].reshape(-1)
-    tags_all = facts[:, micro:].reshape(-1)
+    plan = layer_plan(ranks) * 2
+    wholes = gather_whole(
+        plan, pad_slices(slices[0]) + pad_slices(slices[1]), 16, 1, "gather_weights"
+    )
+    weights = [whole_weights(wholes[:4], ranks), whole_weights(wholes[4:], ranks)]
+
     rest_own = rest_copy.reshape(own_columns, REST_ROWS)
     edges = [0, PD, PD + FREQ, PD + FREQ + D, PD + FREQ + D + CLASSES, REST_ROWS]
     win_t, one_t, two_t, table_t, tail_t = [
         rest_own[:, edges[i] : edges[i + 1]] for i in range(5)
     ]
-    ends = lax.all_gather(
-        jnp.concatenate([win_t, tail_t], axis=1), WORLD_AXES, axis=0, tiled=True
-    )
+    ends_size = own_columns * (2 * PD + 1)
+    told = jnp.concatenate(
+        [
+            jnp.concatenate([win_t, tail_t], axis=1).astype(jnp.float32).reshape(-1),
+            timestep[:, 0].astype(jnp.float32),
+            label[:, 0].astype(jnp.float32),
+        ]
+    )
+    told = pad_to(told, 0, 1280).reshape(-1, 128)
+    told = push_all(told, world, 6, "push_inputs").reshape(world, -1)
+    facts = told[:, ends_size : ends_size + 2 * micro].astype(jnp.int32)
+    facts = facts.reshape(ranks, groups, 2 * micro).transpose(1, 0, 2).reshape(world, -1)
+    stamps = facts[:, :micro].reshape(-1)
+    tags_all = facts[:, micro:].reshape(-1)
+    ends = told[:, :ends_size].reshape(columns, -1).astype(jnp.bfloat16)
     embed_weight = ends[:, :PD].T
     mask_token = ends[:, PD].astype(jnp.float32)
     head_weight = ends[:, PD + 1 :]
+    count_all = micro * world
     features = jax.vmap(time_features)(stamps).astype(jnp.bfloat16)
     pre_time = contract(features, one_t, 1, 1)
     hidden_own = jax.nn.silu(pre_time).astype(jnp.bfloat16)
-    hidden_all = lax.all_gather(hidden_own.T, WORLD_AXES, axis=0, tiled=True)
+    hidden_size = count_all * own_columns
+    hidden_all = pad_to(hidden_own.reshape(-1), 0, 4096).reshape(-1, 128)
+    hidden_all = push_all(hidden_all, world, 7, "push_hidden").reshape(world, -1)
+    hidden_all = hidden_all[:, :hidden_size].reshape(world, count_all, own_columns)
+    hidden_all = hidden_all.transpose(1, 0, 2).reshape(count_all, columns)
     picks = (tags_all[:, None] == jnp.arange(CLASSES, dtype=jnp.int32)[None, :]).astype(
         jnp.bfloat16
     )
-    cond_own = contract(hidden_all, two_t, 0, 1) + contract(picks, table_t, 1, 1)
+    cond_own = contract(hidden_all, two_t, 1, 1) + contract(picks, table_t, 1, 1)
     signal_own = jax.nn.silu(cond_own).astype(jnp.bfloat16)
     ada_own = ada_copy.reshape(own_columns, 14 * columns)
-    mods = lax.psum_scatter(
-        product(signal_own, ada_own), WORLD_AXES, scatter_dimension=0, tiled=True
-    )
-    mod_enc = mods[:, : 6 * columns].reshape(micro, 6, columns)
-    mod_dec = mods[:, 6 * columns : 12 * columns].reshape(micro, 6, columns)
-    final_shift = mods[:, None, 12 * columns : 13 * columns]
-    final_scale = mods[:, None, 13 * columns :]
+    mod_rows = micro * 14
+    mod_entry = (True, 32, columns)
+    mods = product(signal_own, ada_own).reshape(world, mod_rows, columns)
+    mods = pad_to(mods, 1, mod_entry[1]).reshape(whole_shape(mod_entry))
+    mods = sum_slices((mod_entry,), [mods], 16, 3, "sum_mods")[0]
+    mods = mods[:mod_rows].reshape(micro, 14, columns)
+    mod_enc = mods[:, :6]
+    mod_dec = mods[:, 6:12]
+    final_shift = mods[:, 12:13]
+    final_scale = mods[:, 13:]
 
     goals = lax.all_gather(target[:, 0], "dp", axis=0, tiled=False)
     goal = jnp.stack([goals[owner[b, 0], b] for b in range(micro)])
@@ -1052,7 +1469,6 @@
     grad_dec_in, grad_mod_dec, dec_grads = own_backward(
         grad_dec_out, dec_saved, weights[1], mod_dec
     )
-    dec_sums = [scatter_matrix(parts) for parts in dec_grads]
     grad_mask = jnp.sum((1.0 - kept) * grad_dec_in, axis=(0, 1))[None, :]
     grad_sent = jnp.einsum(
         "bpr,bpd->brd",
@@ -1063,24 +1479,35 @@
     grad_embedded, grad_mod_enc, enc_grads = own_backward(
         grad_sent, enc_saved, weights[0], mod_enc
     )
-    enc_sums = [scatter_matrix(parts) for parts in enc_grads]
+    sums = sum_slices(
+        plan, whole_parts(enc_grads, ranks) + whole_parts(dec_grads, ranks), 16, 2, "sum_gradients"
+    )
+    sums = matrices_slots([trim_slices(sums[:4], ranks), trim_slices(sums[4:], ranks)])
     grad_embed = contract_wide(
         patches.reshape(-1, PD), grad_embedded.reshape(-1, columns), 0, 0
     )
 
     vectors = jnp.concatenate([grad_mod_enc, grad_mod_dec, grad_final], axis=1)
-    vectors = lax.all_gather(vectors.astype(jnp.bfloat16), WORLD_AXES, axis=0, tiled=True)
+    vectors = vectors.astype(jnp.bfloat16).reshape(mod_rows, columns)
+    vectors = pad_to(vectors, 0, mod_entry[1])
+    vectors = gather_whole((mod_entry,), [vectors], 16, 4, "gather_vectors")[0]
+    vectors = vectors.reshape(world, mod_entry[1], columns)[:, :mod_rows].reshape(count_all, -1)
     owned_ada = contract(signal_own, vectors, 0, 0).reshape(-1)
     grad_signal = contract(vectors, ada_own, 1, 1)
     grad_cond = silu_back(cond_own, grad_signal)
-    grad_two_t = contract_wide(grad_cond, hidden_all, 0, 1)
+    grad_two_t = contract_wide(grad_cond, hidden_all, 0, 0)
     grad_table_t = contract_wide(grad_cond, picks, 0, 0)
     shared = jnp.concatenate(
         [contract_wide(grad_cond, two_t, 1, 0), grad_embed, grad_mask, grad_head], axis=0
     )
-    shared = shared.reshape(-1, world, own_columns).transpose(1, 0, 2)
-    shared = lax.psum_scatter(shared, WORLD_AXES, scatter_dimension=0, tiled=False)
-    count_all = micro * world
+    shared_rows = shared.shape[0]
+    shared = shared.reshape(shared_rows, ranks, groups, own_columns).transpose(2, 1, 0, 3)
+    shared = pad_to(shared.reshape(world, -1), 1, 4096)
+    shared_entry = (True, 32, 128)
+    shared = sum_slices(
+        (shared_entry,), [shared.reshape(whole_shape(shared_entry))], 32, 5, "sum_shared"
+    )[0]
+    shared = shared.reshape(-1)[: shared_rows * own_columns].reshape(shared_rows, own_columns)
     grad_pre = silu_back(pre_time, shared[:count_all])
     grad_one_t = contract_wide(grad_pre, features, 0, 0)
     ends_t = shared[count_all:].T
@@ -1088,11 +1515,9 @@
         [ends_t[:, :PD], grad_one_t, grad_two_t, grad_table_t, ends_t[:, PD:]], axis=1
     ).reshape(-1)
 
-    sums = matrices_slots(
-        [[part.astype(jnp.float32) for part in level] for level in (enc_sums, dec_sums)]
-    )
     squares = jnp.sum(sums * sums) + jnp.sum(owned_ada * owned_ada) + jnp.sum(owned_rest * owned_rest)
-    totals = lax.psum(jnp.stack([loss_sum, squares]), WORLD_AXES)
+    totals = jnp.broadcast_to(pad_to(jnp.stack([loss_sum, squares]), 0, 128), (8, 128))
+    totals = jnp.sum(push_all(totals, world, 8, "push_totals")[:, 0, :2], axis=0)
     owned_big = slots_to_tiles(sums, tags, dest, slot, rank, counts, rounds)
     grad_norm = jnp.sqrt(totals[1])
     clip = jnp.minimum(1.0, MAX_NORM / (grad_norm + 1e-06))

time: 2560 us -> 1450 us (0.57)
  waiting for transfers between devices: 1620 us -> 42.7 us
  Pallas kernels: 79.7 us -> 799 us
  blocking collectives: 232 us -> 31 us
  other arithmetic: 110 us -> 69.9 us
    reduce_scatter x6 -> x0, waiting for transfers between devices: 852 us -> none  [scatter_matrix(): lax.psum_scatter(merged, ('mp', 'dp'), scatter_dimension=0, tiled=False)]
    pallas_call x0 -> x8, Pallas kernels: none -> 719 us  [the longest x3 332 us: sum_slices(): pl.pallas_call(functools.partial(sum_slices_kernel, plan, chunk), out_sha...]
    all_gather x9 -> x0, waiting for transfers between devices: 501 us -> none  [the longest x8 488 us: gather_matrix(): whole = lax.all_gather(part, ('mp', 'dp'), axis=0, tiled=False)]
    unnamed x23 -> x0, waiting for transfers between devices: 229 us -> none
    all_gather x2 -> x0, blocking collectives: 79.3 us -> none  [the longest x1 41.1 us: local(): hidden_all = lax.all_gather(hidden_own.T, WORLD_AXES, axis=0, tiled=True)]
    unnamed x1 -> x0, blocking collectives: 68.2 us -> none
    reshape x56 -> x37, local copies, waits for them, and re-layouts: 15.4 us -> 69.4 us  [the longest x4 17.8 us: whole_weights(): proj = proj.reshape(4, ranks, PROJ_ROWS, D)[:, :, :own_rows].reshape(-1, D)]
    convert_element_type x24 -> x6, local copies, waits for them, and re-layouts: 47 us -> 3.92 us  [the longest x2 2.68 us: own_backward(): grad_attended = product(back_one, proj_weight.T).astype(jnp.bfloat16)]
  transfers between devices with their start and end apart: 21 -> 3, of which waited for: 19 -> 1; matrix products, arithmetic and copies ran while one was open for 14% -> 4% of each run, Pallas kernels for 1% -> 7%
where the time goes in v2:
time: 1450 us
  Pallas kernels  799 us (55%)
  matrix products  260 us (18%)
  local copies, waits for them, and re-layouts  214 us (15%)
  other arithmetic  69.9 us (5%)
  waiting for transfers between devices  42.7 us (3%)
  blocking collectives  31 us (2%)
  starting transfers between devices  18 us (1%)
    pallas_call x3, Pallas kernels, sum_slices(): pl.pallas_call(functools.partial(sum_slices_kernel, plan, chunk), out_sha...  332 us
    pallas_call x2, Pallas kernels, gather_whole(): pl.pallas_call(functools.partial(gather_whole_kernel, plan, chunk), out_s...  305 us
    dot_general x28, matrix products, product(): return jnp.dot(left, right, preferred_element_type=jnp.float32)  179 us
    pallas_call x3, Pallas kernels, push_all(): pl.pallas_call(functools.partial(push_kernel, world), out_shape=jax.Shape...  81.8 us
    all_to_all x3, waiting for transfers between devices, swap_ranks(): return lax.all_to_all(split, 'dp', 0, 0).reshape(buf.shape)  42.7 us
    unnamed x394, local copies, waits for them, and re-layouts  41.9 us
    pallas_call x1, Pallas kernels, pack_rows(): pl.pallas_call(functools.partial(pack_kernel, n, capacity), out_shape=(ja...  31.6 us
    pallas_call x2, Pallas kernels, gather_rows(): pl.pallas_call(functools.partial(gather_kernel, total), out_shape=jax.Sha...  31.5 us
  transfers between devices with their start and end apart: 3, of which 1 were waited for; matrix products, arithmetic and copies ran while one was open for 4% of the time, Pallas kernels for 7%

profile of v2, /device:TPU:0, one launch (start us, length us, event | category | flops | bytes accessed | tf_op | source)
XLA Modules:
  0.0 1447.6 jit_solution(17137379115517663948)
XLA Ops:
  8.5 12.4 push_inputs.1
  23.7 31.6 %pack_rows.2 = (bf16[9088,128]{1,0:T(8,128)(2,1)S(1)}, s32[9104]{0:T(1024)S(1)}) custom-call(s32[7776]{0:T(1024)S(1)} %get-tuple-element.222.pos_ref, s32[7776]{0:T(1024)S(1)} %get-tuple-element.473.slot_ref, s32[8]{0:T(128)S(1)} %broadcast_clamp_fusion.fill_ref, bf16[7776,128]{1,0:T(8,128)(2,1)S(1)} %bitcast.365), custom_call_target="tpu_custom_call" | custom-call | tf_op jit(solution)/shard_map/pack_rows/pallas_call | solution.py:613
  79.6 59.6 %push_hidden.1 = bf16[32,32,128]{2,1,0:T(8,128)(2,1)} custom-call(bf16[32,128]{1,0:T(8,128)(2,1)} %pad_bitcast_fusion.1.x_ref), custom_call_target="tpu_custom_call" | custom-call | tf_op jit(solution)/shard_map/push_hidden/pallas_call | solution.py:1028
  158.0 37.1 %sum_mods.1 = f32[32,1152]{1,0:T(8,128)S(1)} custom-call(f32[4,4,2,32,1152]{4,3,2,1,0:T(8,128)S(1)} %bitcast.353), custom_call_target="tpu_custom_call" | custom-call | bytes 9437184 | tf_op jit(solution)/shard_map/sum_mods/pallas_call | solution.py:976
  218.3 31.0 %all-gather = f32[16,1,256,16]{2,3,1,0:T(8,128)S(1)} all-gather(f32[2,1,256,16]{2,3,1,0:T(8,128)S(1)} %copy-done.129), channel_id=2, replica_groups=mesh['dp'=8,'mp'=4] {'dp'}, dimensions={0}, use_global_device_ids=true | all-gather | bytes 294912 | tf_op jit(solution)/shard_map/all_gather | solution.py:1432
  252.2 16.5 %scatter_rows.2 = f32[7792,128]{1,0:T(8,128)} custom-call(s32[9088]{0:T(1024)S(1)} %reshape.761.tag_ref.index_ref, bf16[9088,128]{1,0:T(8,128)(2,1)S(1)} %bitcast.355), custom_call_target="tpu_custom_call" | custom-call | tf_op jit(solution)/shard_map/scatter_rows/pallas_call | solution.py:632
  292.1 279.7 %gather_weights.1 = (bf16[4,2,144,3584]{3,2,1,0:T(8,128)(2,1)}, bf16[4,4,2,48,1152]{4,3,2,1,0:T(8,128)(2,1)S(1)}, bf16[4,2,144,4608]{3,2,1,0:T(8,128)(2,1)}, bf1...) custom-call(bf16[144,896]{1,0:T(8,128)(2,1)S(1)} %copy-done.7, ...), custom_call_target="tpu_custom_call" | custom-call | bytes 132120576 | tf_op jit(solution)/shard_map/gather_weights/pallas_call | solution.py:815
  618.7 10.8 multiply_convert_fusion.2
  660.4 8.3 fusion.226
  676.7 10.3 multiply_convert_fusion
  687.0 11.6 fusion.213
  705.4 9.0 convolution_convert_fusion
  714.4 16.1 %fusion.16 = bf16[512,4608]{1,0:T(8,128)(2,1)} fusion(f32[512,4608]{1,0:T(8,128)} %get-tuple-element.308, bf16[512,1152]{1,0:T(8,128)(2,1)S(1)} %bitcast.424, bf16[4608,1152]{1,0:T(8,128)(2,1)} %bitcast.492), kind=kOutput, calls=%fused_computation.37 | convolution fusion | flops 5483003904 | bytes 25952256 | tf_op jit(solution)/shard_map/dot_general | solution.py:41
  730.5 13.5 multiply_reduce_fusion.7
  769.8 13.7 fusion.65
  783.5 13.4 fusion.68
  808.8 8.9 reshape.792
  828.4 10.3 multiply_reduce_fusion.9
  841.0 9.0 fusion.29
  880.7 8.3 multiply_reduce_fusion.21
  889.4 25.4 %gather_vectors.1 = bf16[4,4,2,32,1152]{4,3,2,1,0:T(8,128)(2,1)S(1)} custom-call(bf16[32,1152]{1,0:T(8,128)(2,1)S(1)} %pad.64.refs_0_), custom_call_target="tpu_custom_call" | custom-call | bytes 4718592 | tf_op jit(solution)/shard_map/gather_vectors/pallas_call | solution.py:815
  935.0 8.4 convolution_convert_fusion.1
  979.4 16.8 %sum_shared.1 = f32[32,128]{1,0:T(8,128)S(1)} custom-call(f32[4,4,2,32,128]{4,3,2,1,0:T(8,128)S(1)} %bitcast.358), custom_call_target="tpu_custom_call" | custom-call | bytes 1048576 | tf_op jit(solution)/shard_map/sum_shared/pallas_call | solution.py:976
  997.9 8.9 convolution_convert_fusion.4
  1012.5 278.1 %sum_gradients.1 = (f32[144,896]{1,0:T(8,128)S(1)}, f32[48,1152]{1,0:T(8,128)S(1)}, f32[144,1152]{1,0:T(8,128)S(1)}, f32[144,1152]{1,0:T(8,128)S(1)}, f32[144,89...) custom-call(bf16[4,2,144,3584]{3,2,1,0:T(8,128)(2,1)} %bitcast.370, ...), custom_call_target="tpu_custom_call" | custom-call | bytes 132120576 | tf_op jit(solution)/shard_map/sum_gradients/pallas_call | solution.py:976
  1297.4 11.7 concatenate.45
  1309.1 11.4 concatenate.53.x_ref
  1327.7 9.8 push_totals.1
  1344.3 17.0 %gather_rows.6 = bf16[9088,128]{1,0:T(8,128)(2,1)} custom-call(s32[9088]{0:T(1024)S(1)} %copy-done.12, f32[7792,128]{1,0:T(8,128)} %concatenate.53.x_ref), custom_call_target="tpu_custom_call" | custom-call | tf_op jit(solution)/shard_map/gather_rows/pallas_call | solution.py:645
  1377.6 42.7 %all-to-all-done.6 = bf16[8,1136,128]{2,1,0:T(8,128)(2,1)S(1)} async-done(((bf16[8,1136,128]{2,1,0:T(8,128)(2,1)}), bf16[8,1136,128]{2,1,0:T(8,128)(2,1)S(1)}, u32[]{:S(2)}, u32[]{:S(2)}) %all-to-all-start.6) | async-done | bytes 2326560 | tf_op jit(solution)/shard_map/all_to_all | solution.py:1042
  1420.7 14.5 %gather_rows.7 = f32[7776,128]{1,0:T(8,128)} custom-call(s32[7776]{0:T(1024)S(1)} %copy-done.14, f32[9088,128]{1,0:T(8,128)S(1)} %bitcast_convert_fusion.1.x_ref), custom_call_target="tpu_custom_call" | custom-call | tf_op jit(solution)/shard_map/gather_rows/pallas_call | solution.py:645
  1435.2 11.1 fusion.211
  (642 shorter events, 367.4 us)
Async XLA Ops:
  0.6 23.0 %copy-start.21 = (bf16[1,7776,128]{2,1,0:T(8,128)(2,1)S(1)}, bf16[1,7776,128]{2,1,0:T(8,128)(2,1)}, u32[]{:S(2)}) copy-start(bf16[1,7776,128]{2,1,0:T(8,128)(2,1)} %param.24) | copy-start | bytes 5971972
  2.0 143.6 %copy-start.91 = (bf16[36,2442]{1,0:T(8,128)(2,1)}, bf16[36,2442]{1,0:T(8,128)(2,1)S(1)}, u32[]{:S(2)}) copy-start(bf16[36,2442]{1,0:T(8,128)(2,1)S(1)} %reshape.746) | copy-start | bytes 527476
  5.0 18.7 %copy-start.40 = (s32[7776]{0:T(1024)}, s32[7776]{0:T(1024)S(1)}, u32[]{:S(2)}) copy-start(s32[7776]{0:T(1024)S(1)} %get-tuple-element.472) | copy-start | bytes 93316
  5.0 50.3 %copy-start.79 = (s32[7776]{0:T(1024)}, s32[7776]{0:T(1024)S(1)}, u32[]{:S(2)}) copy-start(s32[7776]{0:T(1024)S(1)} %get-tuple-element.473.slot_ref) | copy-start | bytes 93316
  5.7 58.7 %copy-start.163 = (s32[2,1]{0,1:T(1,128)S(1)}, s32[2,1]{0,1:T(1,128)}, u32[]{:S(2)}) copy-start(s32[2,1]{0,1:T(1,128)} %param.41) | copy-start | bytes 28
  5.8 64.3 %copy-start.144 = (f32[2,1,128,16]{2,3,1,0:T(8,128)S(1)}, f32[2,1,128,16]{2,3,1,0:T(8,128)}, u32[]{:S(2)}) copy-start(f32[2,1,128,16]{2,3,1,0:T(8,128)} %param.37) | copy-start | bytes 49156
  57.6 11.8 copy-start.145
  57.6 11.8 copy-start.147
  58.4 14.1 all-to-all-start.4
  72.5 66.7 %copy-start.104 = (s32[8,1,1136]{2,1,0:T(1,128)}, s32[8,1,1136]{2,1,0:T(1,128)S(1)}, u32[]{:S(2)}) copy-start(s32[8,1,1136]{2,1,0:T(1,128)S(1)} %all-to-all-done.4) | copy-start | bytes 109060
  72.5 179.7 %all-to-all-start.5 = ((bf16[8,1136,128]{2,1,0:T(8,128)(2,1)}), bf16[8,1136,128]{2,1,0:T(8,128)(2,1)S(1)}, u32[]{:S(2)}, u32[]{:S(2)}) async-start(bf16[8,1136,128]{2,1,0:T(8,128)(2,1)} %bitcast.357), calls=%async_computation.5 | async-start | bytes 4653056 | tf_op jit(solution)/shard_map/all_to_all | solution.py:1042
  195.2 14.8 %copy-start.141 = (s32[2,1,128]{2,1,0:T(1,128)S(1)}, s32[2,1,128]{2,1,0:T(1,128)}, u32[]{:S(2)}) copy-start(s32[2,1,128]{2,1,0:T(1,128)} %param.38) | copy-start | bytes 3076
  215.8 34.2 %copy-start.45 = (bf16[1152,33]{1,0:T(8,128)(2,1)S(1)}, bf16[1152,33]{1,0:T(8,128)(2,1)}, u32[]{:S(2)}) copy-start(bf16[1152,33]{1,0:T(8,128)(2,1)} %convert_element_type.308) | copy-start | bytes 228100
  215.8 36.2 %copy-start.105 = (s32[8,1,1136]{2,1,0:T(1,128)S(1)}, s32[8,1,1136]{2,1,0:T(1,128)}, u32[]{:S(2)}) copy-start(s32[8,1,1136]{2,1,0:T(1,128)} %copy-done.104) | copy-start | bytes 109060
  252.0 380.9 %copy-start.137 = (f32[2,256]{1,0:T(2,128)}, f32[2,256]{1,0:T(2,128)S(1)}, u32[]{:S(2)}) copy-start(f32[2,256]{1,0:T(2,128)S(1)} %get-tuple-element.279) | copy-start | bytes 6148
  252.2 16.5 %copy-start.11 = (s32[9088]{0:T(1024)}, s32[9088]{0:T(1024)S(1)}, u32[]{:S(2)}) copy-start(s32[9088]{0:T(1024)S(1)} %reshape.761.tag_ref.index_ref) | copy-start | bytes 109060
  618.0 14.9 %copy-start.24 = (f32[2,128,1152]{2,1,0:T(8,128)}, f32[2,128,1152]{2,1,0:T(8,128)S(1)}, u32[]{:S(2)}) copy-start(f32[2,128,1152]{2,1,0:T(8,128)S(1)} %get-tuple-element.236) | copy-start | bytes 3538948
  618.3 17.9 %slice-start.9 = ((s8[8257536]{0:T(1024)(128)(4,1)}), s8[4194304]{0:T(1024)(128)(4,1)S(1)}, s32[]{:S(2)}) async-start(s8[8257536]{0:T(1024)(128)(4,1)} %bitcast.496), calls=%async_computation.16 | async-start | bytes 8388608
  618.7 17.5 %slice-start.10 = ((s8[8257536]{0:T(1024)(128)(4,1)}), s8[4063232]{0:T(1024)(128)(4,1)S(1)}, s32[]{:S(2)}) async-start(s8[8257536]{0:T(1024)(128)(4,1)} %bitcast.496), calls=%async_computation.17 | async-start | bytes 8126464
  769.8 13.7 copy-start.82
  914.8 20.1 %slice-start.11 = ((s8[4718592]{0:T(1024)(128)(4,1)}), s8[524288]{0:T(1024)(128)(4,1)S(1)}, s32[]{:S(2)}) async-start(s8[4718592]{0:T(1024)(128)(4,1)} %bitcast.500), calls=%async_computation.18 | async-start | bytes 1048576
  978.8 18.0 %copy-start.146 = (bf16[64,128]{1,0:T(8,128)(2,1)S(1)}, bf16[64,128]{1,0:T(8,128)(2,1)}, u32[]{:S(2)}) copy-start(bf16[64,128]{1,0:T(8,128)(2,1)} %copy-done.145) | copy-start | bytes 49156
  978.8 18.0 %copy-start.148 = (bf16[64,128]{1,0:T(8,128)(2,1)S(1)}, bf16[64,128]{1,0:T(8,128)(2,1)}, u32[]{:S(2)}) copy-start(bf16[64,128]{1,0:T(8,128)(2,1)} %copy-done.147) | copy-start | bytes 49156
  978.8 18.0 %copy-start.168 = (f32[64,36]{0,1:T(8,128)S(1)}, f32[64,36]{0,1:T(8,128)}, u32[]{:S(2)}) copy-start(f32[64,36]{0,1:T(8,128)} %get-tuple-element.296) | copy-start | bytes 27652
  978.8 18.1 %copy-start.92 = (f32[36,1152]{1,0:T(8,128)S(1)}, f32[36,1152]{1,0:T(8,128)}, u32[]{:S(2)}) copy-start(f32[36,1152]{1,0:T(8,128)} %fusion.204) | copy-start | bytes 497668
  978.8 18.1 %copy-start.95 = (f32[36,1001]{1,0:T(8,128)S(1)}, f32[36,1001]{1,0:T(8,128)}, u32[]{:S(2)}) copy-start(f32[36,1001]{1,0:T(8,128)} %fusion.111) | copy-start | bytes 432436
  979.3 18.6 %copy-start.86 = (bf16[2,256,1152]{2,1,0:T(8,128)(2,1)S(1)}, bf16[2,256,1152]{2,1,0:T(8,128)(2,1)}, u32[]{:S(2)}) copy-start(bf16[2,256,1152]{2,1,0:T(8,128)(2,1)} %copy-done.85) | copy-start | bytes 3538948
  1320.5 19.3 %copy-start.37 = (f32[36,16128]{1,0:T(8,128)S(1)}, f32[36,16128]{1,0:T(8,128)}, u32[]{:S(2)}) copy-start(f32[36,16128]{1,0:T(8,128)} %get-tuple-element.318) | copy-start | bytes 6967300
  1361.3 59.0 %all-to-all-start.6 = ((bf16[8,1136,128]{2,1,0:T(8,128)(2,1)}), bf16[8,1136,128]{2,1,0:T(8,128)(2,1)S(1)}, u32[]{:S(2)}, u32[]{:S(2)}) async-start(bf16[8,1136,128]{2,1,0:T(8,128)(2,1)} %bitcast.103), calls=%async_computation.6 | async-start | bytes 4653056 | tf_op jit(solution)/shard_map/all_to_all | solution.py:1042
  1377.6 43.0 %copy-start.14 = (s32[7776]{0:T(1024)S(1)}, s32[7776]{0:T(1024)}, u32[]{:S(2)}) copy-start(s32[7776]{0:T(1024)} %get-tuple-element.221.index_ref) | copy-start | bytes 93316
  1420.7 14.5 %copy-start.39 = (s32[7776]{0:T(1024)S(1)}, s32[7776]{0:T(1024)}, u32[]{:S(2)}) copy-start(s32[7776]{0:T(1024)} %copy-done.38) | copy-start | bytes 93316
  1420.7 14.5 %copy-start.42 = (s32[7776]{0:T(1024)S(1)}, s32[7776]{0:T(1024)}, u32[]{:S(2)}) copy-start(s32[7776]{0:T(1024)} %copy-done.40) | copy-start | bytes 93316
  (151 other events, 663.3 us)

commit v3 on v2

--- a/solution.py
+++ b/solution.py
@@ -495,7 +495,7 @@
     )
 
 
-CHUNK_ROWS = 1136
+CHUNK_ROWS = 1152
 REST_ROWS = 2 * PD + FREQ + D + CLASSES + 1
 
 
@@ -541,7 +541,7 @@
 
 
 def widen(source, dest, rows):
-    step = 16
+    step = 128 if rows % 128 == 0 else 16
     whole = rows // step
 
     def body(i, unused):
@@ -552,49 +552,40 @@
     lax.fori_loop(0, whole, body, 0)
 
 
-def pack_kernel(n, capacity, pos_ref, slot_ref, fill_ref, x_ref, buf_ref, tag_ref, wide, sorted_rows):
-    ranks = fill_ref.shape[0]
-    total = ranks * capacity
+def pack_kernel(n, pos_ref, x_ref, buf_ref, wide, sorted_rows):
     widen(x_ref, wide, n)
 
-    def fill(r, unused):
-        def one(i, carry):
-            tag_ref[r * capacity + i] = n
-            return carry
-
-        return lax.fori_loop(fill_ref[r], capacity, one, unused)
-
-    lax.fori_loop(0, ranks, fill, 0)
-
     def move(i, unused):
-        for j in range(16):
-            k = i * 16 + j
-            p = pos_ref[k]
-            sorted_rows[pl.ds(p, 1), :] = wide[pl.ds(k, 1), :]
-            tag_ref[p] = slot_ref[k]
+        places = [pos_ref[i * 16 + j] for j in range(16)]
+        rows = [wide[pl.ds(i * 16 + j, 1), :] for j in range(16)]
+        for place, row in zip(places, rows):
+            sorted_rows[pl.ds(place, 1), :] = row
         return unused
 
     lax.fori_loop(0, n // 16, move, 0)
-    widen(sorted_rows, buf_ref, total)
-
-
-def scatter_kernel(n, total, tag_ref, buf_ref, out_ref, wide):
+    widen(sorted_rows, buf_ref, buf_ref.shape[0])
+
+
+def scatter_kernel(total, tag_ref, buf_ref, out_ref, wide, slots):
     widen(buf_ref, wide, total)
 
     def move(i, unused):
-        for j in range(16):
-            k = i * 16 + j
-            out_ref[pl.ds(tag_ref[k], 1), :] = wide[pl.ds(k, 1), :]
+        tags = [tag_ref[i * 16 + j] for j in range(16)]
+        rows = [wide[pl.ds(i * 16 + j, 1), :] for j in range(16)]
+        for tag, row in zip(tags, rows):
+            slots[pl.ds(tag, 1), :] = row
         return unused
 
     lax.fori_loop(0, total // 16, move, 0)
+    widen(slots, out_ref, out_ref.shape[0])
 
 
 def gather_kernel(total, index_ref, x_ref, out_ref, wide_out):
     def move(i, unused):
+        index = [index_ref[i * 16 + j] for j in range(16)]
+        rows = [x_ref[pl.ds(place, 1), :] for place in index]
         for j in range(16):
-            k = i * 16 + j
-            wide_out[pl.ds(k, 1), :] = x_ref[pl.ds(index_ref[k], 1), :]
+            wide_out[pl.ds(i * 16 + j, 1), :] = rows[j]
         return unused
 
     lax.fori_loop(0, total // 16, move, 0)
@@ -606,35 +597,47 @@
 PARAMS = pltpu.CompilerParams(vmem_limit_bytes=48 * 1024 * 1024)
 
 
-def pack_rows(rows, pos, slot, fill, capacity):
+def pack_rows(rows, pos, total):
     n = rows.shape[0]
-    ranks = fill.shape[0]
-    total = ranks * capacity
     return pl.pallas_call(
-        functools.partial(pack_kernel, n, capacity),
-        out_shape=(
-            jax.ShapeDtypeStruct((total, 128), jnp.bfloat16),
-            jax.ShapeDtypeStruct((total + 16,), jnp.int32),
-        ),
-        in_specs=[SMEM, SMEM, SMEM, VMEM],
-        out_specs=(VMEM, SMEM),
+        functools.partial(pack_kernel, n),
+        out_shape=jax.ShapeDtypeStruct((total, 128), jnp.bfloat16),
+        in_specs=[SMEM, VMEM],
+        out_specs=VMEM,
         scratch_shapes=[
             pltpu.VMEM((n, 128), jnp.float32),
             pltpu.VMEM((total + 16, 128), jnp.float32),
         ],
         compiler_params=PARAMS,
         name="pack_rows",
-    )(pos, slot, fill, rows)
+    )(pos, rows)
+
+
+def pack_tags(pos, slot, fill, capacity):
+    n = pos.shape[0]
+    total = fill.shape[0] * capacity
+    lines = total // 128
+    here = (pos // 128)[:, None] == jnp.arange(lines)[None, :]
+    high = jnp.where(here, (slot // 128)[:, None], 0)
+    low = jnp.where(here, (slot % 128)[:, None], 0)
+    lanes = ((pos % 128)[:, None] == jnp.arange(128)[None, :]).astype(jnp.bfloat16)
+    parts = jnp.concatenate([high, low], axis=1).astype(jnp.bfloat16)
+    found = contract(parts, lanes, 0, 0).astype(jnp.int32)
+    tags = (found[:lines] * 128 + found[lines:]).reshape(fill.shape[0], capacity)
+    return jnp.where(jnp.arange(capacity)[None, :] < fill[:, None], tags, n).reshape(-1)
 
 
 def scatter_rows(rows, tags, n):
     total = rows.shape[0]
     return pl.pallas_call(
-        functools.partial(scatter_kernel, n, total),
-        out_shape=jax.ShapeDtypeStruct((n + 16, 128), jnp.float32),
+        functools.partial(scatter_kernel, total),
+        out_shape=jax.ShapeDtypeStruct((n + 16, 128), jnp.bfloat16),
         in_specs=[SMEM, VMEM],
         out_specs=VMEM,
-        scratch_shapes=[pltpu.VMEM((total, 128), jnp.float32)],
+        scratch_shapes=[
+            pltpu.VMEM((total, 128), jnp.float32),
+            pltpu.VMEM((n + 16, 128), jnp.float32),
+        ],
         compiler_params=PARAMS,
         name="scatter_rows",
     )(tags, rows)
@@ -725,16 +728,14 @@
     )
 
 
-def gather_whole_kernel(plan, chunk, *refs):
+def gather_job(plan, chunk, slices, wholes, scratch):
     count = len(plan)
-    slices, wholes = refs[:count], refs[count : 2 * count]
-    held, other_held, own_sem, out_sem, z_send, z_recv, a_send, a_recv, b_send, b_recv, c_send, c_recv = refs[2 * count :]
+    held, other_held, own_sem, out_sem, z_send, z_recv, a_send, a_recv, b_send, b_recv, c_send, c_recv = scratch
     z, x, y, core = coordinates()
     other, first, second, others = neighbours()
     mine_first = jnp.where(core == 0, y, x)
     mine_second = jnp.where(core == 0, x, y)
     ranges, total = chunk_ranges(plan, chunk)
-    greet([other, first, second] + others)
 
     def copies(stage, k, unit):
         entry = plan[k]
@@ -786,16 +787,15 @@
                     for copy in copies(stage, k, unit):
                         copy.start()
 
-    def step(t, unused):
+    def step(t):
         go(t - 1 - 4 * LAG, (4, 5), ())
         go(t - 4 * LAG, (3,), (5,))
         go(t - 3 * LAG, (2,), (3, 4))
         go(t - 2 * LAG, (1,), (2,))
         go(t - LAG, (0,), (1,))
         go(t, (), (0,))
-        return unused
-
-    lax.fori_loop(0, total + 1 + 4 * LAG, step, 0)
+
+    return step, total + 1 + 4 * LAG
 
 
 def whole_shape(entry):
@@ -803,44 +803,23 @@
     return (4, 4, 2, rows, width) if stacked else (4, 2, rows, 4 * width)
 
 
-def gather_whole(plan, slices, chunk, number, name):
-    ANY = pl.BlockSpec(memory_space=pl.ANY)
-    count = len(plan)
+def gather_scratch(plan, chunk, kind):
     dma = pltpu.SemaphoreType.DMA
-    kind = slices[0].dtype
-    size = sum(math.prod(whole_shape(entry)) for entry in plan) * kind.itemsize
     held = pltpu.VMEM((GATHER_SLOTS, 2, 2, 4, chunk, max(entry[2] for entry in plan)), kind)
     each = dma((GATHER_SLOTS,))
     three = dma((3, GATHER_SLOTS))
-    return pl.pallas_call(
-        functools.partial(gather_whole_kernel, plan, chunk),
-        out_shape=[jax.ShapeDtypeStruct(whole_shape(entry), kind) for entry in plan],
-        in_specs=[ANY] * count,
-        out_specs=[ANY] * count,
-        scratch_shapes=[held, held, each, dma((2, 4, GATHER_SLOTS)), three, three] + [each] * 6,
-        compiler_params=pltpu.CompilerParams(
-            collective_id=number, has_side_effects=True, vmem_limit_bytes=48 * 1024 * 1024
-        ),
-        cost_estimate=pl.CostEstimate(flops=0, bytes_accessed=2 * size, transcendentals=0),
-        name=name,
-    )(*slices)
-
-
-def sum_slices_kernel(plan, chunk, *refs):
+    return [held, held, each, dma((2, 4, GATHER_SLOTS)), three, three] + [each] * 6
+
+
+def sum_job(plan, chunk, parts, outs, scratch):
     count = len(plan)
-    parts, outs = refs[:count], refs[count : 2 * count]
-    (own, from_core, from_first, from_second, from_z, half, quarter, eighth) = refs[
-        2 * count : 2 * count + 8
-    ]
-    own_sem, core_send, core_recv, a_send, a_recv, b_send, b_recv, z_send, z_recv = refs[
-        2 * count + 8 :
-    ]
+    own, from_core, from_first, from_second, from_z, half, quarter, eighth = scratch[:8]
+    own_sem, core_send, core_recv, a_send, a_recv, b_send, b_recv, z_send, z_recv = scratch[8:]
     z, x, y, core = coordinates()
     other, first, second, others = neighbours()
     mine_first = jnp.where(core == 0, y, x)
     mine_second = jnp.where(core == 0, x, y)
     ranges, total = chunk_ranges(plan, chunk)
-    greet([other, first, second] + others)
 
     def copies(stage, width, unit, k=None):
         slot = lax.rem(unit, SLOTS)
@@ -946,23 +925,19 @@
                 for copy in copies(0, plan[k][2], unit, k):
                     copy.start()
 
-    def step(t, unused):
+    def step(t):
         finish(t - 1 - 3 * LAG)
         go(t - 1 - 2 * LAG, 2)
         go(t - 1 - LAG, 1)
         go(t - 1, 0)
         begin(t)
-        return unused
-
-    lax.fori_loop(0, total + 1 + 3 * LAG, step, 0)
-
-
-def sum_slices(plan, parts, chunk, number, name):
-    count = len(plan)
+
+    return step, total + 1 + 3 * LAG
+
+
+def sum_scratch(plan, chunk, kind):
     dma = pltpu.SemaphoreType.DMA
-    kind = parts[0].dtype
     width = max(entry[2] for entry in plan)
-    size = sum(math.prod(whole_shape(entry)) for entry in plan) * kind.itemsize
     buffers = [
         (2, 2, 4, 2, chunk, width),
         (2, 2, 4, 2, chunk, width),
@@ -973,21 +948,145 @@
         (SLOTS, 2, 4, chunk, width),
         (SLOTS, 4, chunk, width),
     ]
-    return pl.pallas_call(
-        functools.partial(sum_slices_kernel, plan, chunk),
-        out_shape=[jax.ShapeDtypeStruct((entry[1], entry[2]), jnp.float32) for entry in plan],
-        in_specs=[pl.BlockSpec(memory_space=pl.ANY)] * count,
-        out_specs=[VMEM] * count,
-        scratch_shapes=[pltpu.VMEM(shape, kind) for shape in buffers]
+    return (
+        [pltpu.VMEM(shape, kind) for shape in buffers]
         + [dma((2, 2))] * 3
         + [dma((SLOTS,))] * 4
-        + [dma((3, SLOTS))] * 2,
+        + [dma((3, SLOTS))] * 2
+    )
+
+
+def direct_job(kind, sources, targets, scratch):
+    source, target = sources[0], targets[0]
+    own_sem, send_sem, recv_sem = scratch
+    ranks, groups = lax.axis_size("dp"), lax.axis_size("mp")
+    rank, group = lax.axis_index("dp"), lax.axis_index("mp")
+    me, count = (rank * groups + group, ranks * groups) if kind == "push" else (rank, ranks)
+
+    def part(index):
+        return source.at[index] if kind == "swap" else source
+
+    own = pltpu.make_async_copy(part(me), target.at[me], own_sem)
+
+    def copy(i):
+        to = lax.rem(me + i, count)
+        peer = (lax.div(to, groups), lax.rem(to, groups)) if kind == "push" else (to, group)
+        return remote(part(to), target.at[me], send_sem.at[i], recv_sem.at[i], peer)
+
+    def start(i, unused):
+        copy(i).start()
+        return unused
+
+    def finish(i, unused):
+        copy(i).wait()
+        return unused
+
+    def begin():
+        own.start()
+        lax.fori_loop(1, count, start, 0)
+
+    def end():
+        own.wait()
+        lax.fori_loop(1, count, finish, 0)
+
+    return begin, end
+
+
+def travel_kernel(jobs, scratch_counts, *refs):
+    refs = list(refs)
+
+    def take(number):
+        taken = refs[:number]
+        del refs[:number]
+        return taken
+
+    sources = [take(len(job[1])) for job in jobs]
+    targets = [take(len(job[1])) for job in jobs]
+    scratch = [take(number) for number in scratch_counts]
+    steps = []
+    direct = []
+    for (kind, plan, chunk), source, target, mine in zip(jobs, sources, targets, scratch):
+        if kind == "gather":
+            steps.append(gather_job(plan, chunk, source, target, mine))
+        elif kind == "sum":
+            steps.append(sum_job(plan, chunk, source, target, mine))
+        else:
+            direct.append(direct_job(kind, source, target, mine))
+    if direct:
+        greet_all()
+    else:
+        other, first, second, others = neighbours()
+        greet([other, first, second] + others)
+    for begin, unused_end in direct:
+        begin()
+
+    def step(t, unused):
+        for one, unused_count in steps:
+            one(t)
+        return unused
+
+    if steps:
+        lax.fori_loop(0, max(count for unused_step, count in steps), step, 0)
+    for unused_begin, end in direct:
+        end()
+
+
+def greet_all():
+    groups = lax.axis_size("mp")
+    world = lax.axis_size("dp") * groups
+    me = lax.axis_index("dp") * groups + lax.axis_index("mp")
+    barrier = pltpu.get_barrier_semaphore()
+
+    def hail(i, unused):
+        to = lax.rem(me + i, world)
+        peer = (lax.div(to, groups), lax.rem(to, groups))
+        pl.semaphore_signal(barrier, inc=1, device_id=peer, device_id_type=MESH)
+        return unused
+
+    lax.fori_loop(1, world, hail, 0)
+    pl.semaphore_wait(barrier, world - 1)
+
+
+def travel(jobs, arrays, number, name):
+    ANY = pl.BlockSpec(memory_space=pl.ANY)
+    dma = pltpu.SemaphoreType.DMA
+    ranks, groups = lax.axis_size("dp"), lax.axis_size("mp")
+    scratch = []
+    shapes = []
+    specs = []
+    for (kind, plan, chunk), mine in zip(jobs, arrays):
+        dtype = mine[0].dtype
+        if kind == "gather":
+            scratch.append(gather_scratch(plan, chunk, dtype))
+            shapes += [jax.ShapeDtypeStruct(whole_shape(entry), dtype) for entry in plan]
+            specs += [ANY] * len(plan)
+        elif kind == "sum":
+            scratch.append(sum_scratch(plan, chunk, dtype))
+            shapes += [jax.ShapeDtypeStruct(entry[1:], jnp.float32) for entry in plan]
+            specs += [VMEM] * len(plan)
+        else:
+            count = ranks * groups if kind == "push" else ranks
+            scratch.append([dma, dma((count,)), dma((count,))])
+            shape = mine[0].shape if kind == "swap" else (count,) + mine[0].shape
+            shapes.append(jax.ShapeDtypeStruct(shape, dtype))
+            specs.append(ANY)
+    flat = [array for mine in arrays for array in mine]
+    outs = pl.pallas_call(
+        functools.partial(travel_kernel, jobs, [len(mine) for mine in scratch]),
+        out_shape=shapes,
+        in_specs=[ANY] * len(flat),
+        out_specs=specs,
+        scratch_shapes=[one for mine in scratch for one in mine],
         compiler_params=pltpu.CompilerParams(
             collective_id=number, has_side_effects=True, vmem_limit_bytes=48 * 1024 * 1024
         ),
-        cost_estimate=pl.CostEstimate(flops=0, bytes_accessed=2 * size, transcendentals=0),
         name=name,
-    )(*parts)
+    )(*flat)
+    results = []
+    for unused_kind, plan, unused_chunk in jobs:
+        results.append(outs[: len(plan)])
+        outs = outs[len(plan) :]
+    return results
 
 
 def push_kernel(world, x_ref, out_ref, send_sem, recv_sem):
@@ -1051,73 +1150,48 @@
     return pos, fill, inside
 
 
-def tiles_to_slots(rows, dest, slot, rank, counts, rounds):
+def tiles_to_slots(rows, dest, slot, rank, counts, rounds, carry_first):
     n = rows.shape[0]
     ranks = counts.shape[0]
-
-    def turn_of(turn):
+    total = ranks * CHUNK_ROWS
+
+    def packed(turn):
         pos, fill, unused = round_positions(dest, rank, counts, CHUNK_ROWS, turn)
-        buf, tags = pack_rows(rows, pos, slot, fill, CHUNK_ROWS)
-        got = swap_ranks(buf, ranks)
-        got_tags = swap_ranks(tags[: ranks * CHUNK_ROWS], ranks)
-        return scatter_rows(got, got_tags, n), got_tags
-
-    first, tags = turn_of(0)
+        return pack_rows(rows, pos, total), pack_tags(pos, slot, fill, CHUNK_ROWS)
+
+    got, tags = carry_first(*packed(0))
+    first = scatter_rows(got, tags, n)
 
     def more(carry):
         turn, slots = carry
-        added, more_tags = turn_of(turn)
+        more_rows, more_tags = [swap_ranks(part, ranks) for part in packed(turn)]
+        added = scatter_rows(more_rows, more_tags, n)
         fresh = jnp.zeros((n + 16,), jnp.bool_).at[more_tags].set(True)
         return turn + 1, jnp.where(fresh[:, None], added, slots)
 
     unused, slots = lax.while_loop(lambda carry: carry[0] < rounds, more, (1, first))
-    return slots[:n], tags
-
-
-def slots_to_tiles(slots, tags, dest, slot, rank, counts, rounds):
-    n = dest.shape[0]
+    return slots, tags
+
+
+def slots_to_tiles(slots, first, dest, slot, rank, counts, rounds):
     ranks = counts.shape[0]
-    padded = jnp.concatenate([slots, jnp.zeros((16, 128), slots.dtype)])
-
-    def turn_of(turn, turn_tags):
+    total = ranks * CHUNK_ROWS
+
+    def landed(got, turn):
         pos, unused, inside = round_positions(dest, rank, counts, CHUNK_ROWS, turn)
-        buf = gather_rows(padded, turn_tags, jnp.bfloat16)
-        got = swap_ranks(buf, ranks).astype(jnp.float32)
-        return gather_rows(got, jnp.minimum(pos, ranks * CHUNK_ROWS - 1), jnp.float32), inside
-
-    first, unused = turn_of(0, tags)
+        return gather_rows(got, jnp.minimum(pos, total - 1), jnp.float32), inside
 
     def more(carry):
         turn, rows = carry
         pos, fill, unused = round_positions(dest, rank, counts, CHUNK_ROWS, turn)
-        empty = jnp.full((ranks * CHUNK_ROWS + 1,), n, jnp.int32)
-        turn_tags = swap_ranks(empty.at[pos].set(slot)[:-1].at[:].get(), ranks)
-        added, inside = turn_of(turn, turn_tags)
+        turn_tags = swap_ranks(pack_tags(pos, slot, fill, CHUNK_ROWS), ranks)
+        got = swap_ranks(gather_rows(slots, turn_tags, jnp.bfloat16), ranks)
+        added, inside = landed(got.astype(jnp.float32), turn)
         return turn + 1, jnp.where(inside[:, None], added, rows)
 
-    unused, rows = lax.while_loop(lambda carry: carry[0] < rounds, more, (1, first))
+    start = (1, landed(first.astype(jnp.float32), 0)[0])
+    unused, rows = lax.while_loop(lambda carry: carry[0] < rounds, more, start)
     return rows
-
-
-def slot_matrices(slots, ranks):
-    widths = [3 * HEADS * HD // 4, D, FF // 4, D]
-    levels = [[], []]
-    base = 0
-    for total, width in zip(matrix_tiles(), widths):
-        count = total // ranks
-        for level in range(2):
-            part = slots[base : base + count]
-            levels[level].append(part.reshape(count * 128 // width, width))
-            base += count
-    return levels
-
-
-def matrices_slots(levels):
-    parts = []
-    for index in range(4):
-        for level in range(2):
-            parts.append(levels[level][index].reshape(-1, 128))
-    return jnp.concatenate(parts)
 
 
 QKV_WIDTH = 896
@@ -1139,42 +1213,253 @@
     return jnp.pad(values, widths)
 
 
-def pad_slices(level):
-    return [pad_to(level[0], 1, QKV_WIDTH), pad_to(level[1], 0, PROJ_ROWS), level[2], level[3]]
-
-
-def trim_slices(level, ranks):
-    return [level[0][:, : 3 * HEADS * HD // 4], level[1][: HEADS * HD // 4 // ranks], level[2], level[3]]
+def slice_places(ranks):
+    widths = [3 * HEADS * HD // 4, D, FF // 4, D]
+    places = []
+    base = 0
+    for total, width in zip(matrix_tiles(), widths):
+        count = total // ranks
+        places.append((count * 128 // width, width, (base, base + count)))
+        base += 2 * count
+    return places
+
+
+def row_group(width):
+    rows = 128 // math.gcd(width, 128)
+    return rows, rows * width // 128
+
+
+def lane_pieces(start, size, source_width):
+    pieces = []
+    done = 0
+    while done < size:
+        row, column = divmod(start + done, source_width)
+        block, lane = divmod(column, 128)
+        length = min(128 - lane, source_width - column, size - done)
+        pieces.append((row, block, lane, done, length))
+        done += length
+    return pieces
+
+
+def join_pieces(pieces, load, rows):
+    lanes = lax.broadcasted_iota(jnp.int32, (rows, 128), 1)
+    value = None
+    for row, block, lane, here, length in pieces:
+        part = load(row, block)
+        if lane != here:
+            part = pltpu.roll(part, (here - lane) % 128, 1)
+        if value is None:
+            inside = lanes < here + length
+            value = part if here + length == 128 else jnp.where(inside, part, 0.0)
+        else:
+            value = jnp.where((lanes >= here) & (lanes < here + length), part, value)
+    return value
+
+
+def spread_kernel(ranks, low_ref, *refs):
+    outs, wide, slots_ref = refs[:8], refs[8], refs[9]
+    widen(low_ref, slots_ref, low_ref.shape[0])
+    for index, (rows, width, bases) in enumerate(slice_places(ranks)):
+        group, tiles = row_group(width)
+        count = rows // group
+        blocks = -(-width // 128)
+        for level in range(2):
+            out = outs[level * 4 + index]
+            for row in range(group):
+                for block in range(blocks):
+                    start = row * width + block * 128
+                    pieces = lane_pieces(start, min(128, width - block * 128), 128)
+
+                    def load(tile, unused, base=bases[level]):
+                        return slots_ref[pl.ds(base + tile, count, stride=tiles), :]
+
+                    value = join_pieces(pieces, load, count)
+                    at = pl.ds(row, count, stride=group) if group > 1 else pl.ds(0, count)
+                    wide[block, at, :] = value
+            padded = out.shape[0]
+            for block in range(blocks):
+                if padded > rows:
+                    wide[block, rows:padded, :] = jnp.zeros((padded - rows, 128), jnp.float32)
+                out[:, block * 128 : (block + 1) * 128] = wide[block, :padded, :].astype(out.dtype)
+
+
+def collect_kernel(ranks, *refs):
+    parts, slots_ref, square_ref, wide = refs[:8], refs[8], refs[9], refs[10]
+    square_ref[...] = jnp.zeros_like(square_ref)
+    end = slots_ref.shape[0]
+    total = 0
+    for index, (rows, width, bases) in enumerate(slice_places(ranks)):
+        group, tiles = row_group(width)
+        count = rows // group
+        total += 2 * count * tiles
+        for level in range(2):
+            part = parts[level * 4 + index]
+            for block in range(-(-width // 128)):
+                wide[block, :rows, :] = part[:rows, block * 128 : (block + 1) * 128]
+            for tile in range(tiles):
+                pieces = lane_pieces(tile * 128, 128, width)
+
+                def load(row, block):
+                    at = pl.ds(row, count, stride=group) if group > 1 else pl.ds(0, count)
+                    return wide[block, at, :]
+
+                value = join_pieces(pieces, load, count)
+                slots_ref[pl.ds(bases[level] + tile, count, stride=tiles), :] = value
+                square_ref[:1, :] += jnp.sum(value * value, axis=0, keepdims=True)
+    slots_ref[total:end, :] = jnp.zeros((end - total, 128), jnp.float32)
+
+
+def spread_slots(slots, ranks):
+    plan = layer_plan(ranks) * 2
+    tall = max(entry[1] for entry in plan)
+    broad = max(entry[2] for entry in plan)
+    return pl.pallas_call(
+        functools.partial(spread_kernel, ranks),
+        out_shape=[jax.ShapeDtypeStruct(entry[1:], jnp.bfloat16) for entry in plan],
+        in_specs=[VMEM],
+        out_specs=[VMEM] * len(plan),
+        scratch_shapes=[
+            pltpu.VMEM((broad // 128, tall, 128), jnp.float32),
+            pltpu.VMEM(slots.shape, jnp.float32),
+        ],
+        compiler_params=PARAMS,
+        name="spread_slots",
+    )(slots)
+
+
+def collect_slots(parts, rows, ranks):
+    tall = max(part.shape[0] for part in parts)
+    broad = max(part.shape[1] for part in parts)
+    return pl.pallas_call(
+        functools.partial(collect_kernel, ranks),
+        out_shape=(
+            jax.ShapeDtypeStruct((rows, 128), jnp.float32),
+            jax.ShapeDtypeStruct((8, 128), jnp.float32),
+        ),
+        in_specs=[VMEM] * len(parts),
+        out_specs=(VMEM, VMEM),
+        scratch_shapes=[pltpu.VMEM((broad // 128, tall, 128), jnp.float32)],
+        compiler_params=PARAMS,
+        name="collect_slots",
+    )(*parts)
 
 
 def whole_weights(wholes, ranks):
     qkv, proj, up, down = wholes
-    own_rows = HEADS * HD // 4 // ranks
-    proj = proj.reshape(4, ranks, PROJ_ROWS, D)[:, :, :own_rows].reshape(-1, D)
-    return (qkv.reshape(D, -1), proj, up.reshape(D, -1), down.reshape(-1, D))
+    return (qkv.reshape(D, -1), proj.reshape(-1, D), up.reshape(D, -1), down.reshape(-1, D))
 
 
 def whole_parts(grads, ranks):
     qkv, proj, up, down = grads
     shapes = [whole_shape(entry) for entry in layer_plan(ranks)]
-    proj = pad_to(proj.reshape(4, ranks, -1, D), 2, PROJ_ROWS)
     return [part.reshape(shape) for part, shape in zip((qkv, proj, up, down), shapes)]
 
 
-def heads_of(packed, images):
-    split = packed.reshape(images, -1, 4, QKV_WIDTH)[..., : 3 * HEADS * HD // 4]
-    split = split.reshape(images, -1, 4, 3, HEADS // 4, HD).transpose(3, 0, 2, 4, 1, 5)
-    split = split.reshape(3, images, HEADS, -1, HD)
-    return split[0], split[1], split[2]
-
-
-def columns_of(parts, images):
-    stacked = jnp.stack(parts).reshape(3, images, 4, HEADS // 4, -1, HD)
-    flat = stacked.transpose(1, 4, 2, 0, 3, 5).reshape(-1, 4, 3 * HEADS * HD // 4)
-    return pad_to(flat, 2, QKV_WIDTH).reshape(-1, 4 * QKV_WIDTH)
-
-
-def own_forward(state, weights, modulate):
+GROUP_HEADS = HEADS // 4
+GROUP_WIDTH = HEADS * HD // 4
+
+
+def dot_nt(left, right):
+    return lax.dot_general(left, right, (((1,), (1,)), ((), ())), preferred_element_type=jnp.float32)
+
+
+def dot_tn(left, right):
+    return lax.dot_general(left, right, (((0,), (0,)), ((), ())), preferred_element_type=jnp.float32)
+
+
+def head_parts(packed_ref, head):
+    return [
+        packed_ref[:, index * GROUP_WIDTH + head * HD : index * GROUP_WIDTH + (head + 1) * HD]
+        for index in range(3)
+    ]
+
+
+def head_probs(queries, key_rows):
+    scores = dot_nt(queries, key_rows) * HD ** (-0.5)
+    powers = jnp.exp(scores - jnp.max(scores, axis=-1, keepdims=True))
+    return powers / jnp.sum(powers, axis=-1, keepdims=True)
+
+
+def pad_columns(values, own):
+    rows = values.shape[0]
+    gap = jnp.zeros((rows, PROJ_ROWS - own), values.dtype)
+    parts = []
+    for start in range(0, values.shape[1], own):
+        parts += [values[:, start : start + own], gap]
+    return jnp.concatenate(parts, axis=1)
+
+
+def attend_kernel(own, packed_ref, out_ref):
+    heads = [head_parts(packed_ref, head) for head in range(GROUP_HEADS)]
+    probs = [head_probs(queries, key_rows) for queries, key_rows, unused in heads]
+    mixed = [
+        product(prob.astype(jnp.bfloat16), parts[2]).astype(out_ref.dtype)
+        for prob, parts in zip(probs, heads)
+    ]
+    out_ref[...] = pad_columns(jnp.concatenate(mixed, axis=1), own)
+
+
+def attend_back_kernel(packed_ref, grad_ref, spread_ref, out_ref):
+    heads = [head_parts(packed_ref, head) for head in range(GROUP_HEADS)]
+    every = range(GROUP_HEADS)
+    grads = grad_ref[...]
+    grad_mixed = [dot_nt(grads, spread_ref[head]).astype(jnp.bfloat16) for head in every]
+    probs = [head_probs(queries, key_rows) for queries, key_rows, unused in heads]
+    grad_probs = [dot_nt(grad_mixed[head], heads[head][2]) for head in every]
+    grad_values = [dot_tn(probs[head].astype(jnp.bfloat16), grad_mixed[head]) for head in every]
+    grad_scores = []
+    for prob, grad_prob in zip(probs, grad_probs):
+        score = prob * (grad_prob - jnp.sum(grad_prob * prob, axis=-1, keepdims=True))
+        grad_scores.append((score * HD ** (-0.5)).astype(jnp.bfloat16))
+    grad_queries = [product(grad_scores[head], heads[head][1]) for head in every]
+    grad_keys = [dot_tn(grad_scores[head], heads[head][0]) for head in every]
+    for index, parts in enumerate((grad_queries, grad_keys, grad_values)):
+        for head, part in enumerate(parts):
+            start = index * GROUP_WIDTH + head * HD
+            out_ref[:, start : start + HD] = part.astype(out_ref.dtype)
+    rows, width = out_ref.shape
+    out_ref[:, 3 * GROUP_WIDTH :] = jnp.zeros((rows, width - 3 * GROUP_WIDTH), out_ref.dtype)
+
+
+def spread_heads(own):
+    columns = jnp.arange(GROUP_WIDTH // own * PROJ_ROWS)
+    source = columns // PROJ_ROWS * own + columns % PROJ_ROWS
+    source = jnp.where(columns % PROJ_ROWS < own, source, -1)
+    hot = jnp.arange(GROUP_WIDTH)[:, None] == source[None, :]
+    return hot.astype(jnp.bfloat16).reshape(GROUP_HEADS, HD, -1)
+
+
+def attend_call(kernel, images, inputs, constants, out_width, name):
+    rows = inputs[0].shape[0] // images
+
+    def block(width):
+        return pl.BlockSpec((rows, width), lambda image, group: (image, group))
+
+    return pl.pallas_call(
+        kernel,
+        grid=(images, 4),
+        out_shape=jax.ShapeDtypeStruct((images * rows, 4 * out_width), jnp.bfloat16),
+        in_specs=[block(one.shape[1] // 4) for one in inputs]
+        + [pl.BlockSpec(one.shape, lambda image, group: (0, 0, 0)) for one in constants],
+        out_specs=block(out_width),
+        compiler_params=PARAMS,
+        name=name,
+    )(*inputs, *constants)
+
+
+def attend(packed, own, images):
+    kernel = functools.partial(attend_kernel, own)
+    return attend_call(kernel, images, [packed], [], GROUP_WIDTH // own * PROJ_ROWS, "attend")
+
+
+def attend_back(packed, grads, own, images):
+    constants = [spread_heads(own)]
+    return attend_call(
+        attend_back_kernel, images, [packed, grads], constants, QKV_WIDTH, "attend_back"
+    )
+
+
+def own_forward(state, weights, modulate, own):
     qkv_weight, proj_weight, up_weight, down_weight = weights
     images, rows, columns = state.shape
     shift_one, scale_one, gate_one, shift_two, scale_two, gate_two = [
@@ -1184,18 +1469,7 @@
     full_one = (normed_one * (1.0 + scale_one) + shift_one).astype(jnp.bfloat16)
     flat_one = full_one.reshape(-1, columns)
     packed = product(flat_one, qkv_weight).astype(jnp.bfloat16)
-    queries, key_rows, value_rows = heads_of(packed, images)
-    scores = jnp.einsum(
-        "ghqe,ghke->ghqk", queries, key_rows, preferred_element_type=jnp.float32
-    )
-    probs = jax.nn.softmax(scores * HD ** (-0.5), axis=-1)
-    mixed = jnp.einsum(
-        "ghqk,ghke->ghqe",
-        probs.astype(jnp.bfloat16),
-        value_rows,
-        preferred_element_type=jnp.float32,
-    ).astype(jnp.bfloat16)
-    attended = mixed.transpose(0, 2, 1, 3).reshape(-1, columns)
+    attended = attend(packed, own, images)
     branch_one = product(attended, proj_weight).reshape(state.shape)
     middle = state + gate_one * branch_one
     normed_two, spread_two = normalize(middle)
@@ -1209,9 +1483,7 @@
         normed_one,
         spread_one,
         flat_one,
-        queries,
-        key_rows,
-        value_rows,
+        packed,
         attended,
         branch_one,
         normed_two,
@@ -1224,14 +1496,12 @@
     return (result, saved)
 
 
-def own_backward(grad_out, saved, weights, modulate):
+def own_backward(grad_out, saved, weights, modulate, own):
     (
         normed_one,
         spread_one,
         flat_one,
-        queries,
-        key_rows,
-        value_rows,
+        packed,
         attended,
         branch_one,
         normed_two,
@@ -1264,31 +1534,7 @@
     back_one = (gate_one * grad_middle).astype(jnp.bfloat16).reshape(-1, columns)
     grad_proj = product(attended.T, back_one).astype(jnp.bfloat16)
     grad_attended = product(back_one, proj_weight.T).astype(jnp.bfloat16)
-    grad_mixed = grad_attended.reshape(images, rows, HEADS, HD).transpose(0, 2, 1, 3)
-    scores = jnp.einsum(
-        "ghqe,ghke->ghqk", queries, key_rows, preferred_element_type=jnp.float32
-    )
-    probs = jax.nn.softmax(scores * HD ** (-0.5), axis=-1)
-    grad_probs = jnp.einsum(
-        "ghqe,ghke->ghqk", grad_mixed, value_rows, preferred_element_type=jnp.float32
-    )
-    grad_values = jnp.einsum(
-        "ghqk,ghqe->ghke",
-        probs.astype(jnp.bfloat16),
-        grad_mixed,
-        preferred_element_type=jnp.float32,
-    )
-    grad_scores = (
-        probs * (grad_probs - jnp.sum(grad_probs * probs, axis=-1, keepdims=True)) * HD ** (-0.5)
-    ).astype(jnp.bfloat16)
-    grad_queries = jnp.einsum(
-        "ghqk,ghke->ghqe", grad_scores, key_rows, preferred_element_type=jnp.float32
-    )
-    grad_keys = jnp.einsum(
-        "ghqk,ghqe->ghke", grad_scores, queries, preferred_element_type=jnp.float32
-    )
-    parts = [part.astype(jnp.bfloat16) for part in (grad_queries, grad_keys, grad_values)]
-    grad_packed = columns_of(parts, images)
+    grad_packed = attend_back(packed, grad_attended, own, images)
     grad_qkv = product(flat_one.T, grad_packed).astype(jnp.bfloat16)
     grad_hidden_one = product(grad_packed, qkv_weight.T)
     grad_hidden_one = grad_hidden_one.reshape(grad_out.shape)
@@ -1372,46 +1618,54 @@
     own_tiles = lax.dynamic_slice(owner_tiles, (my_rank * owned,), (owned,))
     dest, slot = tile_place(own_tiles, ranks)
     rank, counts = rank_within(dest, ranks)
-    slots, tags = tiles_to_slots(big_copy[0], dest, slot, rank, counts, rounds)
-    slices = slot_matrices(slots.astype(jnp.bfloat16), ranks)
-    plan = layer_plan(ranks) * 2
-    wholes = gather_whole(
-        plan, pad_slices(slices[0]) + pad_slices(slices[1]), 16, 1, "gather_weights"
-    )
-    weights = [whole_weights(wholes[:4], ranks), whole_weights(wholes[4:], ranks)]
-
     rest_own = rest_copy.reshape(own_columns, REST_ROWS)
     edges = [0, PD, PD + FREQ, PD + FREQ + D, PD + FREQ + D + CLASSES, REST_ROWS]
     win_t, one_t, two_t, table_t, tail_t = [
         rest_own[:, edges[i] : edges[i + 1]] for i in range(5)
     ]
     ends_size = own_columns * (2 * PD + 1)
+    one_size = own_columns * FREQ
+    whole_numbers = jnp.concatenate([timestep[:, 0], label[:, 0]])
     told = jnp.concatenate(
         [
-            jnp.concatenate([win_t, tail_t], axis=1).astype(jnp.float32).reshape(-1),
-            timestep[:, 0].astype(jnp.float32),
-            label[:, 0].astype(jnp.float32),
+            jnp.concatenate([win_t, tail_t], axis=1).reshape(-1),
+            one_t.reshape(-1),
+            (whole_numbers // 32).astype(jnp.bfloat16),
+            (whole_numbers % 32).astype(jnp.bfloat16),
         ]
     )
-    told = pad_to(told, 0, 1280).reshape(-1, 128)
-    told = push_all(told, world, 6, "push_inputs").reshape(world, -1)
-    facts = told[:, ends_size : ends_size + 2 * micro].astype(jnp.int32)
+    told = pad_to(told, 0, -(-told.shape[0] // 2048) * 2048).reshape(-1, 128)
+    brought = []
+
+    def carry_first(buf, new_tags):
+        arrays = [
+            [told],
+            [target.reshape(-1, 128)],
+            [new_tags.reshape(ranks, -1, 128)],
+            [buf.reshape(ranks, -1, 128)],
+        ]
+        kinds = ("push", "share", "swap", "swap")
+        got = travel([(kind, (None,), 0) for kind in kinds], arrays, 6, "exchange_inputs")
+        brought.extend(got)
+        return got[3][0].reshape(buf.shape), got[2][0].reshape(new_tags.shape)
+
+    slots, tags = tiles_to_slots(big_copy[0], dest, slot, rank, counts, rounds, carry_first)
+    told = brought[0][0].reshape(world, -1)
+    goals = brought[1][0].reshape(ranks, micro, SEQ, PD)
+    facts = told[:, ends_size + one_size :][:, : 4 * micro].astype(jnp.int32)
+    facts = facts[:, : 2 * micro] * 32 + facts[:, 2 * micro :]
     facts = facts.reshape(ranks, groups, 2 * micro).transpose(1, 0, 2).reshape(world, -1)
     stamps = facts[:, :micro].reshape(-1)
     tags_all = facts[:, micro:].reshape(-1)
-    ends = told[:, :ends_size].reshape(columns, -1).astype(jnp.bfloat16)
+    ends = told[:, :ends_size].reshape(columns, -1)
     embed_weight = ends[:, :PD].T
     mask_token = ends[:, PD].astype(jnp.float32)
     head_weight = ends[:, PD + 1 :]
     count_all = micro * world
     features = jax.vmap(time_features)(stamps).astype(jnp.bfloat16)
     pre_time = contract(features, one_t, 1, 1)
-    hidden_own = jax.nn.silu(pre_time).astype(jnp.bfloat16)
-    hidden_size = count_all * own_columns
-    hidden_all = pad_to(hidden_own.reshape(-1), 0, 4096).reshape(-1, 128)
-    hidden_all = push_all(hidden_all, world, 7, "push_hidden").reshape(world, -1)
-    hidden_all = hidden_all[:, :hidden_size].reshape(world, count_all, own_columns)
-    hidden_all = hidden_all.transpose(1, 0, 2).reshape(count_all, columns)
+    one_whole = told[:, ends_size : ends_size + one_size].reshape(columns, FREQ)
+    hidden_all = jax.nn.silu(contract(features, one_whole, 1, 1)).astype(jnp.bfloat16)
     picks = (tags_all[:, None] == jnp.arange(CLASSES, dtype=jnp.int32)[None, :]).astype(
         jnp.bfloat16
     )
@@ -1422,14 +1676,21 @@
     mod_entry = (True, 32, columns)
     mods = product(signal_own, ada_own).reshape(world, mod_rows, columns)
     mods = pad_to(mods, 1, mod_entry[1]).reshape(whole_shape(mod_entry))
-    mods = sum_slices((mod_entry,), [mods], 16, 3, "sum_mods")[0]
-    mods = mods[:mod_rows].reshape(micro, 14, columns)
+    plan = layer_plan(ranks) * 2
+    wholes, mods = travel(
+        (("gather", plan, 16), ("sum", (mod_entry,), 16)),
+        [spread_slots(slots, ranks), [mods]],
+        1,
+        "gather_weights",
+    )
+    weights = [whole_weights(wholes[:4], ranks), whole_weights(wholes[4:], ranks)]
+    own = GROUP_WIDTH // ranks
+    mods = mods[0][:mod_rows].reshape(micro, 14, columns)
     mod_enc = mods[:, :6]
     mod_dec = mods[:, 6:12]
     final_shift = mods[:, 12:13]
     final_scale = mods[:, 13:]
 
-    goals = lax.all_gather(target[:, 0], "dp", axis=0, tiled=False)
     goal = jnp.stack([goals[owner[b, 0], b] for b in range(micro)])
     positions = position_table(columns)
     images = ranks * groups
@@ -1443,14 +1704,14 @@
     kept = jnp.sum(hits, axis=2)[:, :, None]
     embedded = product(patches.reshape(-1, PD), embed_weight).reshape(micro, KEEP, columns)
     embedded = embedded + jnp.take(positions, place, axis=0)
-    enc_out, enc_saved = own_forward(embedded, weights[0], mod_enc)
+    enc_out, enc_saved = own_forward(embedded, weights[0], mod_enc, own)
     sent = enc_out.astype(jnp.bfloat16)
     dec_in = (
         jnp.einsum("bpr,brd->bpd", hits_low, sent, preferred_element_type=jnp.float32)
         + (1.0 - kept) * mask_token[None, None, :]
         + positions[None]
     )
-    dec_out, dec_saved = own_forward(dec_in, weights[1], mod_dec)
+    dec_out, dec_saved = own_forward(dec_in, weights[1], mod_dec, own)
     normed_final, spread_final = normalize(dec_out)
     head_in = (normed_final * (1.0 + final_scale) + final_shift).astype(jnp.bfloat16)
     flat_head = head_in.reshape(-1, columns)
@@ -1467,7 +1728,7 @@
     )
     grad_dec_out = normalize_back(grad_head_in * (1.0 + final_scale), normed_final, spread_final)
     grad_dec_in, grad_mod_dec, dec_grads = own_backward(
-        grad_dec_out, dec_saved, weights[1], mod_dec
+        grad_dec_out, dec_saved, weights[1], mod_dec, own
     )
     grad_mask = jnp.sum((1.0 - kept) * grad_dec_in, axis=(0, 1))[None, :]
     grad_sent = jnp.einsum(
@@ -1477,12 +1738,8 @@
         preferred_element_type=jnp.float32,
     )
     grad_embedded, grad_mod_enc, enc_grads = own_backward(
-        grad_sent, enc_saved, weights[0], mod_enc
-    )
-    sums = sum_slices(
-        plan, whole_parts(enc_grads, ranks) + whole_parts(dec_grads, ranks), 16, 2, "sum_gradients"
-    )
-    sums = matrices_slots([trim_slices(sums[:4], ranks), trim_slices(sums[4:], ranks)])
+        grad_sent, enc_saved, weights[0], mod_enc, own
+    )
     grad_embed = contract_wide(
         patches.reshape(-1, PD), grad_embedded.reshape(-1, columns), 0, 0
     )
@@ -1490,7 +1747,15 @@
     vectors = jnp.concatenate([grad_mod_enc, grad_mod_dec, grad_final], axis=1)
     vectors = vectors.astype(jnp.bfloat16).reshape(mod_rows, columns)
     vectors = pad_to(vectors, 0, mod_entry[1])
-    vectors = gather_whole((mod_entry,), [vectors], 16, 4, "gather_vectors")[0]
+    sums, vectors = travel(
+        (("sum", plan, 16), ("gather", (mod_entry,), 16)),
+        [whole_parts(enc_grads, ranks) + whole_parts(dec_grads, ranks), [vectors]],
+        2,
+        "sum_gradients",
+    )
+    sums, big_squares = collect_slots(sums, owned + 16, ranks)
+    vectors = vectors[0]
+    back = gather_rows(sums, tags, jnp.bfloat16)
     vectors = vectors.reshape(world, mod_entry[1], columns)[:, :mod_rows].reshape(count_all, -1)
     owned_ada = contract(signal_own, vectors, 0, 0).reshape(-1)
     grad_signal = contract(vectors, ada_own, 1, 1)
@@ -1504,9 +1769,13 @@
     shared = shared.reshape(shared_rows, ranks, groups, own_columns).transpose(2, 1, 0, 3)
     shared = pad_to(shared.reshape(world, -1), 1, 4096)
     shared_entry = (True, 32, 128)
-    shared = sum_slices(
-        (shared_entry,), [shared.reshape(whole_shape(shared_entry))], 32, 5, "sum_shared"
-    )[0]
+    shared, back = travel(
+        (("sum", (shared_entry,), 32), ("swap", (None,), 0)),
+        [[shared.reshape(whole_shape(shared_entry))], [back.reshape(ranks, -1, 128)]],
+        5,
+        "sum_shared",
+    )
+    shared = shared[0]
     shared = shared.reshape(-1)[: shared_rows * own_columns].reshape(shared_rows, own_columns)
     grad_pre = silu_back(pre_time, shared[:count_all])
     grad_one_t = contract_wide(grad_pre, features, 0, 0)
@@ -1515,10 +1784,11 @@
         [ends_t[:, :PD], grad_one_t, grad_two_t, grad_table_t, ends_t[:, PD:]], axis=1
     ).reshape(-1)
 
-    squares = jnp.sum(sums * sums) + jnp.sum(owned_ada * owned_ada) + jnp.sum(owned_rest * owned_rest)
+    squares = jnp.sum(big_squares) + jnp.sum(owned_ada * owned_ada) + jnp.sum(owned_rest * owned_rest)
     totals = jnp.broadcast_to(pad_to(jnp.stack([loss_sum, squares]), 0, 128), (8, 128))
     totals = jnp.sum(push_all(totals, world, 8, "push_totals")[:, 0, :2], axis=0)
-    owned_big = slots_to_tiles(sums, tags, dest, slot, rank, counts, rounds)
+    back = back[0].reshape(-1, 128)
+    owned_big = slots_to_tiles(sums, back, dest, slot, rank, counts, rounds)
     grad_norm = jnp.sqrt(totals[1])
     clip = jnp.minimum(1.0, MAX_NORM / (grad_norm + 1e-06))
     count = step[0].astype(jnp.float32)

time: 1450 us -> 1210 us (0.83)
  local copies, waits for them, and re-layouts: 214 us -> 63.4 us
  Pallas kernels: 799 us -> 858 us
  matrix products: 260 us -> 202 us
  waiting for transfers between devices: 42.7 us -> 0 us
  blocking collectives: 31 us -> 0 us
  starting transfers between devices: 18 us -> 0 us
    pallas_call x7 -> x12, Pallas kernels: 685 us -> 821 us  [the longest x4 735 us: travel(): pl.pallas_call(functools.partial(travel_kernel, jobs, [len(mine) for mine...]
    pallas_call x3 -> x1, Pallas kernels: 81.8 us -> 9.61 us  [push_all(): pl.pallas_call(functools.partial(push_kernel, world), out_shape=jax.Shape...]
    reshape x35 -> x10, local copies, waits for them, and re-layouts: 63.2 us -> 5.15 us  [the longest x1 1.91 us: local(): goals = brought[1][0].reshape(ranks, micro, SEQ, PD)]
    dot_general x10 -> x0, matrix products: 54.6 us -> none  [the longest x2 17.7 us: own_backward(): jnp.einsum('ghqk,ghke->ghqe', grad_scores, key_rows, preferred_element_ty...]
    all_to_all x3 -> x0, waiting for transfers between devices: 42.7 us -> none  [swap_ranks(): return lax.all_to_all(split, 'dp', 0, 0).reshape(buf.shape)]
    all_gather x1 -> x0, blocking collectives: 31 us -> none  [local(): goals = lax.all_gather(target[:, 0], 'dp', axis=0, tiled=False)]
    unnamed x394 -> x350, local copies, waits for them, and re-layouts: 41.9 us -> 16.5 us
    concatenate x3 -> x1, local copies, waits for them, and re-layouts: 23.2 us -> 0.1 us  [local(): jnp.concatenate([jnp.concatenate([win_t, tail_t], axis=1).reshape(-1), on...]
  transfers between devices with their start and end apart: 3 -> 0, of which waited for: 1 -> 0; matrix products, arithmetic and copies ran while one was open for 4% -> 0% of each run, Pallas kernels for 7% -> 0%
where the time goes in v3:
time: 1210 us; the launch traced here: 1200 us
  Pallas kernels  858 us (71%)
  matrix products  202 us (17%)
  local copies, waits for them, and re-layouts  63.4 us (5%)
  other arithmetic  59.4 us (5%)
  between operations  13.3 us (1%)
    pallas_call x4, Pallas kernels, travel(): pl.pallas_call(functools.partial(travel_kernel, jobs, [len(mine) for mine...  735 us
    dot_general x28, matrix products, product(): return jnp.dot(left, right, preferred_element_type=jnp.float32)  186 us
    pallas_call x4, Pallas kernels, attend_call(): pl.pallas_call(kernel, grid=(images, 4), out_shape=jax.ShapeDtypeStruct((...  48.2 us
    pallas_call x2, Pallas kernels, gather_rows(): pl.pallas_call(functools.partial(gather_kernel, total), out_shape=jax.Sha...  27.1 us

profile of v3, /device:TPU:0, one launch (start us, length us, event | category | flops | bytes accessed | tf_op | source)
XLA Modules:
  0.0 1205.0 jit_solution(2517108725000235938)
XLA Ops:
  33.9 13.0 %pack_rows.7 = bf16[9216,128]{1,0:T(8,128)(2,1)S(1)} custom-call(s32[7776]{0:T(1024)S(1)} %get-tuple-element.565.pos_ref, bf16[7776,128]{1,0:T(8,128)(2,1)S(1)} %bitcast.307), custom_call_target="tpu_custom_call" | custom-call | tf_op jit(solution)/shard_map/pack_rows/pallas_call | solution.py:602
  47.0 65.1 %exchange_inputs.1 = (bf16[32,96,128]{2,1,0:T(8,128)(2,1)S(1)}, f32[8,64,128]{2,1,0:T(8,128)S(1)}, s32[8,9,128]{2,1,0:T(8,128)S(1)}, bf16[8,1152,128]{2,1,0:T(8,128)(2,1)S(1)}) custom-call(bf16[96,128]{1,0:T(8,128)(2,1)S(1)} %pad_bitcast_fusion.1.refs_0_, f32[64,128]{1,0:T(8,128)S(1)} %reshape.915.refs_1_, s32[8,9,128]{2,1,0:T(8,128)S(1)} %compare_select_fusion.5.refs_2_, ...), custom_call_target="tpu_custom_call" | custom-call | tf_op jit(solution)/shard_map/exchange_inputs/pallas_call | solution.py:1074
  115.2 16.1 %scatter_rows.7 = bf16[7792,128]{1,0:T(8,128)(2,1)} custom-call(s32[9216]{0:T(1024)S(1)} %reshape.921.tag_ref.index_ref, bf16[9216,128]{1,0:T(8,128)(2,1)S(1)} %bitcast.300), custom_call_target="tpu_custom_call" | custom-call | tf_op jit(solution)/shard_map/scatter_rows/pallas_call | solution.py:632
  131.3 8.7 while.28
  176.0 316.2 %gather_weights.1 = (bf16[4,2,144,3584]{3,2,1,0:T(8,128)(2,1)}, bf16[4,4,2,48,1152]{4,3,2,1,0:T(8,128)(2,1)S(1)}, bf16[4,2,144,4608]{3,2,1,0:T(8,128)(2,1)}, bf1...) custom-call(bf16[144,896]{1,0:T(8,128)(2,1)S(1)} %copy-done.21, ...), custom_call_target="tpu_custom_call" | custom-call | tf_op jit(solution)/shard_map/gather_weights/pallas_call | solution.py:1074
  499.3 5.9 convolution_convert_fusion.9.packed_ref
  505.2 8.4 attend.2
  516.9 10.9 multiply_convert_fusion.1
  533.6 8.9 convolution_convert_fusion.8.packed_ref
  542.6 13.3 %attend.3 = bf16[512,1536]{1,0:T(8,128)(2,1)S(1)} custom-call(bf16[512,3584]{1,0:T(8,128)(2,1)S(1)} %convolution_convert_fusion.8.packed_ref), custom_call_target="tpu_custom_call" | custom-call | tf_op jit(solution)/shard_map/attend/pallas_call | solution.py:1438
  560.5 14.8 %multiply_convert_fusion = (bf16[512,4608]{1,0:T(8,128)(2,1)S(1)}, f32[512,4608]{1,0:T(8,128)}) fusion(bf16[512,1152]{1,0:T(8,128)(2,1)S(1)} %bitcast.335, bf16[1152,4608]{1,0:T(8,128)(2,1)} %bitcast.394), kind=kOutput, calls=%fused_computation.91 | convolution fusion | flops 5457051648 | bytes 25952256 | tf_op jit(solution)/shard_map/dot_general | solution.py:41
  575.4 7.8 fusion.185
  594.4 16.9 %fusion.34 = bf16[512,4608]{1,0:T(8,128)(2,1)} fusion(f32[512,4608]{1,0:T(8,128)} %get-tuple-element.653, bf16[512,1152]{1,0:T(8,128)(2,1)S(1)} %bitcast.337, bf16[4608,1152]{1,0:T(8,128)(2,1)} %bitcast.396), kind=kOutput, calls=%fused_computation.90 | convolution fusion | flops 5483003904 | bytes 25952256 | tf_op jit(solution)/shard_map/dot_general | solution.py:41
  611.3 12.7 %multiply_reduce_fusion.4 = (bf16[2,1152]{1,0:T(2,128)(2,1)S(1)}, f32[2,256]{1,0:T(2,128)S(1)}, f32[2,256]{1,0:T(2,128)S(1)}, bf16[2,1152]{1,0:T(2,128)(2,1)S(1)}, f32[2,256,1152]{2,1,0:T(8,128)}) fusion(f32[2,256,1152]{2,1,0:T(8,128)S(1)} %copy-done.42, f32[2,256]{1,0:T(2,128)S(1)} %add_rsqrt_fusion.1, f32[2,256]{1,0:T(2,128)S(1)} %broadcast_multiply_fusion.10, ...), kind=kOutput, calls=%fused_computation.123 | convolution fusion | flops 5441121280 | bytes 20080640 | tf_op jit(solution)/shard_map/dot_general | solution.py:41
  631.4 17.9 %attend_back.2 = bf16[512,3584]{1,0:T(8,128)(2,1)S(1)} custom-call(bf16[512,3584]{1,0:T(8,128)(2,1)} %copy-done, bf16[512,1536]{1,0:T(8,128)(2,1)S(1)} %convolution_convert_fusion.10.grad_ref, bf16[4,72,384]{2,1,0:T(8,128)(2,1)S(1)} %copy-done.9), custom_call_target="tpu_custom_call" | custom-call | tf_op jit(solution)/shard_map/attend_back/pallas_call | solution.py:1438
  649.4 10.0 multiply_reduce_fusion.6
  669.0 8.8 fusion.41
  677.8 8.3 multiply_reduce_fusion.18
  689.7 8.6 attend_back.3
  698.4 6.1 multiply_reduce_fusion.16
  711.8 12.8 %convolution_convert_fusion = bf16[4608,1152]{1,0:T(8,128)(2,1)} fusion(bf16[512,4608]{1,0:T(8,128)(2,1)} %copy-done.149, bf16[512,1152]{1,0:T(8,128)(2,1)S(1)} %bitcast.338), kind=kOutput, calls=%fused_computation.76 | convolution fusion | flops 5441126400 | bytes 16515072 | tf_op jit(solution)/shard_map/dot_general | solution.py:41
  724.7 6.8 convolution_convert_fusion.4
  737.1 5.9 convolution_convert_fusion.2
  743.0 8.4 convolution_convert_fusion.1
  751.4 5.8 convolution_convert_fusion.3
  757.2 294.7 %sum_gradients.1 = (f32[144,896]{1,0:T(8,128)S(1)}, f32[48,1152]{1,0:T(8,128)S(1)}, f32[144,1152]{1,0:T(8,128)S(1)}, f32[144,1152]{1,0:T(8,128)S(1)}, f32[144,89...) custom-call(bf16[4,2,144,3584]{3,2,1,0:T(8,128)(2,1)} %bitcast.310, ...), custom_call_target="tpu_custom_call" | custom-call | tf_op jit(solution)/shard_map/sum_gradients/pallas_call | solution.py:1074
  1074.6 12.6 %gather_rows.14 = bf16[9216,128]{1,0:T(8,128)(2,1)S(1)} custom-call(s32[9216]{0:T(1024)S(1)} %copy-done.19, f32[7792,128]{1,0:T(8,128)} %get-tuple-element.895.x_ref), custom_call_target="tpu_custom_call" | custom-call | tf_op jit(solution)/shard_map/gather_rows/pallas_call | solution.py:648
  1087.3 59.3 %sum_shared.1 = (f32[32,128]{1,0:T(8,128)S(1)}, bf16[8,1152,128]{2,1,0:T(8,128)(2,1)S(1)}) custom-call(f32[4,4,2,32,128]{4,3,2,1,0:T(8,128)S(1)} %bitcast.301, bf16[8,1152,128]{2,1,0:T(8,128)(2,1)S(1)} %bitcast.292), custom_call_target="tpu_custom_call" | custom-call | tf_op jit(solution)/shard_map/sum_shared/pallas_call | solution.py:1074
  1149.6 9.6 push_totals.1
  1171.1 14.5 %gather_rows.15 = f32[7776,128]{1,0:T(8,128)} custom-call(s32[7776]{0:T(1024)S(1)} %copy-done.25, f32[9216,128]{1,0:T(8,128)S(1)} %bitcast_convert_fusion.1.x_ref), custom_call_target="tpu_custom_call" | custom-call | tf_op jit(solution)/shard_map/gather_rows/pallas_call | solution.py:648
  1185.9 8.6 fusion.181
  1195.9 7.7 fusion.183
  (531 shorter events, 166.8 us)
Async XLA Ops:
  0.6 18.6 %copy-start.103 = (s32[62208]{0:T(1024)S(1)}, s32[62208]{0:T(1024)}, u32[]{:S(2)}) copy-start(s32[62208]{0:T(1024)} %param.36) | copy-start | bytes 746500
  0.7 21.4 %copy-start.126 = (f32[2,1,256,16]{2,3,1,0:T(8,128)S(1)}, f32[2,1,256,16]{2,3,1,0:T(8,128)}, u32[]{:S(2)}) copy-start(f32[2,1,256,16]{2,3,1,0:T(8,128)} %param.42) | copy-start | bytes 98308
  0.7 21.6 %copy-start.93 = (bf16[580608]{0:T(1024)(128)(2,1)S(1)}, bf16[580608]{0:T(1024)(128)(2,1)}, u32[]{:S(2)}) copy-start(bf16[580608]{0:T(1024)(128)(2,1)} %param.28) | copy-start | bytes 3483652
  18.0 135.9 %copy-start.94 = (bf16[36,2442]{1,0:T(8,128)(2,1)}, bf16[36,2442]{1,0:T(8,128)(2,1)S(1)}, u32[]{:S(2)}) copy-start(bf16[36,2442]{1,0:T(8,128)(2,1)S(1)} %reshape.911) | copy-start | bytes 527476
  47.0 67.2 %copy-start.146 = (f32[128]{0:T(128)S(1)}, f32[128]{0:T(128)}, u32[]{:S(2)}) copy-start(f32[128]{0:T(128)} %multiply_exponential_fusion) | copy-start | bytes 1540
  113.6 17.8 %copy-start.150 = (s32[8]{0:T(128)S(1)}, s32[8]{0:T(128)}, u32[]{:S(2)}) copy-start(s32[8]{0:T(128)} %convert_element_type.273) | copy-start | bytes 100
  114.0 39.9 %copy-start.144 = (s32[64]{0:T(128)}, s32[64]{0:T(128)S(1)}, u32[]{:S(2)}) copy-start(s32[64]{0:T(128)S(1)} %eq.267) | copy-start | bytes 772
  114.4 38.8 %copy-start.133 = (bf16[64,128]{1,0:T(8,128)(2,1)}, bf16[64,128]{1,0:T(8,128)(2,1)S(1)}, u32[]{:S(2)}) copy-start(bf16[64,128]{1,0:T(8,128)(2,1)S(1)} %get-tuple-element.639) | copy-start | bytes 49156
  114.4 38.8 %copy-start.135 = (bf16[64,128]{1,0:T(8,128)(2,1)}, bf16[64,128]{1,0:T(8,128)(2,1)S(1)}, u32[]{:S(2)}) copy-start(bf16[64,128]{1,0:T(8,128)(2,1)S(1)} %get-tuple-element.640) | copy-start | bytes 49156
  115.2 16.1 %copy-start.18 = (s32[9216]{0:T(1024)}, s32[9216]{0:T(1024)S(1)}, u32[]{:S(2)}) copy-start(s32[9216]{0:T(1024)S(1)} %reshape.921.tag_ref.index_ref) | copy-start | bytes 110596
  492.9 20.7 %copy-start.7 = (bf16[4,4,2,48,1152]{4,3,2,1,0:T(8,128)(2,1)}, bf16[4,4,2,48,1152]{4,3,2,1,0:T(8,128)(2,1)S(1)}, u32[]{:S(2)}) copy-start(bf16[4,4,2,48,1152]{4,3,2,1,0:T(8,128)(2,1)S(1)} %get-tuple-element.460) | copy-start | bytes 10616836
  496.6 87.0 %copy-start.112 = (f32[2,1,1152]{2,0,1:T(2,128)}, f32[2,1,1152]{2,0,1:T(2,128)S(1)}, u32[]{:S(2)}) copy-start(f32[2,1,1152]{2,0,1:T(2,128)S(1)} %copy.223) | copy-start | bytes 27652
  496.6 63.3 %copy-start.115 = (f32[2,1,1152]{2,0,1:T(2,128)}, f32[2,1,1152]{2,0,1:T(2,128)S(1)}, u32[]{:S(2)}) copy-start(f32[2,1,1152]{2,0,1:T(2,128)S(1)} %copy.226) | copy-start | bytes 27652
  496.7 78.6 %copy-start.123 = (f32[2,1,1152]{2,0,1:T(2,128)}, f32[2,1,1152]{2,0,1:T(2,128)S(1)}, u32[]{:S(2)}) copy-start(f32[2,1,1152]{2,0,1:T(2,128)S(1)} %copy.227) | copy-start | bytes 27652
  496.7 36.4 %copy-start.113 = (f32[2,1,1152]{2,0,1:T(2,128)}, f32[2,1,1152]{2,0,1:T(2,128)S(1)}, u32[]{:S(2)}) copy-start(f32[2,1,1152]{2,0,1:T(2,128)S(1)} %copy.229) | copy-start | bytes 27652
  496.7 59.1 %copy-start.121 = (f32[2,1,1152]{2,0,1:T(2,128)}, f32[2,1,1152]{2,0,1:T(2,128)S(1)}, u32[]{:S(2)}) copy-start(f32[2,1,1152]{2,0,1:T(2,128)S(1)} %copy.230) | copy-start | bytes 27652
  496.8 19.7 %copy-start.106 = (f32[2,1,1152]{2,0,1:T(2,128)}, f32[2,1,1152]{2,0,1:T(2,128)S(1)}, u32[]{:S(2)}) copy-start(f32[2,1,1152]{2,0,1:T(2,128)S(1)} %copy.232) | copy-start | bytes 27652
  496.8 34.3 %copy-start.110 = (f32[2,1,1152]{2,0,1:T(2,128)}, f32[2,1,1152]{2,0,1:T(2,128)S(1)}, u32[]{:S(2)}) copy-start(f32[2,1,1152]{2,0,1:T(2,128)S(1)} %copy.233) | copy-start | bytes 27652
  498.4 15.2 %copy-start.104 = (f32[2,1,1152]{2,0,1:T(2,128)}, f32[2,1,1152]{2,0,1:T(2,128)S(1)}, u32[]{:S(2)}) copy-start(f32[2,1,1152]{2,0,1:T(2,128)S(1)} %copy.236) | copy-start | bytes 27652
  532.7 23.2 %copy-start.35 = (f32[2,256,1152]{2,1,0:T(8,128)}, f32[2,256,1152]{2,1,0:T(8,128)S(1)}, u32[]{:S(2)}) copy-start(f32[2,256,1152]{2,1,0:T(8,128)S(1)} %get-tuple-element.650) | copy-start | bytes 7077892
  559.6 15.7 %copy-start.41 = (f32[2,256,1152]{2,1,0:T(8,128)}, f32[2,256,1152]{2,1,0:T(8,128)S(1)}, u32[]{:S(2)}) copy-start(f32[2,256,1152]{2,1,0:T(8,128)S(1)} %get-tuple-element.577) | copy-start | bytes 7077892
  560.0 15.3 %slice-start.3 = ((s8[10616832]{0:T(1024)(128)(4,1)}), s8[4194304]{0:T(1024)(128)(4,1)S(1)}, s32[]{:S(2)}) async-start(s8[10616832]{0:T(1024)(128)(4,1)} %bitcast.397), calls=%async_computation.7 | async-start | bytes 8388608
  594.4 16.9 %copy-start.90 = (bf16[2,256,1152]{2,1,0:T(8,128)(2,1)}, bf16[2,256,1152]{2,1,0:T(8,128)(2,1)S(1)}, u32[]{:S(2)}) copy-start(bf16[2,256,1152]{2,1,0:T(8,128)(2,1)S(1)} %multiply_convert_fusion.3) | copy-start | bytes 3538948
  594.4 16.9 %copy-start.42 = (f32[2,256,1152]{2,1,0:T(8,128)S(1)}, f32[2,256,1152]{2,1,0:T(8,128)}, u32[]{:S(2)}) copy-start(f32[2,256,1152]{2,1,0:T(8,128)} %copy-done.41) | copy-start | bytes 7077892
  594.4 16.9 %copy-start.116 = (f32[2,1,1152]{2,0,1:T(2,128)S(1)}, f32[2,1,1152]{2,0,1:T(2,128)}, u32[]{:S(2)}) copy-start(f32[2,1,1152]{2,0,1:T(2,128)} %copy-done.115) | copy-start | bytes 27652
  631.4 18.0 %copy-start.36 = (f32[2,256,1152]{2,1,0:T(8,128)S(1)}, f32[2,256,1152]{2,1,0:T(8,128)}, u32[]{:S(2)}) copy-start(f32[2,256,1152]{2,1,0:T(8,128)} %copy-done.35) | copy-start | bytes 7077892
  631.4 18.0 %copy-start.114 = (f32[2,1,1152]{2,0,1:T(2,128)S(1)}, f32[2,1,1152]{2,0,1:T(2,128)}, u32[]{:S(2)}) copy-start(f32[2,1,1152]{2,0,1:T(2,128)} %copy-done.113) | copy-start | bytes 27652
  631.4 18.0 %copy-start.128 = (f32[2,256]{1,0:T(2,128)S(1)}, f32[2,256]{1,0:T(2,128)}, u32[]{:S(2)}) copy-start(f32[2,256]{1,0:T(2,128)} %copy-done.127) | copy-start | bytes 6148
  1087.3 59.8 %copy-start.134 = (bf16[64,128]{1,0:T(8,128)(2,1)S(1)}, bf16[64,128]{1,0:T(8,128)(2,1)}, u32[]{:S(2)}) copy-start(bf16[64,128]{1,0:T(8,128)(2,1)} %copy-done.133) | copy-start | bytes 49156
  1087.3 59.8 %copy-start.136 = (bf16[64,128]{1,0:T(8,128)(2,1)S(1)}, bf16[64,128]{1,0:T(8,128)(2,1)}, u32[]{:S(2)}) copy-start(bf16[64,128]{1,0:T(8,128)(2,1)} %copy-done.135) | copy-start | bytes 49156
  1087.3 59.8 %copy-start.152 = (f32[64,36]{0,1:T(8,128)S(1)}, f32[64,36]{0,1:T(8,128)}, u32[]{:S(2)}) copy-start(f32[64,36]{0,1:T(8,128)} %fusion.143) | copy-start | bytes 27652
  1087.3 60.0 %copy-start.95 = (f32[36,1152]{1,0:T(8,128)S(1)}, f32[36,1152]{1,0:T(8,128)}, u32[]{:S(2)}) copy-start(f32[36,1152]{1,0:T(8,128)} %fusion.176) | copy-start | bytes 497668
  (127 other events, 841.1 us)

commit v4 on v3

--- a/solution.py
+++ b/solution.py
@@ -3,6 +3,7 @@
 
 import jax
 import jax.numpy as jnp
+import numpy as np
 from jax import lax
 from jax.experimental import pallas as pl
 from jax.experimental.pallas import tpu as pltpu
@@ -63,6 +64,18 @@
         return jnp.concatenate([jnp.sin(angles), jnp.cos(angles)], axis=1)
 
     return jnp.concatenate([half_table(places % GRID), half_table(places // GRID)], axis=1)
+
+
+def position_constant(columns):
+    quarter = columns // 4
+    omegas = np.float32(1.0) / np.float32(10000.0) ** (np.arange(quarter, dtype=np.float32) / np.float32(quarter))
+    places = np.arange(GRID * GRID)
+
+    def half_table(coords):
+        angles = (coords.astype(np.float32)[:, None] * omegas[None, :]).astype(np.float64)
+        return np.concatenate([np.sin(angles), np.cos(angles)], axis=1).astype(np.float32)
+
+    return np.concatenate([half_table(places % GRID), half_table(places // GRID)], axis=1)
 
 
 def time_features(stamp):
@@ -728,7 +741,7 @@
     )
 
 
-def gather_job(plan, chunk, slices, wholes, scratch):
+def gather_job(plan, chunk, lag, slices, wholes, scratch):
     count = len(plan)
     held, other_held, own_sem, out_sem, z_send, z_recv, a_send, a_recv, b_send, b_recv, c_send, c_recv = scratch
     z, x, y, core = coordinates()
@@ -788,14 +801,14 @@
                         copy.start()
 
     def step(t):
-        go(t - 1 - 4 * LAG, (4, 5), ())
-        go(t - 4 * LAG, (3,), (5,))
-        go(t - 3 * LAG, (2,), (3, 4))
-        go(t - 2 * LAG, (1,), (2,))
-        go(t - LAG, (0,), (1,))
+        go(t - 1 - 4 * lag, (4, 5), ())
+        go(t - 4 * lag, (3,), (5,))
+        go(t - 3 * lag, (2,), (3, 4))
+        go(t - 2 * lag, (1,), (2,))
+        go(t - lag, (0,), (1,))
         go(t, (), (0,))
 
-    return step, total + 1 + 4 * LAG
+    return step, total + 1 + 4 * lag
 
 
 def whole_shape(entry):
@@ -811,7 +824,7 @@
     return [held, held, each, dma((2, 4, GATHER_SLOTS)), three, three] + [each] * 6
 
 
-def sum_job(plan, chunk, parts, outs, scratch):
+def sum_job(plan, chunk, lag, parts, outs, scratch):
     count = len(plan)
     own, from_core, from_first, from_second, from_z, half, quarter, eighth = scratch[:8]
     own_sem, core_send, core_recv, a_send, a_recv, b_send, b_recv, z_send, z_recv = scratch[8:]
@@ -926,13 +939,13 @@
                     copy.start()
 
     def step(t):
-        finish(t - 1 - 3 * LAG)
-        go(t - 1 - 2 * LAG, 2)
-        go(t - 1 - LAG, 1)
+        finish(t - 1 - 3 * lag)
+        go(t - 1 - 2 * lag, 2)
+        go(t - 1 - lag, 1)
         go(t - 1, 0)
         begin(t)
 
-    return step, total + 1 + 3 * LAG
+    return step, total + 1 + 3 * lag
 
 
 def sum_scratch(plan, chunk, kind):
@@ -1005,11 +1018,11 @@
     scratch = [take(number) for number in scratch_counts]
     steps = []
     direct = []
-    for (kind, plan, chunk), source, target, mine in zip(jobs, sources, targets, scratch):
+    for (kind, plan, chunk, lag), source, target, mine in zip(jobs, sources, targets, scratch):
         if kind == "gather":
-            steps.append(gather_job(plan, chunk, source, target, mine))
+            steps.append(gather_job(plan, chunk, lag, source, target, mine))
         elif kind == "sum":
-            steps.append(sum_job(plan, chunk, source, target, mine))
+            steps.append(sum_job(plan, chunk, lag, source, target, mine))
         else:
             direct.append(direct_job(kind, source, target, mine))
     if direct:
@@ -1054,7 +1067,7 @@
     scratch = []
     shapes = []
     specs = []
-    for (kind, plan, chunk), mine in zip(jobs, arrays):
+    for (kind, plan, chunk, unused_lag), mine in zip(jobs, arrays):
         dtype = mine[0].dtype
         if kind == "gather":
             scratch.append(gather_scratch(plan, chunk, dtype))
@@ -1074,7 +1087,9 @@
     outs = pl.pallas_call(
         functools.partial(travel_kernel, jobs, [len(mine) for mine in scratch]),
         out_shape=shapes,
-        in_specs=[ANY] * len(flat),
+        in_specs=[
+            VMEM if job[0] == "gather" else ANY for job, mine in zip(jobs, arrays) for unused in mine
+        ],
         out_specs=specs,
         scratch_shapes=[one for mine in scratch for one in mine],
         compiler_params=pltpu.CompilerParams(
@@ -1083,7 +1098,7 @@
         name=name,
     )(*flat)
     results = []
-    for unused_kind, plan, unused_chunk in jobs:
+    for unused_kind, plan, unused_chunk, unused_lag in jobs:
         results.append(outs[: len(plan)])
         outs = outs[len(plan) :]
     return results
@@ -1459,11 +1474,20 @@
     )
 
 
+def gelu_and_slope(values):
+    factor = math.sqrt(2.0 / math.pi)
+    square = values * values
+    bend = jnp.tanh(factor * values * (1.0 + 0.044715 * square))
+    half = 0.5 * (1.0 + bend)
+    slope = half + 0.5 * values * (1.0 - bend * bend) * factor * (1.0 + 3.0 * 0.044715 * square)
+    return values * half, slope
+
+
 def own_forward(state, weights, modulate, own):
     qkv_weight, proj_weight, up_weight, down_weight = weights
     images, rows, columns = state.shape
     shift_one, scale_one, gate_one, shift_two, scale_two, gate_two = [
-        modulate[:, index, None, :] for index in range(6)
+        modulate[index] for index in range(6)
     ]
     normed_one, spread_one = normalize(state)
     full_one = (normed_one * (1.0 + scale_one) + shift_one).astype(jnp.bfloat16)
@@ -1475,8 +1499,8 @@
     normed_two, spread_two = normalize(middle)
     full_two = (normed_two * (1.0 + scale_two) + shift_two).astype(jnp.bfloat16)
     flat_two = full_two.reshape(-1, columns)
-    hidden_pre = product(flat_two, up_weight)
-    activated = jax.nn.gelu(hidden_pre, approximate=True).astype(jnp.bfloat16)
+    activated, slope = gelu_and_slope(product(flat_two, up_weight))
+    activated = activated.astype(jnp.bfloat16)
     branch_two = product(activated, down_weight).reshape(state.shape)
     result = middle + gate_two * branch_two
     saved = (
@@ -1489,7 +1513,7 @@
         normed_two,
         spread_two,
         flat_two,
-        hidden_pre,
+        slope,
         activated,
         branch_two,
     )
@@ -1507,21 +1531,19 @@
         normed_two,
         spread_two,
         flat_two,
-        hidden_pre,
+        slope,
         activated,
         branch_two,
     ) = saved
     qkv_weight, proj_weight, up_weight, down_weight = weights
     images, rows, columns = grad_out.shape
     shift_one, scale_one, gate_one, shift_two, scale_two, gate_two = [
-        modulate[:, index, None, :] for index in range(6)
+        modulate[index] for index in range(6)
     ]
     grad_gate_two = jnp.sum(grad_out * branch_two, axis=1)
     back_two = (gate_two * grad_out).astype(jnp.bfloat16).reshape(-1, columns)
     grad_down = product(activated.T, back_two).astype(jnp.bfloat16)
-    grad_act = product(back_two, down_weight.T)
-    unused, gelu_back = jax.vjp(lambda pre: jax.nn.gelu(pre, approximate=True), hidden_pre)
-    grad_pre = gelu_back(grad_act)[0].astype(jnp.bfloat16)
+    grad_pre = (product(back_two, down_weight.T) * slope).astype(jnp.bfloat16)
     grad_up = product(flat_two.T, grad_pre).astype(jnp.bfloat16)
     grad_hidden_two = product(grad_pre, up_weight.T)
     grad_hidden_two = grad_hidden_two.reshape(grad_out.shape)
@@ -1645,13 +1667,13 @@
             [buf.reshape(ranks, -1, 128)],
         ]
         kinds = ("push", "share", "swap", "swap")
-        got = travel([(kind, (None,), 0) for kind in kinds], arrays, 6, "exchange_inputs")
+        got = travel([(kind, (None,), 0, 0) for kind in kinds], arrays, 6, "exchange_inputs")
         brought.extend(got)
         return got[3][0].reshape(buf.shape), got[2][0].reshape(new_tags.shape)
 
     slots, tags = tiles_to_slots(big_copy[0], dest, slot, rank, counts, rounds, carry_first)
     told = brought[0][0].reshape(world, -1)
-    goals = brought[1][0].reshape(ranks, micro, SEQ, PD)
+    goals = brought[1][0].reshape(ranks, micro, -1, 128)
     facts = told[:, ends_size + one_size :][:, : 4 * micro].astype(jnp.int32)
     facts = facts[:, : 2 * micro] * 32 + facts[:, 2 * micro :]
     facts = facts.reshape(ranks, groups, 2 * micro).transpose(1, 0, 2).reshape(world, -1)
@@ -1676,23 +1698,26 @@
     mod_entry = (True, 32, columns)
     mods = product(signal_own, ada_own).reshape(world, mod_rows, columns)
     mods = pad_to(mods, 1, mod_entry[1]).reshape(whole_shape(mod_entry))
-    plan = layer_plan(ranks) * 2
+    plan = (layer_plan(ranks) * 2)[:-1]
+    spread = spread_slots(slots, ranks)
     wholes, mods = travel(
-        (("gather", plan, 16), ("sum", (mod_entry,), 16)),
-        [spread_slots(slots, ranks), [mods]],
+        (("gather", plan, 16, LAG), ("sum", (mod_entry,), 16, 6)),
+        [spread[:-1], [mods]],
         1,
         "gather_weights",
     )
-    weights = [whole_weights(wholes[:4], ranks), whole_weights(wholes[4:], ranks)]
+    last, wholes = lax.optimization_barrier((spread[-1], wholes))
+    last = lax.all_gather(last, ("mp", "dp"), axis=0, tiled=True)
+    weights = [whole_weights(wholes[:4], ranks), whole_weights((*wholes[4:], last), ranks)]
     own = GROUP_WIDTH // ranks
-    mods = mods[0][:mod_rows].reshape(micro, 14, columns)
-    mod_enc = mods[:, :6]
-    mod_dec = mods[:, 6:12]
-    final_shift = mods[:, 12:13]
-    final_scale = mods[:, 13:]
-
-    goal = jnp.stack([goals[owner[b, 0], b] for b in range(micro)])
-    positions = position_table(columns)
+    mods = mods[0][:mod_rows].reshape(micro, 14, columns).transpose(1, 0, 2)[:, :, None, :]
+    mod_enc = mods[:6]
+    mod_dec = mods[6:12]
+    final_shift = mods[12]
+    final_scale = mods[13]
+
+    goal = jnp.stack([goals[owner[b, 0], b] for b in range(micro)]).reshape(micro, SEQ, PD)
+    positions = jnp.asarray(position_constant(columns))
     images = ranks * groups
     inv_count = 1.0 / (PD * micro * images * KEEP)
     place = kept_pos[:, 0]
@@ -1730,6 +1755,7 @@
     grad_dec_in, grad_mod_dec, dec_grads = own_backward(
         grad_dec_out, dec_saved, weights[1], mod_dec, own
     )
+    last_sum = lax.psum_scatter(dec_grads[3], ("mp", "dp"), scatter_dimension=0, tiled=True)
     grad_mask = jnp.sum((1.0 - kept) * grad_dec_in, axis=(0, 1))[None, :]
     grad_sent = jnp.einsum(
         "bpr,bpd->brd",
@@ -1748,11 +1774,12 @@
     vectors = vectors.astype(jnp.bfloat16).reshape(mod_rows, columns)
     vectors = pad_to(vectors, 0, mod_entry[1])
     sums, vectors = travel(
-        (("sum", plan, 16), ("gather", (mod_entry,), 16)),
-        [whole_parts(enc_grads, ranks) + whole_parts(dec_grads, ranks), [vectors]],
+        (("sum", plan, 16, LAG), ("gather", (mod_entry,), 16, 6)),
+        [whole_parts(enc_grads, ranks) + whole_parts(dec_grads, ranks)[:-1], [vectors]],
         2,
         "sum_gradients",
     )
+    sums = list(sums) + [last_sum.astype(jnp.float32)]
     sums, big_squares = collect_slots(sums, owned + 16, ranks)
     vectors = vectors[0]
     back = gather_rows(sums, tags, jnp.bfloat16)
@@ -1770,7 +1797,7 @@
     shared = pad_to(shared.reshape(world, -1), 1, 4096)
     shared_entry = (True, 32, 128)
     shared, back = travel(
-        (("sum", (shared_entry,), 32), ("swap", (None,), 0)),
+        (("sum", (shared_entry,), 32, LAG), ("swap", (None,), 0, 0)),
         [[shared.reshape(whole_shape(shared_entry))], [back.reshape(ranks, -1, 128)]],
         5,
         "sum_shared",

time: 1210 us -> 1150 us (0.950)
  Pallas kernels: 858 us -> 771 us
  local copies, waits for them, and re-layouts: 63.4 us -> 88.6 us
  between operations: 13.3 us -> 26.7 us
    pallas_call x4, Pallas kernels: 735 us -> 648 us  [travel(): pl.pallas_call(functools.partial(travel_kernel, jobs, [len(mine) for mine...]
    unnamed x350 -> x364, local copies, waits for them, and re-layouts: 16.5 us -> 36.4 us
  transfers between devices with their start and end apart: 0 -> 2, of which waited for: 0 -> 0; matrix products, arithmetic and copies ran while one was open for 0% -> 19% of each run, Pallas kernels for 0% -> 26%
where the time goes in v4:
time: 1150 us; the launch traced here: 1140 us
  Pallas kernels  771 us (67%)
  matrix products  198 us (17%)
  local copies, waits for them, and re-layouts  88.6 us (8%)
  other arithmetic  49.7 us (4%)
  between operations  26.7 us (2%)
    pallas_call x4, Pallas kernels, travel(): pl.pallas_call(functools.partial(travel_kernel, jobs, [len(mine) for mine...  648 us
    dot_general x28, matrix products, product(): return jnp.dot(left, right, preferred_element_type=jnp.float32)  177 us
    pallas_call x4, Pallas kernels, attend_call(): pl.pallas_call(kernel, grid=(images, 4), out_shape=jax.ShapeDtypeStruct((...  48.6 us
    unnamed x364, local copies, waits for them, and re-layouts  36.4 us
    pallas_call x2, Pallas kernels, gather_rows(): pl.pallas_call(functools.partial(gather_kernel, total), out_shape=jax.Sha...  27.1 us
  transfers between devices with their start and end apart: 2, of which 0 were waited for; matrix products, arithmetic and copies ran while one was open for 19% of the time, Pallas kernels for 26%

profile of v4, /device:TPU:0, one launch (start us, length us, event | category | flops | bytes accessed | tf_op | source)
XLA Modules:
  0.0 1141.5 jit_solution(5717961029622849048)
XLA Ops:
  18.9 13.0 %pack_rows.7 = bf16[9216,128]{1,0:T(8,128)(2,1)S(1)} custom-call(s32[7776]{0:T(1024)S(1)} %get-tuple-element.577.pos_ref, bf16[7776,128]{1,0:T(8,128)(2,1)S(1)} %bitcast.308), custom_call_target="tpu_custom_call" | custom-call | tf_op jit(solution)/shard_map/pack_rows/pallas_call | solution.py:615
  32.0 65.1 %exchange_inputs.1 = (bf16[32,96,128]{2,1,0:T(8,128)(2,1)S(1)}, f32[8,64,128]{2,1,0:T(8,128)S(1)}, s32[8,9,128]{2,1,0:T(8,128)S(1)}, bf16[8,1152,128]{2,1,0:T(8,128)(2,1)S(1)}) custom-call(bf16[96,128]{1,0:T(8,128)(2,1)S(1)} %pad_bitcast_fusion.1.refs_0_, f32[64,128]{1,0:T(8,128)S(1)} %reshape.969.refs_1_, s32[8,9,128]{2,1,0:T(8,128)S(1)} %compare_select_fusion.5.refs_2_, ...), custom_call_target="tpu_custom_call" | custom-call | tf_op jit(solution)/shard_map/exchange_inputs/pallas_call | solution.py:1087
  103.1 16.1 %scatter_rows.7 = bf16[7792,128]{1,0:T(8,128)(2,1)} custom-call(s32[9216]{0:T(1024)S(1)} %reshape.975.tag_ref.index_ref, bf16[9216,128]{1,0:T(8,128)(2,1)S(1)} %bitcast.299), custom_call_target="tpu_custom_call" | custom-call | tf_op jit(solution)/shard_map/scatter_rows/pallas_call | solution.py:645
  119.3 7.8 while.28
  127.2 5.5 spread_slots.1
  143.7 5.3 reshape.981
  154.1 273.8 %gather_weights.1 = (bf16[4,2,144,3584]{3,2,1,0:T(8,128)(2,1)}, bf16[4,4,2,48,1152]{4,3,2,1,0:T(8,128)(2,1)S(1)}, bf16[4,2,144,4608]{3,2,1,0:T(8,128)(2,1)}, bf1...) custom-call(bf16[144,896]{1,0:T(8,128)(2,1)S(1)} %copy-done.29, ...), custom_call_target="tpu_custom_call" | custom-call | tf_op jit(solution)/shard_map/gather_weights/pallas_call | solution.py:1087
  467.2 5.9 convolution_convert_fusion.9.packed_ref
  473.2 8.6 attend.2
  485.6 10.6 multiply_convert_fusion.2
  508.0 13.7 %attend.3 = bf16[512,1536]{1,0:T(8,128)(2,1)S(1)} custom-call(bf16[512,3584]{1,0:T(8,128)(2,1)S(1)} %convolution_convert_fusion.8.packed_ref), custom_call_target="tpu_custom_call" | custom-call | tf_op jit(solution)/shard_map/attend/pallas_call | solution.py:1453
  529.4 12.7 %fusion.182 = f32[512,4608]{1,0:T(8,128)} fusion(bf16[512,1152]{1,0:T(8,128)(2,1)S(1)} %bitcast.335, bf16[1152,4608]{1,0:T(8,128)(2,1)} %bitcast.395), kind=kOutput, calls=%fused_computation.486 | convolution fusion | flops 5435817984 | bytes 21233664 | tf_op jit(solution)/shard_map/dot_general | solution.py:42
  542.1 12.5 %fusion.163 = f32[512,1152]{1,0:T(8,128)S(1)} fusion(bf16[4608,1152]{1,0:T(8,128)(2,1)} %all-gather.2.cloned.1.call-done, f32[512,4608]{1,0:T(8,128)} %fusion.182), kind=kOutput, calls=%fused_computation.471 | convolution fusion | flops 5457051648 | bytes 22413312 | tf_op jit(solution)/shard_map/dot_general | solution.py:42
  562.2 9.9 convolution_convert_fusion
  572.2 15.7 %multiply_convert_fusion = bf16[512,4608]{1,0:T(8,128)(2,1)} fusion(f32[512,4608]{1,0:T(8,128)} %fusion.182, bf16[512,1152]{1,0:T(8,128)(2,1)} %bitcast.340, bf16[4608,1152]{1,0:T(8,128)(2,1)} %all-gather.2.cloned.1.call-done), kind=kOutput, calls=%fused_computation.82 | convolution fusion | flops 5478285312 | bytes 25952256 | tf_op jit(solution)/shard_map/dot_general | solution.py:42
  587.9 13.5 %multiply_reduce_fusion.4 = (bf16[2,1152]{1,0:T(2,128)(2,1)S(1)}, f32[2,256]{1,0:T(2,128)S(1)}, f32[2,256]{1,0:T(2,128)S(1)}, bf16[2,1152]{1,0:T(2,128)(2,1)S(1)}, f32[2,256,1152]{2,1,0:T(8,128)}) fusion(f32[2,256,1152]{2,1,0:T(8,128)S(1)} %copy-done.53, f32[2,256]{1,0:T(2,128)S(1)} %add_rsqrt_fusion.1, f32[2,256]{1,0:T(2,128)S(1)} %broadcast_multiply_fusion.10, ...), kind=kOutput, calls=%fused_computation.112 | convolution fusion | flops 5441121280 | bytes 20080640 | tf_op jit(solution)/shard_map/dot_general | solution.py:42
  609.0 17.5 %attend_back.2 = bf16[512,3584]{1,0:T(8,128)(2,1)S(1)} custom-call(bf16[512,3584]{1,0:T(8,128)(2,1)} %copy-done, bf16[512,1536]{1,0:T(8,128)(2,1)S(1)} %convolution_convert_fusion.10.grad_ref, bf16[4,72,384]{2,1,0:T(8,128)(2,1)S(1)} %compare_convert_fusion.spread_ref), custom_call_target="tpu_custom_call" | custom-call | tf_op jit(solution)/shard_map/attend_back/pallas_call | solution.py:1453
  626.6 10.1 multiply_reduce_fusion.6
  639.2 8.3 fusion.28
  661.6 8.7 attend_back.3
  670.4 7.0 multiply_reduce_fusion.16
  692.1 5.6 convolution_convert_fusion.5
  697.7 5.7 convolution_convert_fusion.3
  703.4 6.1 convolution_convert_fusion.2
  709.5 8.4 convolution_convert_fusion.1
  717.9 6.7 convolution_convert_fusion.4
  724.7 250.3 %sum_gradients.1 = (f32[144,896]{1,0:T(8,128)S(1)}, f32[48,1152]{1,0:T(8,128)S(1)}, f32[144,1152]{1,0:T(8,128)S(1)}, f32[144,1152]{1,0:T(8,128)S(1)}, f32[144,89...) custom-call(bf16[4,2,144,3584]{3,2,1,0:T(8,128)(2,1)} %bitcast.311, ...), custom_call_target="tpu_custom_call" | custom-call | tf_op jit(solution)/shard_map/sum_gradients/pallas_call | solution.py:1087
  1005.9 12.6 %gather_rows.14 = bf16[9216,128]{1,0:T(8,128)(2,1)S(1)} custom-call(s32[9216]{0:T(1024)S(1)} %copy-done.27, f32[7792,128]{1,0:T(8,128)} %get-tuple-element.896.x_ref), custom_call_target="tpu_custom_call" | custom-call | tf_op jit(solution)/shard_map/gather_rows/pallas_call | solution.py:661
  1018.6 58.7 %sum_shared.1 = (f32[32,128]{1,0:T(8,128)S(1)}, bf16[8,1152,128]{2,1,0:T(8,128)(2,1)S(1)}) custom-call(f32[4,4,2,32,128]{4,3,2,1,0:T(8,128)S(1)} %bitcast.301, bf16[8,1152,128]{2,1,0:T(8,128)(2,1)S(1)} %bitcast.291), custom_call_target="tpu_custom_call" | custom-call | tf_op jit(solution)/shard_map/sum_shared/pallas_call | solution.py:1087
  1081.5 9.6 push_totals.1
  1100.7 14.5 %gather_rows.15 = f32[7776,128]{1,0:T(8,128)} custom-call(s32[7776]{0:T(1024)S(1)} %copy-done.37, f32[9216,128]{1,0:T(8,128)S(1)} %bitcast_convert_fusion.1.x_ref), custom_call_target="tpu_custom_call" | custom-call | tf_op jit(solution)/shard_map/gather_rows/pallas_call | solution.py:661
  1122.0 11.1 fusion.168
  (552 shorter events, 184.1 us)
Async XLA Ops:
  7.2 534.9 %all-gather.2.cloned.1.call-start = ((), (), s32[]{:S(2)}) async-start(), calls=%async_computation.5 | async-start | bytes 10948608 | tf_op jit(solution)/shard_map/all_gather | solution.py:1710
  9.8 130.8 %copy-start.102 = (bf16[36,2442]{1,0:T(8,128)(2,1)}, bf16[36,2442]{1,0:T(8,128)(2,1)S(1)}, u32[]{:S(2)}) copy-start(bf16[36,2442]{1,0:T(8,128)(2,1)S(1)} %reshape.965) | copy-start | bytes 527476
  102.9 37.8 %copy-start.150 = (s32[64]{0:T(128)}, s32[64]{0:T(128)S(1)}, u32[]{:S(2)}) copy-start(s32[64]{0:T(128)S(1)} %eq.265) | copy-start | bytes 772
  103.1 16.1 %copy-start.26 = (s32[9216]{0:T(1024)}, s32[9216]{0:T(1024)S(1)}, u32[]{:S(2)}) copy-start(s32[9216]{0:T(1024)S(1)} %reshape.975.tag_ref.index_ref) | copy-start | bytes 110596
  127.1 13.2 %copy-start.62 = (s32[7776]{0:T(1024)}, s32[7776]{0:T(1024)S(1)}, u32[]{:S(2)}) copy-start(s32[7776]{0:T(1024)S(1)} %get-tuple-element.937) | copy-start | bytes 93316
  127.1 13.2 %copy-start.65 = (s32[7776]{0:T(1024)}, s32[7776]{0:T(1024)S(1)}, u32[]{:S(2)}) copy-start(s32[7776]{0:T(1024)S(1)} %get-tuple-element.938) | copy-start | bytes 93316
  127.2 13.8 %copy-start.59 = (bf16[36,16128]{1,0:T(8,128)(2,1)S(1)}, bf16[36,16128]{1,0:T(8,128)(2,1)}, u32[]{:S(2)}) copy-start(bf16[36,16128]{1,0:T(8,128)(2,1)} %reshape.980) | copy-start | bytes 3483652
  154.1 281.0 %copy-start.139 = (f32[2,1,128,16]{2,3,1,0:T(8,128)S(1)}, f32[2,1,128,16]{2,3,1,0:T(8,128)}, u32[]{:S(2)}) copy-start(f32[2,1,128,16]{2,3,1,0:T(8,128)} %param.38) | copy-start | bytes 49156
  428.6 53.6 %copy-start.7 = (bf16[4,4,2,48,1152]{4,3,2,1,0:T(8,128)(2,1)}, bf16[4,4,2,48,1152]{4,3,2,1,0:T(8,128)(2,1)S(1)}, u32[]{:S(2)}) copy-start(bf16[4,4,2,48,1152]{4,3,2,1,0:T(8,128)(2,1)S(1)} %get-tuple-element.473) | copy-start | bytes 10616836
  428.7 570.1 %reduce-scatter.2.cloned.1.call-start = ((), (), s32[]{:S(2)}) async-start(), calls=%async_computation.6 | async-start | bytes 10948608 | tf_op jit(solution)/shard_map/reduce_scatter | solution.py:1758
  484.8 14.6 %copy-start.54 = (f32[2,128,1152]{2,1,0:T(8,128)}, f32[2,128,1152]{2,1,0:T(8,128)S(1)}, u32[]{:S(2)}) copy-start(f32[2,128,1152]{2,1,0:T(8,128)S(1)} %get-tuple-element.591) | copy-start | bytes 3538948
  485.2 17.6 %slice-start.6 = ((s8[8257536]{0:T(1024)(128)(4,1)}), s8[4194304]{0:T(1024)(128)(4,1)S(1)}, s32[]{:S(2)}) async-start(s8[8257536]{0:T(1024)(128)(4,1)} %bitcast.400), calls=%async_computation.13 | async-start | bytes 8388608
  485.5 17.2 %slice-start.7 = ((s8[8257536]{0:T(1024)(128)(4,1)}), s8[4063232]{0:T(1024)(128)(4,1)S(1)}, s32[]{:S(2)}) async-start(s8[8257536]{0:T(1024)(128)(4,1)} %bitcast.400), calls=%async_computation.14 | async-start | bytes 8126464
  500.5 21.2 %copy-start.49 = (f32[2,256,1152]{2,1,0:T(8,128)}, f32[2,256,1152]{2,1,0:T(8,128)S(1)}, u32[]{:S(2)}) copy-start(f32[2,256,1152]{2,1,0:T(8,128)S(1)} %get-tuple-element.656) | copy-start | bytes 7077892
  507.9 13.7 %copy-start = (bf16[512,3584]{1,0:T(8,128)(2,1)}, bf16[512,3584]{1,0:T(8,128)(2,1)S(1)}, u32[]{:S(2)}) copy-start(bf16[512,3584]{1,0:T(8,128)(2,1)S(1)} %convolution_convert_fusion.8.packed_ref) | copy-start | bytes 11010052
  508.0 13.8 %copy-start.132 = (f32[1,2,1152]{2,1,0:T(2,128)S(1)}, f32[1,2,1152]{2,1,0:T(2,128)}, u32[]{:S(2)}) copy-start(f32[1,2,1152]{2,1,0:T(2,128)} %copy.229) | copy-start | bytes 27652
  508.0 13.8 %copy-start.152 = (bf16[4,4,2,48,1152]{4,3,2,1,0:T(8,128)(2,1)S(1)}, bf16[4,4,2,48,1152]{4,3,2,1,0:T(8,128)(2,1)}, u32[]{:S(2)}) copy-start(bf16[4,4,2,48,1152]{4,3,2,1,0:T(8,128)(2,1)} %get-tuple-element.477) | copy-start | bytes 10616836
  572.2 15.7 %copy-start.53 = (f32[2,256,1152]{2,1,0:T(8,128)S(1)}, f32[2,256,1152]{2,1,0:T(8,128)}, u32[]{:S(2)}) copy-start(f32[2,256,1152]{2,1,0:T(8,128)} %copy-done.51) | copy-start | bytes 7077892
  587.8 13.5 %copy-start.58 = (f32[2,256,1152]{2,1,0:T(8,128)S(1)}, f32[2,256,1152]{2,1,0:T(8,128)}, u32[]{:S(2)}) copy-start(f32[2,256,1152]{2,1,0:T(8,128)} %copy-done.57) | copy-start | bytes 7077892
  587.8 13.5 %copy-start.90 = (f32[2,256,1152]{2,1,0:T(8,128)S(1)}, f32[2,256,1152]{2,1,0:T(8,128)}, u32[]{:S(2)}) copy-start(f32[2,256,1152]{2,1,0:T(8,128)} %get-tuple-element.657) | copy-start | bytes 7077892
  609.0 17.6 %copy-start.50 = (f32[2,256,1152]{2,1,0:T(8,128)S(1)}, f32[2,256,1152]{2,1,0:T(8,128)}, u32[]{:S(2)}) copy-start(f32[2,256,1152]{2,1,0:T(8,128)} %copy-done.49) | copy-start | bytes 7077892
  1018.5 59.2 %copy-start.142 = (bf16[64,128]{1,0:T(8,128)(2,1)S(1)}, bf16[64,128]{1,0:T(8,128)(2,1)}, u32[]{:S(2)}) copy-start(bf16[64,128]{1,0:T(8,128)(2,1)} %copy-done.140) | copy-start | bytes 49156
  1018.5 59.2 %copy-start.145 = (bf16[64,128]{1,0:T(8,128)(2,1)S(1)}, bf16[64,128]{1,0:T(8,128)(2,1)}, u32[]{:S(2)}) copy-start(bf16[64,128]{1,0:T(8,128)(2,1)} %copy-done.143) | copy-start | bytes 49156
  1018.5 59.2 %copy-start.156 = (f32[64,36]{0,1:T(8,128)S(1)}, f32[64,36]{0,1:T(8,128)}, u32[]{:S(2)}) copy-start(f32[64,36]{0,1:T(8,128)} %fusion.130) | copy-start | bytes 27652
  1018.5 59.4 %copy-start.103 = (f32[36,1152]{1,0:T(8,128)S(1)}, f32[36,1152]{1,0:T(8,128)}, u32[]{:S(2)}) copy-start(f32[36,1152]{1,0:T(8,128)} %fusion.160) | copy-start | bytes 497668
  1018.5 59.4 %copy-start.104 = (f32[36,1001]{1,0:T(8,128)S(1)}, f32[36,1001]{1,0:T(8,128)}, u32[]{:S(2)}) copy-start(f32[36,1001]{1,0:T(8,128)} %fusion.62) | copy-start | bytes 432436
  1100.7 14.5 %copy-start.110 = (f32[87912]{0:T(1024)S(1)}, f32[87912]{0:T(1024)}, u32[]{:S(2)}) copy-start(f32[87912]{0:T(1024)} %param.34) | copy-start | bytes 1054948
  1100.7 14.5 %copy-start.111 = (f32[87912]{0:T(1024)S(1)}, f32[87912]{0:T(1024)}, u32[]{:S(2)}) copy-start(f32[87912]{0:T(1024)} %param.36) | copy-start | bytes 1054948
  1100.7 14.5 %copy-start.112 = (f32[87912]{0:T(1024)S(1)}, f32[87912]{0:T(1024)}, u32[]{:S(2)}) copy-start(f32[87912]{0:T(1024)} %param.35) | copy-start | bytes 1054948
  1100.7 15.7 %copy-start.92 = (f32[580608]{0:T(1024)S(1)}, f32[580608]{0:T(1024)}, u32[]{:S(2)}) copy-start(f32[580608]{0:T(1024)} %param.30) | copy-start | bytes 6967300
  1100.7 15.7 %copy-start.93 = (f32[580608]{0:T(1024)S(1)}, f32[580608]{0:T(1024)}, u32[]{:S(2)}) copy-start(f32[580608]{0:T(1024)} %param.32) | copy-start | bytes 6967300
  1100.7 15.7 %copy-start.94 = (f32[580608]{0:T(1024)S(1)}, f32[580608]{0:T(1024)}, u32[]{:S(2)}) copy-start(f32[580608]{0:T(1024)} %param.31) | copy-start | bytes 6967300
  (136 other events, 637.4 us)
Sparse Core Ops, SparseCore 0:
  428.8 88.2 all-gather.1
  572.3 143.0 reduce-scatter.1

commit v5 on v4

--- a/solution.py
+++ b/solution.py
@@ -1030,16 +1030,19 @@
     else:
         other, first, second, others = neighbours()
         greet([other, first, second] + others)
-    for begin, unused_end in direct:
-        begin()
 
     def step(t, unused):
         for one, unused_count in steps:
             one(t)
         return unused
 
+    if direct and steps:
+        step(0, 0)
+    for begin, unused_end in direct:
+        begin()
     if steps:
-        lax.fori_loop(0, max(count for unused_step, count in steps), step, 0)
+        first_step = 1 if direct else 0
+        lax.fori_loop(first_step, max(count for unused_step, count in steps), step, 0)
     for unused_begin, end in direct:
         end()
 
@@ -1184,7 +1187,12 @@
         fresh = jnp.zeros((n + 16,), jnp.bool_).at[more_tags].set(True)
         return turn + 1, jnp.where(fresh[:, None], added, slots)
 
-    unused, slots = lax.while_loop(lambda carry: carry[0] < rounds, more, (1, first))
+    slots = lax.cond(
+        rounds > 1,
+        lambda start: lax.while_loop(lambda carry: carry[0] < rounds, more, (1, start))[1],
+        lambda start: start,
+        first,
+    )
     return slots, tags
 
 
@@ -1657,6 +1665,7 @@
         ]
     )
     told = pad_to(told, 0, -(-told.shape[0] // 2048) * 2048).reshape(-1, 128)
+    told_entry = (True, told.shape[0], 128)
     brought = []
 
     def carry_first(buf, new_tags):
@@ -1666,17 +1675,20 @@
             [new_tags.reshape(ranks, -1, 128)],
             [buf.reshape(ranks, -1, 128)],
         ]
-        kinds = ("push", "share", "swap", "swap")
-        got = travel([(kind, (None,), 0, 0) for kind in kinds], arrays, 6, "exchange_inputs")
+        kinds = ("share", "swap", "swap")
+        jobs = [("gather", (told_entry,), told_entry[1], LAG)]
+        jobs += [(kind, (None,), 0, 0) for kind in kinds]
+        got = travel(jobs, arrays, 6, "exchange_inputs")
         brought.extend(got)
         return got[3][0].reshape(buf.shape), got[2][0].reshape(new_tags.shape)
 
     slots, tags = tiles_to_slots(big_copy[0], dest, slot, rank, counts, rounds, carry_first)
-    told = brought[0][0].reshape(world, -1)
+    told = brought[0][0].reshape(groups, ranks, -1)
+    facts = told[:, :, ends_size + one_size : ends_size + one_size + 4 * micro].astype(jnp.int32)
+    facts = facts.reshape(world, -1)
+    told = told.transpose(1, 0, 2).reshape(world, -1)
     goals = brought[1][0].reshape(ranks, micro, -1, 128)
-    facts = told[:, ends_size + one_size :][:, : 4 * micro].astype(jnp.int32)
     facts = facts[:, : 2 * micro] * 32 + facts[:, 2 * micro :]
-    facts = facts.reshape(ranks, groups, 2 * micro).transpose(1, 0, 2).reshape(world, -1)
     stamps = facts[:, :micro].reshape(-1)
     tags_all = facts[:, micro:].reshape(-1)
     ends = told[:, :ends_size].reshape(columns, -1)
@@ -1696,8 +1708,9 @@
     ada_own = ada_copy.reshape(own_columns, 14 * columns)
     mod_rows = micro * 14
     mod_entry = (True, 32, columns)
-    mods = product(signal_own, ada_own).reshape(world, mod_rows, columns)
-    mods = pad_to(mods, 1, mod_entry[1]).reshape(whole_shape(mod_entry))
+    padded = mod_entry[1] // micro
+    mods = product(signal_own, pad_to(ada_own, 1, padded * columns)).reshape(-1, padded, columns)
+    mods = mods.reshape(whole_shape(mod_entry))
     plan = (layer_plan(ranks) * 2)[:-1]
     spread = spread_slots(slots, ranks)
     wholes, mods = travel(
@@ -1710,7 +1723,7 @@
     last = lax.all_gather(last, ("mp", "dp"), axis=0, tiled=True)
     weights = [whole_weights(wholes[:4], ranks), whole_weights((*wholes[4:], last), ranks)]
     own = GROUP_WIDTH // ranks
-    mods = mods[0][:mod_rows].reshape(micro, 14, columns).transpose(1, 0, 2)[:, :, None, :]
+    mods = mods[0].reshape(micro, padded, columns).transpose(1, 0, 2)[:, :, None, :]
     mod_enc = mods[:6]
     mod_dec = mods[6:12]
     final_shift = mods[12]
@@ -1766,6 +1779,7 @@
     grad_embedded, grad_mod_enc, enc_grads = own_backward(
         grad_sent, enc_saved, weights[0], mod_enc, own
     )
+    down_sum = lax.psum_scatter(enc_grads[3], ("mp", "dp"), scatter_dimension=0, tiled=True)
     grad_embed = contract_wide(
         patches.reshape(-1, PD), grad_embedded.reshape(-1, columns), 0, 0
     )
@@ -1774,12 +1788,12 @@
     vectors = vectors.astype(jnp.bfloat16).reshape(mod_rows, columns)
     vectors = pad_to(vectors, 0, mod_entry[1])
     sums, vectors = travel(
-        (("sum", plan, 16, LAG), ("gather", (mod_entry,), 16, 6)),
-        [whole_parts(enc_grads, ranks) + whole_parts(dec_grads, ranks)[:-1], [vectors]],
+        (("sum", (layer_plan(ranks)[:-1]) * 2, 16, LAG), ("gather", (mod_entry,), 16, 6)),
+        [whole_parts(enc_grads, ranks)[:-1] + whole_parts(dec_grads, ranks)[:-1], [vectors]],
         2,
         "sum_gradients",
     )
-    sums = list(sums) + [last_sum.astype(jnp.float32)]
+    sums = [*sums[:3], down_sum.astype(jnp.float32), *sums[3:], last_sum.astype(jnp.float32)]
     sums, big_squares = collect_slots(sums, owned + 16, ranks)
     vectors = vectors[0]
     back = gather_rows(sums, tags, jnp.bfloat16)

time: 1150 us -> 1130 us (0.983)
  Pallas kernels: 771 us -> 744 us
    pallas_call x4, Pallas kernels: 648 us -> 623 us  [travel(): pl.pallas_call(functools.partial(travel_kernel, jobs, [len(mine) for mine...]
    unnamed x364 -> x348, local copies, waits for them, and re-layouts: 36.4 us -> 42.5 us
  transfers between devices with their start and end apart: 2 -> 3, of which waited for: 0 -> 0; matrix products, arithmetic and copies ran while one was open for 19% -> 20% of each run, Pallas kernels for 26% -> 26%
where the time goes in v5:
time: 1130 us; the launch traced here: 1120 us
  Pallas kernels  744 us (66%)
  matrix products  202 us (18%)
  local copies, waits for them, and re-layouts  93.8 us (8%)
  other arithmetic  49.6 us (4%)
  between operations  26.1 us (2%)
    pallas_call x4, Pallas kernels, travel(): pl.pallas_call(functools.partial(travel_kernel, jobs, [len(mine) for mine...  623 us
    dot_general x28, matrix products, product(): return jnp.dot(left, right, preferred_element_type=jnp.float32)  181 us
    pallas_call x4, Pallas kernels, attend_call(): pl.pallas_call(kernel, grid=(images, 4), out_shape=jax.ShapeDtypeStruct((...  48.9 us
    unnamed x348, local copies, waits for them, and re-layouts  42.5 us
    pallas_call x2, Pallas kernels, gather_rows(): pl.pallas_call(functools.partial(gather_kernel, total), out_shape=jax.Sha...  26.1 us
  transfers between devices with their start and end apart: 3, of which 0 were waited for; matrix products, arithmetic and copies ran while one was open for 20% of the time, Pallas kernels for 26%

profile of v5, /device:TPU:0, one launch (start us, length us, event | category | flops | bytes accessed | tf_op | source)
XLA Modules:
  0.0 1122.6 jit_solution(17883912335156592483)
XLA Ops:
  20.0 13.0 %pack_rows.7 = bf16[9216,128]{1,0:T(8,128)(2,1)S(1)} custom-call(s32[7776]{0:T(1024)S(1)} %get-tuple-element.601.pos_ref, bf16[7776,128]{1,0:T(8,128)(2,1)S(1)} %bitcast.306), custom_call_target="tpu_custom_call" | custom-call | tf_op jit(solution)/shard_map/pack_rows/pallas_call | solution.py:615
  33.1 54.6 %exchange_inputs.1 = (bf16[4,4,2,96,128]{4,3,2,1,0:T(8,128)(2,1)S(1)}, f32[8,64,128]{2,1,0:T(8,128)S(1)}, s32[8,9,128]{2,1,0:T(8,128)S(1)}, bf16[8,1152,128]{2,1,0:T(8,128)(2,1)S(1)}) custom-call(bf16[96,128]{1,0:T(8,128)(2,1)S(1)} %pad_bitcast_fusion.1.refs_0_, f32[64,128]{1,0:T(8,128)S(1)} %reshape.965.refs_1_, ...), custom_call_target="tpu_custom_call" | custom-call | tf_op jit(solution)/shard_map/exchange_inputs/pallas_call | solution.py:1090
  97.1 16.1 %scatter_rows.7 = bf16[7792,128]{1,0:T(8,128)(2,1)} custom-call(s32[9216]{0:T(1024)S(1)} %reshape.972.tag_ref.index_ref, bf16[9216,128]{1,0:T(8,128)(2,1)S(1)} %bitcast.298), custom_call_target="tpu_custom_call" | custom-call | tf_op jit(solution)/shard_map/scatter_rows/pallas_call | solution.py:645
  113.2 7.5 conditional.1
  120.8 5.4 spread_slots.1
  149.0 271.1 %gather_weights.1 = (bf16[4,2,144,3584]{3,2,1,0:T(8,128)(2,1)}, bf16[4,4,2,48,1152]{4,3,2,1,0:T(8,128)(2,1)S(1)}, bf16[4,2,144,4608]{3,2,1,0:T(8,128)(2,1)}, bf1...) custom-call(bf16[144,896]{1,0:T(8,128)(2,1)S(1)} %copy-done.27, ...), custom_call_target="tpu_custom_call" | custom-call | tf_op jit(solution)/shard_map/gather_weights/pallas_call | solution.py:1090
  457.3 5.9 convolution_convert_fusion.9.packed_ref
  463.3 8.6 attend.2
  475.6 10.5 multiply_convert_fusion.2
  497.9 13.7 %attend.3 = bf16[512,1536]{1,0:T(8,128)(2,1)S(1)} custom-call(bf16[512,3584]{1,0:T(8,128)(2,1)S(1)} %convolution_convert_fusion.8.packed_ref), custom_call_target="tpu_custom_call" | custom-call | tf_op jit(solution)/shard_map/attend/pallas_call | solution.py:1461
  517.7 12.6 %fusion.186 = f32[512,4608]{1,0:T(8,128)} fusion(bf16[512,1152]{1,0:T(8,128)(2,1)S(1)} %bitcast.329, bf16[1152,4608]{1,0:T(8,128)(2,1)} %bitcast.385), kind=kOutput, calls=%fused_computation.492 | convolution fusion | flops 5435817984 | bytes 21233664 | tf_op jit(solution)/shard_map/dot_general | solution.py:42
  530.4 12.5 %fusion.166 = f32[512,1152]{1,0:T(8,128)S(1)} fusion(bf16[4608,1152]{1,0:T(8,128)(2,1)} %all-gather.2.cloned.1.call-done, f32[512,4608]{1,0:T(8,128)} %fusion.186), kind=kOutput, calls=%fused_computation.476 | convolution fusion | flops 5457051648 | bytes 22413312 | tf_op jit(solution)/shard_map/dot_general | solution.py:42
  550.5 9.9 convolution_convert_fusion
  564.3 15.9 %multiply_convert_fusion = bf16[512,4608]{1,0:T(8,128)(2,1)} fusion(f32[512,4608]{1,0:T(8,128)} %fusion.186, bf16[512,1152]{1,0:T(8,128)(2,1)} %bitcast.334, bf16[4608,1152]{1,0:T(8,128)(2,1)} %all-gather.2.cloned.1.call-done), kind=kOutput, calls=%fused_computation.82 | convolution fusion | flops 5478285312 | bytes 25952256 | tf_op jit(solution)/shard_map/dot_general | solution.py:42
  580.2 13.3 %multiply_reduce_fusion.4 = (bf16[2,1152]{1,0:T(2,128)(2,1)S(1)}, f32[2,256]{1,0:T(2,128)S(1)}, f32[2,256]{1,0:T(2,128)S(1)}, bf16[2,1152]{1,0:T(2,128)(2,1)S(1)}, f32[2,256,1152]{2,1,0:T(8,128)}) fusion(f32[2,256,1152]{2,1,0:T(8,128)S(1)} %copy-done.54, f32[2,256]{1,0:T(2,128)S(1)} %add_rsqrt_fusion.1, f32[2,256]{1,0:T(2,128)S(1)} %broadcast_multiply_fusion.10, ...), kind=kOutput, calls=%fused_computation.112 | convolution fusion | flops 5441121280 | bytes 20080640 | tf_op jit(solution)/shard_map/dot_general | solution.py:42
  601.2 17.9 %attend_back.2 = bf16[512,3584]{1,0:T(8,128)(2,1)S(1)} custom-call(bf16[512,3584]{1,0:T(8,128)(2,1)} %copy-done, bf16[512,1536]{1,0:T(8,128)(2,1)S(1)} %convolution_convert_fusion.10.grad_ref, bf16[4,72,384]{2,1,0:T(8,128)(2,1)S(1)} %compare_convert_fusion.spread_ref), custom_call_target="tpu_custom_call" | custom-call | tf_op jit(solution)/shard_map/attend_back/pallas_call | solution.py:1461
  619.1 10.0 multiply_reduce_fusion.6
  632.4 5.8 convolution_convert_fusion.1
  638.2 9.2 fusion.28
  650.8 8.9 multiply_reduce_fusion.18
  663.9 8.7 attend_back.3
  672.7 7.0 multiply_reduce_fusion.16
  693.4 5.6 convolution_convert_fusion.5
  699.0 5.7 convolution_convert_fusion.3
  704.7 8.6 convolution_convert_fusion.2
  713.3 6.7 convolution_convert_fusion.4
  720.0 238.6 %sum_gradients.1 = (f32[144,896]{1,0:T(8,128)S(1)}, f32[48,1152]{1,0:T(8,128)S(1)}, f32[144,1152]{1,0:T(8,128)S(1)}, f32[144,896]{1,0:T(8,128)S(1)}, f32[48,1152...) custom-call(bf16[4,2,144,3584]{3,2,1,0:T(8,128)(2,1)} %bitcast.308, ...), custom_call_target="tpu_custom_call" | custom-call | tf_op jit(solution)/shard_map/sum_gradients/pallas_call | solution.py:1090
  987.4 11.6 %gather_rows.14 = bf16[9216,128]{1,0:T(8,128)(2,1)S(1)} custom-call(s32[9216]{0:T(1024)S(1)} %copy-done.25, f32[7792,128]{1,0:T(8,128)S(1)} %get-tuple-element.920.x_ref), custom_call_target="tpu_custom_call" | custom-call | tf_op jit(solution)/shard_map/gather_rows/pallas_call | solution.py:661
  999.1 59.0 %sum_shared.1 = (f32[32,128]{1,0:T(8,128)S(1)}, bf16[8,1152,128]{2,1,0:T(8,128)(2,1)S(1)}) custom-call(f32[4,4,2,32,128]{4,3,2,1,0:T(8,128)S(1)} %bitcast.300, bf16[8,1152,128]{2,1,0:T(8,128)(2,1)S(1)} %bitcast.290), custom_call_target="tpu_custom_call" | custom-call | tf_op jit(solution)/shard_map/sum_shared/pallas_call | solution.py:1090
  1062.9 9.6 push_totals.1
  1082.2 14.5 %gather_rows.15 = f32[7776,128]{1,0:T(8,128)} custom-call(s32[7776]{0:T(1024)S(1)} %copy-done.34, f32[9216,128]{1,0:T(8,128)S(1)} %bitcast_convert_fusion.1.x_ref), custom_call_target="tpu_custom_call" | custom-call | tf_op jit(solution)/shard_map/gather_rows/pallas_call | solution.py:661
  1103.4 11.1 fusion.171
  (534 shorter events, 187.1 us)
Async XLA Ops:
  7.2 523.2 %all-gather.2.cloned.1.call-start = ((), (), s32[]{:S(2)}) async-start(), calls=%async_computation.6 | async-start | bytes 10948608 | tf_op jit(solution)/shard_map/all_gather | solution.py:1723
  8.9 104.3 %copy-start.65 = (s32[7776]{0:T(1024)}, s32[7776]{0:T(1024)S(1)}, u32[]{:S(2)}) copy-start(s32[7776]{0:T(1024)S(1)} %get-tuple-element.917) | copy-start | bytes 93316
  8.9 104.3 %copy-start.67 = (s32[7776]{0:T(1024)}, s32[7776]{0:T(1024)S(1)}, u32[]{:S(2)}) copy-start(s32[7776]{0:T(1024)S(1)} %get-tuple-element.914) | copy-start | bytes 93316
  9.2 103.9 %copy-start.152 = (s32[8]{0:T(128)}, s32[8]{0:T(128)S(1)}, u32[]{:S(2)}) copy-start(s32[8]{0:T(128)S(1)} %convert_element_type.262) | copy-start | bytes 100
  16.8 96.4 %copy-start.62 = (s32[7776]{0:T(1024)}, s32[7776]{0:T(1024)S(1)}, u32[]{:S(2)}) copy-start(s32[7776]{0:T(1024)S(1)} %convert_element_type.264) | copy-start | bytes 93316
  96.9 36.9 %copy-start.148 = (s32[64]{0:T(128)}, s32[64]{0:T(128)S(1)}, u32[]{:S(2)}) copy-start(s32[64]{0:T(128)S(1)} %eq.265) | copy-start | bytes 772
  97.1 16.1 %copy-start.24 = (s32[9216]{0:T(1024)}, s32[9216]{0:T(1024)S(1)}, u32[]{:S(2)}) copy-start(s32[9216]{0:T(1024)S(1)} %reshape.972.tag_ref.index_ref) | copy-start | bytes 110596
  149.0 277.6 %copy-start.137 = (f32[2,1,128,16]{2,3,1,0:T(8,128)S(1)}, f32[2,1,128,16]{2,3,1,0:T(8,128)}, u32[]{:S(2)}) copy-start(f32[2,1,128,16]{2,3,1,0:T(8,128)} %param.40) | copy-start | bytes 49156
  420.8 51.5 %copy-start.7 = (bf16[4,4,2,48,1152]{4,3,2,1,0:T(8,128)(2,1)}, bf16[4,4,2,48,1152]{4,3,2,1,0:T(8,128)(2,1)S(1)}, u32[]{:S(2)}) copy-start(bf16[4,4,2,48,1152]{4,3,2,1,0:T(8,128)(2,1)S(1)} %get-tuple-element.496) | copy-start | bytes 10616836
  420.8 561.4 %reduce-scatter.5.cloned.1.call-start = ((), (), s32[]{:S(2)}) async-start(), calls=%async_computation.8 | async-start | bytes 10948608 | tf_op jit(solution)/shard_map/reduce_scatter | solution.py:1771
  474.9 14.5 %copy-start.55 = (f32[2,128,1152]{2,1,0:T(8,128)}, f32[2,128,1152]{2,1,0:T(8,128)S(1)}, u32[]{:S(2)}) copy-start(f32[2,128,1152]{2,1,0:T(8,128)S(1)} %get-tuple-element.615) | copy-start | bytes 3538948
  475.3 17.5 %slice-start.3 = ((s8[8257536]{0:T(1024)(128)(4,1)}), s8[4194304]{0:T(1024)(128)(4,1)S(1)}, s32[]{:S(2)}) async-start(s8[8257536]{0:T(1024)(128)(4,1)} %bitcast.390), calls=%async_computation.12 | async-start | bytes 8388608
  475.6 17.1 %slice-start.4 = ((s8[8257536]{0:T(1024)(128)(4,1)}), s8[4063232]{0:T(1024)(128)(4,1)S(1)}, s32[]{:S(2)}) async-start(s8[8257536]{0:T(1024)(128)(4,1)} %bitcast.390), calls=%async_computation.13 | async-start | bytes 8126464
  490.5 21.2 %copy-start.50 = (f32[2,256,1152]{2,1,0:T(8,128)}, f32[2,256,1152]{2,1,0:T(8,128)S(1)}, u32[]{:S(2)}) copy-start(f32[2,256,1152]{2,1,0:T(8,128)S(1)} %get-tuple-element.680) | copy-start | bytes 7077892
  497.9 13.7 %copy-start = (bf16[512,3584]{1,0:T(8,128)(2,1)}, bf16[512,3584]{1,0:T(8,128)(2,1)S(1)}, u32[]{:S(2)}) copy-start(bf16[512,3584]{1,0:T(8,128)(2,1)S(1)} %convolution_convert_fusion.8.packed_ref) | copy-start | bytes 11010052
  497.9 13.7 %copy-start.130 = (f32[1,2,1152]{2,1,0:T(2,128)S(1)}, f32[1,2,1152]{2,1,0:T(2,128)}, u32[]{:S(2)}) copy-start(f32[1,2,1152]{2,1,0:T(2,128)} %copy.202) | copy-start | bytes 27652
  497.9 13.7 %copy-start.150 = (bf16[4,4,2,48,1152]{4,3,2,1,0:T(8,128)(2,1)S(1)}, bf16[4,4,2,48,1152]{4,3,2,1,0:T(8,128)(2,1)}, u32[]{:S(2)}) copy-start(bf16[4,4,2,48,1152]{4,3,2,1,0:T(8,128)(2,1)} %get-tuple-element.500) | copy-start | bytes 10616836
  560.5 422.7 %reduce-scatter.3.cloned.1.call-start = ((), (), s32[]{:S(2)}) async-start(), calls=%async_computation.7 | async-start | bytes 10948608 | tf_op jit(solution)/shard_map/reduce_scatter | solution.py:1782
  564.3 15.9 %copy-start.54 = (f32[2,256,1152]{2,1,0:T(8,128)S(1)}, f32[2,256,1152]{2,1,0:T(8,128)}, u32[]{:S(2)}) copy-start(f32[2,256,1152]{2,1,0:T(8,128)} %copy-done.52) | copy-start | bytes 7077892
  580.2 13.4 %copy-start.86 = (f32[2,256,1152]{2,1,0:T(8,128)S(1)}, f32[2,256,1152]{2,1,0:T(8,128)}, u32[]{:S(2)}) copy-start(f32[2,256,1152]{2,1,0:T(8,128)} %get-tuple-element.681) | copy-start | bytes 7077892
  601.2 17.9 %copy-start.51 = (f32[2,256,1152]{2,1,0:T(8,128)S(1)}, f32[2,256,1152]{2,1,0:T(8,128)}, u32[]{:S(2)}) copy-start(f32[2,256,1152]{2,1,0:T(8,128)} %copy-done.50) | copy-start | bytes 7077892
  999.0 59.5 %copy-start.140 = (bf16[64,128]{1,0:T(8,128)(2,1)S(1)}, bf16[64,128]{1,0:T(8,128)(2,1)}, u32[]{:S(2)}) copy-start(bf16[64,128]{1,0:T(8,128)(2,1)} %copy-done.138) | copy-start | bytes 49156
  999.1 59.5 %copy-start.143 = (bf16[64,128]{1,0:T(8,128)(2,1)S(1)}, bf16[64,128]{1,0:T(8,128)(2,1)}, u32[]{:S(2)}) copy-start(bf16[64,128]{1,0:T(8,128)(2,1)} %copy-done.141) | copy-start | bytes 49156
  999.1 59.5 %copy-start.154 = (f32[64,36]{0,1:T(8,128)S(1)}, f32[64,36]{0,1:T(8,128)}, u32[]{:S(2)}) copy-start(f32[64,36]{0,1:T(8,128)} %fusion.132) | copy-start | bytes 27652
  999.1 59.7 %copy-start.103 = (f32[36,1152]{1,0:T(8,128)S(1)}, f32[36,1152]{1,0:T(8,128)}, u32[]{:S(2)}) copy-start(f32[36,1152]{1,0:T(8,128)} %fusion.163) | copy-start | bytes 497668
  999.1 59.7 %copy-start.104 = (f32[36,1001]{1,0:T(8,128)S(1)}, f32[36,1001]{1,0:T(8,128)}, u32[]{:S(2)}) copy-start(f32[36,1001]{1,0:T(8,128)} %fusion.64) | copy-start | bytes 432436
  1082.1 14.5 %copy-start.109 = (f32[87912]{0:T(1024)S(1)}, f32[87912]{0:T(1024)}, u32[]{:S(2)}) copy-start(f32[87912]{0:T(1024)} %param.36) | copy-start | bytes 1054948
  1082.1 14.5 %copy-start.110 = (f32[87912]{0:T(1024)S(1)}, f32[87912]{0:T(1024)}, u32[]{:S(2)}) copy-start(f32[87912]{0:T(1024)} %param.38) | copy-start | bytes 1054948
  1082.1 14.5 %copy-start.111 = (f32[87912]{0:T(1024)S(1)}, f32[87912]{0:T(1024)}, u32[]{:S(2)}) copy-start(f32[87912]{0:T(1024)} %param.37) | copy-start | bytes 1054948
  1082.1 15.7 %copy-start.87 = (f32[580608]{0:T(1024)S(1)}, f32[580608]{0:T(1024)}, u32[]{:S(2)}) copy-start(f32[580608]{0:T(1024)} %param.32) | copy-start | bytes 6967300
  1082.2 15.7 %copy-start.88 = (f32[580608]{0:T(1024)S(1)}, f32[580608]{0:T(1024)}, u32[]{:S(2)}) copy-start(f32[580608]{0:T(1024)} %param.34) | copy-start | bytes 6967300
  1082.2 15.7 %copy-start.89 = (f32[580608]{0:T(1024)S(1)}, f32[580608]{0:T(1024)}, u32[]{:S(2)}) copy-start(f32[580608]{0:T(1024)} %param.33) | copy-start | bytes 6967300
  (130 other events, 537.8 us)
Sparse Core Ops, SparseCore 0:
  420.9 88.5 all-gather.1
  560.6 142.6 reduce-scatter.4
  709.4 185.7 reduce-scatter.2

commit v6 on v5

--- a/solution.py
+++ b/solution.py
@@ -508,7 +508,8 @@
     )
 
 
-CHUNK_ROWS = 1152
+CHUNK_ROWS = 1088
+TAG_LANES = 64
 REST_ROWS = 2 * PD + FREQ + D + CLASSES + 1
 
 
@@ -629,11 +630,11 @@
 def pack_tags(pos, slot, fill, capacity):
     n = pos.shape[0]
     total = fill.shape[0] * capacity
-    lines = total // 128
-    here = (pos // 128)[:, None] == jnp.arange(lines)[None, :]
+    lines = total // TAG_LANES
+    here = (pos // TAG_LANES)[:, None] == jnp.arange(lines)[None, :]
     high = jnp.where(here, (slot // 128)[:, None], 0)
     low = jnp.where(here, (slot % 128)[:, None], 0)
-    lanes = ((pos % 128)[:, None] == jnp.arange(128)[None, :]).astype(jnp.bfloat16)
+    lanes = ((pos % TAG_LANES)[:, None] == jnp.arange(TAG_LANES)[None, :]).astype(jnp.bfloat16)
     parts = jnp.concatenate([high, low], axis=1).astype(jnp.bfloat16)
     found = contract(parts, lanes, 0, 0).astype(jnp.int32)
     tags = (found[:lines] * 128 + found[lines:]).reshape(fill.shape[0], capacity)
@@ -1672,7 +1673,7 @@
         arrays = [
             [told],
             [target.reshape(-1, 128)],
-            [new_tags.reshape(ranks, -1, 128)],
+            [new_tags.reshape(ranks, -1, TAG_LANES)],
             [buf.reshape(ranks, -1, 128)],
         ]
         kinds = ("share", "swap", "swap")

time: 1130 us -> 1130 us (level)
  no operation moved by 1% of the time
where the time goes in v6:
time: 1130 us; the launch traced here: 1120 us
  Pallas kernels  738 us (65%)
  matrix products  202 us (18%)
  local copies, waits for them, and re-layouts  93.3 us (8%)
  other arithmetic  49.4 us (4%)
  between operations  26.1 us (2%)
    pallas_call x4, Pallas kernels, travel(): pl.pallas_call(functools.partial(travel_kernel, jobs, [len(mine) for mine...  619 us
    dot_general x28, matrix products, product(): return jnp.dot(left, right, preferred_element_type=jnp.float32)  181 us
    pallas_call x4, Pallas kernels, attend_call(): pl.pallas_call(kernel, grid=(images, 4), out_shape=jax.ShapeDtypeStruct((...  48.9 us
    unnamed x348, local copies, waits for them, and re-layouts  43.7 us
    pallas_call x2, Pallas kernels, gather_rows(): pl.pallas_call(functools.partial(gather_kernel, total), out_shape=jax.Sha...  25.5 us
  transfers between devices with their start and end apart: 3, of which 0 were waited for; matrix products, arithmetic and copies ran while one was open for 20% of the time, Pallas kernels for 26%

profile of v6, /device:TPU:0, one launch (start us, length us, event | category | flops | bytes accessed | tf_op | source)
XLA Modules:
  0.0 1116.7 jit_solution(4187467331229152550)
XLA Ops:
  17.6 13.5 %pack_rows.7 = bf16[8704,128]{1,0:T(8,128)(2,1)S(1)} custom-call(s32[7776]{0:T(1024)S(1)} %get-tuple-element.619.pos_ref, bf16[7776,128]{1,0:T(8,128)(2,1)} %bitcast.284), custom_call_target="tpu_custom_call" | custom-call | tf_op jit(solution)/shard_map/pack_rows/pallas_call | solution.py:616
  33.7 53.1 %exchange_inputs.1 = (bf16[4,4,2,96,128]{4,3,2,1,0:T(8,128)(2,1)S(1)}, f32[8,64,128]{2,1,0:T(8,128)S(1)}, s32[8,17,64]{2,1,0:T(8,128)S(1)}, bf16[8,1088,128]{2,1,0:T(8,128)(2,1)S(1)}) custom-call(bf16[96,128]{1,0:T(8,128)(2,1)S(1)} %pad_bitcast_fusion.1.refs_0_, f32[64,128]{1,0:T(8,128)S(1)} %reshape.965.refs_1_, ...), custom_call_target="tpu_custom_call" | custom-call | tf_op jit(solution)/shard_map/exchange_inputs/pallas_call | solution.py:1091
  94.9 15.5 %scatter_rows.7 = bf16[7792,128]{1,0:T(8,128)(2,1)} custom-call(s32[8704]{0:T(1024)S(1)} %reshape.972.tag_ref.index_ref, bf16[8704,128]{1,0:T(8,128)(2,1)S(1)} %bitcast.278), custom_call_target="tpu_custom_call" | custom-call | tf_op jit(solution)/shard_map/scatter_rows/pallas_call | solution.py:646
  110.5 7.5 conditional.1
  118.0 5.4 spread_slots.1
  146.4 270.6 %gather_weights.1 = (bf16[4,2,144,3584]{3,2,1,0:T(8,128)(2,1)}, bf16[4,4,2,48,1152]{4,3,2,1,0:T(8,128)(2,1)S(1)}, bf16[4,2,144,4608]{3,2,1,0:T(8,128)(2,1)}, bf1...) custom-call(bf16[144,896]{1,0:T(8,128)(2,1)S(1)} %copy-done.29, ...), custom_call_target="tpu_custom_call" | custom-call | tf_op jit(solution)/shard_map/gather_weights/pallas_call | solution.py:1091
  454.3 5.9 convolution_convert_fusion.9.packed_ref
  460.2 8.5 attend.2
  472.5 10.5 multiply_convert_fusion.2
  494.9 13.7 %attend.3 = bf16[512,1536]{1,0:T(8,128)(2,1)S(1)} custom-call(bf16[512,3584]{1,0:T(8,128)(2,1)S(1)} %convolution_convert_fusion.8.packed_ref), custom_call_target="tpu_custom_call" | custom-call | tf_op jit(solution)/shard_map/attend/pallas_call | solution.py:1462
  514.7 12.6 %fusion.189 = f32[512,4608]{1,0:T(8,128)} fusion(bf16[512,1152]{1,0:T(8,128)(2,1)S(1)} %bitcast.306, bf16[1152,4608]{1,0:T(8,128)(2,1)} %bitcast.361), kind=kOutput, calls=%fused_computation.495 | convolution fusion | flops 5435817984 | bytes 21233664 | tf_op jit(solution)/shard_map/dot_general | solution.py:42
  527.3 12.5 %fusion.169 = f32[512,1152]{1,0:T(8,128)S(1)} fusion(bf16[4608,1152]{1,0:T(8,128)(2,1)} %all-gather.2.cloned.1.call-done, f32[512,4608]{1,0:T(8,128)} %fusion.189), kind=kOutput, calls=%fused_computation.479 | convolution fusion | flops 5457051648 | bytes 22413312 | tf_op jit(solution)/shard_map/dot_general | solution.py:42
  547.4 10.0 convolution_convert_fusion
  561.2 16.0 %multiply_convert_fusion = bf16[512,4608]{1,0:T(8,128)(2,1)} fusion(f32[512,4608]{1,0:T(8,128)} %fusion.189, bf16[512,1152]{1,0:T(8,128)(2,1)} %bitcast.311, bf16[4608,1152]{1,0:T(8,128)(2,1)} %all-gather.2.cloned.1.call-done), kind=kOutput, calls=%fused_computation.85 | convolution fusion | flops 5478285312 | bytes 25952256 | tf_op jit(solution)/shard_map/dot_general | solution.py:42
  577.2 13.3 %multiply_reduce_fusion.4 = (bf16[2,1152]{1,0:T(2,128)(2,1)S(1)}, f32[2,256]{1,0:T(2,128)S(1)}, f32[2,256]{1,0:T(2,128)S(1)}, bf16[2,1152]{1,0:T(2,128)(2,1)S(1)}, f32[2,256,1152]{2,1,0:T(8,128)}) fusion(f32[2,256,1152]{2,1,0:T(8,128)S(1)} %copy-done.54, f32[2,256]{1,0:T(2,128)S(1)} %add_rsqrt_fusion.1, f32[2,256]{1,0:T(2,128)S(1)} %broadcast_multiply_fusion.10, ...), kind=kOutput, calls=%fused_computation.119 | convolution fusion | flops 5441121280 | bytes 20080640 | tf_op jit(solution)/shard_map/dot_general | solution.py:42
  598.2 17.9 %attend_back.2 = bf16[512,3584]{1,0:T(8,128)(2,1)S(1)} custom-call(bf16[512,3584]{1,0:T(8,128)(2,1)} %copy-done, bf16[512,1536]{1,0:T(8,128)(2,1)S(1)} %convolution_convert_fusion.10.grad_ref, bf16[4,72,384]{2,1,0:T(8,128)(2,1)S(1)} %compare_convert_fusion.spread_ref), custom_call_target="tpu_custom_call" | custom-call | tf_op jit(solution)/shard_map/attend_back/pallas_call | solution.py:1462
  616.1 10.0 multiply_reduce_fusion.6
  629.4 5.8 convolution_convert_fusion.1
  635.2 9.1 fusion.31
  647.7 8.9 multiply_reduce_fusion.18
  660.9 8.7 attend_back.3
  669.7 7.0 multiply_reduce_fusion.16
  690.4 5.6 convolution_convert_fusion.5
  696.0 5.7 convolution_convert_fusion.3
  701.8 8.6 convolution_convert_fusion.2
  710.4 6.7 convolution_convert_fusion.4
  717.1 239.7 %sum_gradients.1 = (f32[144,896]{1,0:T(8,128)S(1)}, f32[48,1152]{1,0:T(8,128)S(1)}, f32[144,1152]{1,0:T(8,128)S(1)}, f32[144,896]{1,0:T(8,128)S(1)}, f32[48,1152...) custom-call(bf16[4,2,144,3584]{3,2,1,0:T(8,128)(2,1)} %bitcast.287, ...), custom_call_target="tpu_custom_call" | custom-call | tf_op jit(solution)/shard_map/sum_gradients/pallas_call | solution.py:1091
  985.6 11.0 gather_rows.14
  996.7 55.5 %sum_shared.1 = (f32[32,128]{1,0:T(8,128)S(1)}, bf16[8,1088,128]{2,1,0:T(8,128)(2,1)S(1)}) custom-call(f32[4,4,2,32,128]{4,3,2,1,0:T(8,128)S(1)} %bitcast.279, bf16[8,1088,128]{2,1,0:T(8,128)(2,1)S(1)} %bitcast.272), custom_call_target="tpu_custom_call" | custom-call | tf_op jit(solution)/shard_map/sum_shared/pallas_call | solution.py:1091
  1057.0 9.6 push_totals.1
  1076.2 14.5 %gather_rows.15 = f32[7776,128]{1,0:T(8,128)} custom-call(s32[7776]{0:T(1024)S(1)} %copy-done.36, f32[8704,128]{1,0:T(8,128)S(1)} %bitcast_convert_fusion.1.x_ref), custom_call_target="tpu_custom_call" | custom-call | tf_op jit(solution)/shard_map/gather_rows/pallas_call | solution.py:662
  1097.5 11.1 fusion.174
  (535 shorter events, 186.5 us)
Async XLA Ops:
  7.2 520.1 %all-gather.2.cloned.1.call-start = ((), (), s32[]{:S(2)}) async-start(), calls=%async_computation.6 | async-start | bytes 10948608 | tf_op jit(solution)/shard_map/all_gather | solution.py:1724
  8.9 101.5 %copy-start.65 = (s32[7776]{0:T(1024)}, s32[7776]{0:T(1024)S(1)}, u32[]{:S(2)}) copy-start(s32[7776]{0:T(1024)S(1)} %get-tuple-element.935) | copy-start | bytes 93316
  8.9 101.5 %copy-start.67 = (s32[7776]{0:T(1024)}, s32[7776]{0:T(1024)S(1)}, u32[]{:S(2)}) copy-start(s32[7776]{0:T(1024)S(1)} %get-tuple-element.938) | copy-start | bytes 93316
  9.2 101.2 %copy-start.151 = (s32[8]{0:T(128)}, s32[8]{0:T(128)S(1)}, u32[]{:S(2)}) copy-start(s32[8]{0:T(128)S(1)} %convert_element_type.262) | copy-start | bytes 100
  10.5 120.8 %copy-start.101 = (bf16[36,2442]{1,0:T(8,128)(2,1)}, bf16[36,2442]{1,0:T(8,128)(2,1)S(1)}, u32[]{:S(2)}) copy-start(bf16[36,2442]{1,0:T(8,128)(2,1)S(1)} %reshape.961) | copy-start | bytes 527476
  16.3 94.1 %copy-start.62 = (s32[7776]{0:T(1024)}, s32[7776]{0:T(1024)S(1)}, u32[]{:S(2)}) copy-start(s32[7776]{0:T(1024)S(1)} %convert_element_type.264) | copy-start | bytes 93316
  94.7 36.5 %copy-start.147 = (s32[64]{0:T(128)}, s32[64]{0:T(128)S(1)}, u32[]{:S(2)}) copy-start(s32[64]{0:T(128)S(1)} %eq.269) | copy-start | bytes 772
  94.9 15.5 %copy-start.26 = (s32[8704]{0:T(1024)}, s32[8704]{0:T(1024)S(1)}, u32[]{:S(2)}) copy-start(s32[8704]{0:T(1024)S(1)} %reshape.972.tag_ref.index_ref) | copy-start | bytes 104452
  146.4 277.0 %copy-start.136 = (f32[2,1,128,16]{2,3,1,0:T(8,128)S(1)}, f32[2,1,128,16]{2,3,1,0:T(8,128)}, u32[]{:S(2)}) copy-start(f32[2,1,128,16]{2,3,1,0:T(8,128)} %param.40) | copy-start | bytes 49156
  417.7 51.5 %copy-start.7 = (bf16[4,4,2,48,1152]{4,3,2,1,0:T(8,128)(2,1)}, bf16[4,4,2,48,1152]{4,3,2,1,0:T(8,128)(2,1)S(1)}, u32[]{:S(2)}) copy-start(bf16[4,4,2,48,1152]{4,3,2,1,0:T(8,128)(2,1)S(1)} %get-tuple-element.514) | copy-start | bytes 10616836
  417.7 562.6 %reduce-scatter.5.cloned.1.call-start = ((), (), s32[]{:S(2)}) async-start(), calls=%async_computation.8 | async-start | bytes 10948608 | tf_op jit(solution)/shard_map/reduce_scatter | solution.py:1772
  471.8 14.5 %copy-start.55 = (f32[2,128,1152]{2,1,0:T(8,128)}, f32[2,128,1152]{2,1,0:T(8,128)S(1)}, u32[]{:S(2)}) copy-start(f32[2,128,1152]{2,1,0:T(8,128)S(1)} %get-tuple-element.633) | copy-start | bytes 3538948
  472.2 17.5 %slice-start.3 = ((s8[8257536]{0:T(1024)(128)(4,1)}), s8[4194304]{0:T(1024)(128)(4,1)S(1)}, s32[]{:S(2)}) async-start(s8[8257536]{0:T(1024)(128)(4,1)} %bitcast.366), calls=%async_computation.12 | async-start | bytes 8388608
  472.5 17.1 %slice-start.4 = ((s8[8257536]{0:T(1024)(128)(4,1)}), s8[4063232]{0:T(1024)(128)(4,1)S(1)}, s32[]{:S(2)}) async-start(s8[8257536]{0:T(1024)(128)(4,1)} %bitcast.366), calls=%async_computation.13 | async-start | bytes 8126464
  487.4 21.2 %copy-start.50 = (f32[2,256,1152]{2,1,0:T(8,128)}, f32[2,256,1152]{2,1,0:T(8,128)S(1)}, u32[]{:S(2)}) copy-start(f32[2,256,1152]{2,1,0:T(8,128)S(1)} %get-tuple-element.699) | copy-start | bytes 7077892
  494.8 13.7 %copy-start = (bf16[512,3584]{1,0:T(8,128)(2,1)}, bf16[512,3584]{1,0:T(8,128)(2,1)S(1)}, u32[]{:S(2)}) copy-start(bf16[512,3584]{1,0:T(8,128)(2,1)S(1)} %convolution_convert_fusion.8.packed_ref) | copy-start | bytes 11010052
  494.8 13.8 %copy-start.129 = (f32[1,2,1152]{2,1,0:T(2,128)S(1)}, f32[1,2,1152]{2,1,0:T(2,128)}, u32[]{:S(2)}) copy-start(f32[1,2,1152]{2,1,0:T(2,128)} %copy.284) | copy-start | bytes 27652
  494.9 13.8 %copy-start.149 = (bf16[4,4,2,48,1152]{4,3,2,1,0:T(8,128)(2,1)S(1)}, bf16[4,4,2,48,1152]{4,3,2,1,0:T(8,128)(2,1)}, u32[]{:S(2)}) copy-start(bf16[4,4,2,48,1152]{4,3,2,1,0:T(8,128)(2,1)} %get-tuple-element.518) | copy-start | bytes 10616836
  557.5 423.9 %reduce-scatter.3.cloned.1.call-start = ((), (), s32[]{:S(2)}) async-start(), calls=%async_computation.7 | async-start | bytes 10948608 | tf_op jit(solution)/shard_map/reduce_scatter | solution.py:1783
  561.2 16.0 %copy-start.54 = (f32[2,256,1152]{2,1,0:T(8,128)S(1)}, f32[2,256,1152]{2,1,0:T(8,128)}, u32[]{:S(2)}) copy-start(f32[2,256,1152]{2,1,0:T(8,128)} %copy-done.52) | copy-start | bytes 7077892
  598.2 17.9 %copy-start.51 = (f32[2,256,1152]{2,1,0:T(8,128)S(1)}, f32[2,256,1152]{2,1,0:T(8,128)}, u32[]{:S(2)}) copy-start(f32[2,256,1152]{2,1,0:T(8,128)} %copy-done.50) | copy-start | bytes 7077892
  996.6 56.0 %copy-start.139 = (bf16[64,128]{1,0:T(8,128)(2,1)S(1)}, bf16[64,128]{1,0:T(8,128)(2,1)}, u32[]{:S(2)}) copy-start(bf16[64,128]{1,0:T(8,128)(2,1)} %copy-done.137) | copy-start | bytes 49156
  996.6 56.0 %copy-start.142 = (bf16[64,128]{1,0:T(8,128)(2,1)S(1)}, bf16[64,128]{1,0:T(8,128)(2,1)}, u32[]{:S(2)}) copy-start(bf16[64,128]{1,0:T(8,128)(2,1)} %copy-done.140) | copy-start | bytes 49156
  996.7 56.0 %copy-start.153 = (f32[64,36]{0,1:T(8,128)S(1)}, f32[64,36]{0,1:T(8,128)}, u32[]{:S(2)}) copy-start(f32[64,36]{0,1:T(8,128)} %fusion.135) | copy-start | bytes 27652
  996.7 56.2 %copy-start.102 = (f32[36,1152]{1,0:T(8,128)S(1)}, f32[36,1152]{1,0:T(8,128)}, u32[]{:S(2)}) copy-start(f32[36,1152]{1,0:T(8,128)} %fusion.166) | copy-start | bytes 497668
  996.7 56.2 %copy-start.103 = (f32[36,1001]{1,0:T(8,128)S(1)}, f32[36,1001]{1,0:T(8,128)}, u32[]{:S(2)}) copy-start(f32[36,1001]{1,0:T(8,128)} %fusion.67) | copy-start | bytes 432436
  1076.2 14.5 %copy-start.108 = (f32[87912]{0:T(1024)S(1)}, f32[87912]{0:T(1024)}, u32[]{:S(2)}) copy-start(f32[87912]{0:T(1024)} %param.36) | copy-start | bytes 1054948
  1076.2 14.5 %copy-start.109 = (f32[87912]{0:T(1024)S(1)}, f32[87912]{0:T(1024)}, u32[]{:S(2)}) copy-start(f32[87912]{0:T(1024)} %param.38) | copy-start | bytes 1054948
  1076.2 14.5 %copy-start.110 = (f32[87912]{0:T(1024)S(1)}, f32[87912]{0:T(1024)}, u32[]{:S(2)}) copy-start(f32[87912]{0:T(1024)} %param.37) | copy-start | bytes 1054948
  1076.2 15.7 %copy-start.87 = (f32[580608]{0:T(1024)S(1)}, f32[580608]{0:T(1024)}, u32[]{:S(2)}) copy-start(f32[580608]{0:T(1024)} %param.32) | copy-start | bytes 6967300
  1076.2 15.7 %copy-start.88 = (f32[580608]{0:T(1024)S(1)}, f32[580608]{0:T(1024)}, u32[]{:S(2)}) copy-start(f32[580608]{0:T(1024)} %param.34) | copy-start | bytes 6967300
  1076.2 15.7 %copy-start.89 = (f32[580608]{0:T(1024)S(1)}, f32[580608]{0:T(1024)}, u32[]{:S(2)}) copy-start(f32[580608]{0:T(1024)} %param.33) | copy-start | bytes 6967300
  (130 other events, 550.0 us)
Sparse Core Ops, SparseCore 0:
  417.8 88.5 all-gather.1
  557.6 142.7 reduce-scatter.4
  706.5 187.2 reduce-scatter.2

commit v7 on v6

--- a/solution.py
+++ b/solution.py
@@ -1248,6 +1248,9 @@
     return places
 
 
+SPARE_ROWS = 24
+
+
 def row_group(width):
     rows = 128 // math.gcd(width, 128)
     return rows, rows * width // 128
@@ -1343,7 +1346,7 @@
         in_specs=[VMEM],
         out_specs=[VMEM] * len(plan),
         scratch_shapes=[
-            pltpu.VMEM((broad // 128, tall, 128), jnp.float32),
+            pltpu.VMEM((broad // 128, tall + SPARE_ROWS, 128), jnp.float32),
             pltpu.VMEM(slots.shape, jnp.float32),
         ],
         compiler_params=PARAMS,
@@ -1362,7 +1365,7 @@
         ),
         in_specs=[VMEM] * len(parts),
         out_specs=(VMEM, VMEM),
-        scratch_shapes=[pltpu.VMEM((broad // 128, tall, 128), jnp.float32)],
+        scratch_shapes=[pltpu.VMEM((broad // 128, tall + SPARE_ROWS, 128), jnp.float32)],
         compiler_params=PARAMS,
         name="collect_slots",
     )(*parts)

time: 1130 us -> 1130 us (level)
  no operation moved by 1% of the time
where the time goes in v7:
time: 1130 us; the launch traced here: 1120 us
  Pallas kernels  740 us (65%)
  matrix products  202 us (18%)
  local copies, waits for them, and re-layouts  93.3 us (8%)
  other arithmetic  49.4 us (4%)
  between operations  26.1 us (2%)
    pallas_call x4, Pallas kernels, travel(): pl.pallas_call(functools.partial(travel_kernel, jobs, [len(mine) for mine...  620 us
    dot_general x28, matrix products, product(): return jnp.dot(left, right, preferred_element_type=jnp.float32)  181 us
    pallas_call x4, Pallas kernels, attend_call(): pl.pallas_call(kernel, grid=(images, 4), out_shape=jax.ShapeDtypeStruct((...  48.9 us
    unnamed x348, local copies, waits for them, and re-layouts  43.7 us
    pallas_call x2, Pallas kernels, gather_rows(): pl.pallas_call(functools.partial(gather_kernel, total), out_shape=jax.Sha...  25.5 us
  transfers between devices with their start and end apart: 3, of which 0 were waited for; matrix products, arithmetic and copies ran while one was open for 20% of the time, Pallas kernels for 26%

profile of v7, /device:TPU:0, one launch (start us, length us, event | category | flops | bytes accessed | tf_op | source)
XLA Modules:
  0.0 1118.0 jit_solution(18277320375987695348)
XLA Ops:
  17.6 13.5 %pack_rows.7 = bf16[8704,128]{1,0:T(8,128)(2,1)S(1)} custom-call(s32[7776]{0:T(1024)S(1)} %get-tuple-element.619.pos_ref, bf16[7776,128]{1,0:T(8,128)(2,1)} %bitcast.284), custom_call_target="tpu_custom_call" | custom-call | tf_op jit(solution)/shard_map/pack_rows/pallas_call | solution.py:616
  33.7 53.1 %exchange_inputs.1 = (bf16[4,4,2,96,128]{4,3,2,1,0:T(8,128)(2,1)S(1)}, f32[8,64,128]{2,1,0:T(8,128)S(1)}, s32[8,17,64]{2,1,0:T(8,128)S(1)}, bf16[8,1088,128]{2,1,0:T(8,128)(2,1)S(1)}) custom-call(bf16[96,128]{1,0:T(8,128)(2,1)S(1)} %pad_bitcast_fusion.1.refs_0_, f32[64,128]{1,0:T(8,128)S(1)} %reshape.965.refs_1_, ...), custom_call_target="tpu_custom_call" | custom-call | tf_op jit(solution)/shard_map/exchange_inputs/pallas_call | solution.py:1091
  94.9 15.5 %scatter_rows.7 = bf16[7792,128]{1,0:T(8,128)(2,1)} custom-call(s32[8704]{0:T(1024)S(1)} %reshape.972.tag_ref.index_ref, bf16[8704,128]{1,0:T(8,128)(2,1)S(1)} %bitcast.278), custom_call_target="tpu_custom_call" | custom-call | tf_op jit(solution)/shard_map/scatter_rows/pallas_call | solution.py:646
  110.5 7.5 conditional.1
  118.0 5.4 spread_slots.1
  146.4 270.6 %gather_weights.1 = (bf16[4,2,144,3584]{3,2,1,0:T(8,128)(2,1)}, bf16[4,4,2,48,1152]{4,3,2,1,0:T(8,128)(2,1)S(1)}, bf16[4,2,144,4608]{3,2,1,0:T(8,128)(2,1)}, bf1...) custom-call(bf16[144,896]{1,0:T(8,128)(2,1)S(1)} %copy-done.29, ...), custom_call_target="tpu_custom_call" | custom-call | tf_op jit(solution)/shard_map/gather_weights/pallas_call | solution.py:1091
  454.3 5.9 convolution_convert_fusion.9.packed_ref
  460.2 8.6 attend.2
  472.6 10.5 multiply_convert_fusion.2
  494.9 13.7 %attend.3 = bf16[512,1536]{1,0:T(8,128)(2,1)S(1)} custom-call(bf16[512,3584]{1,0:T(8,128)(2,1)S(1)} %convolution_convert_fusion.8.packed_ref), custom_call_target="tpu_custom_call" | custom-call | tf_op jit(solution)/shard_map/attend/pallas_call | solution.py:1465
  514.7 12.6 %fusion.189 = f32[512,4608]{1,0:T(8,128)} fusion(bf16[512,1152]{1,0:T(8,128)(2,1)S(1)} %bitcast.306, bf16[1152,4608]{1,0:T(8,128)(2,1)} %bitcast.361), kind=kOutput, calls=%fused_computation.495 | convolution fusion | flops 5435817984 | bytes 21233664 | tf_op jit(solution)/shard_map/dot_general | solution.py:42
  527.3 12.5 %fusion.169 = f32[512,1152]{1,0:T(8,128)S(1)} fusion(bf16[4608,1152]{1,0:T(8,128)(2,1)} %all-gather.2.cloned.1.call-done, f32[512,4608]{1,0:T(8,128)} %fusion.189), kind=kOutput, calls=%fused_computation.479 | convolution fusion | flops 5457051648 | bytes 22413312 | tf_op jit(solution)/shard_map/dot_general | solution.py:42
  547.5 10.0 convolution_convert_fusion
  561.2 16.0 %multiply_convert_fusion = bf16[512,4608]{1,0:T(8,128)(2,1)} fusion(f32[512,4608]{1,0:T(8,128)} %fusion.189, bf16[512,1152]{1,0:T(8,128)(2,1)} %bitcast.311, bf16[4608,1152]{1,0:T(8,128)(2,1)} %all-gather.2.cloned.1.call-done), kind=kOutput, calls=%fused_computation.85 | convolution fusion | flops 5478285312 | bytes 25952256 | tf_op jit(solution)/shard_map/dot_general | solution.py:42
  577.2 13.3 %multiply_reduce_fusion.4 = (bf16[2,1152]{1,0:T(2,128)(2,1)S(1)}, f32[2,256]{1,0:T(2,128)S(1)}, f32[2,256]{1,0:T(2,128)S(1)}, bf16[2,1152]{1,0:T(2,128)(2,1)S(1)}, f32[2,256,1152]{2,1,0:T(8,128)}) fusion(f32[2,256,1152]{2,1,0:T(8,128)S(1)} %copy-done.54, f32[2,256]{1,0:T(2,128)S(1)} %add_rsqrt_fusion.1, f32[2,256]{1,0:T(2,128)S(1)} %broadcast_multiply_fusion.10, ...), kind=kOutput, calls=%fused_computation.119 | convolution fusion | flops 5441121280 | bytes 20080640 | tf_op jit(solution)/shard_map/dot_general | solution.py:42
  598.2 17.9 %attend_back.2 = bf16[512,3584]{1,0:T(8,128)(2,1)S(1)} custom-call(bf16[512,3584]{1,0:T(8,128)(2,1)} %copy-done, bf16[512,1536]{1,0:T(8,128)(2,1)S(1)} %convolution_convert_fusion.10.grad_ref, bf16[4,72,384]{2,1,0:T(8,128)(2,1)S(1)} %compare_convert_fusion.spread_ref), custom_call_target="tpu_custom_call" | custom-call | tf_op jit(solution)/shard_map/attend_back/pallas_call | solution.py:1465
  616.2 10.0 multiply_reduce_fusion.6
  629.4 5.8 convolution_convert_fusion.1
  635.3 9.1 fusion.31
  647.8 8.9 multiply_reduce_fusion.18
  660.9 8.7 attend_back.3
  669.7 7.0 multiply_reduce_fusion.16
  690.4 5.6 convolution_convert_fusion.5
  696.0 5.7 convolution_convert_fusion.3
  701.8 8.6 convolution_convert_fusion.2
  710.4 6.7 convolution_convert_fusion.4
  717.1 239.0 %sum_gradients.1 = (f32[144,896]{1,0:T(8,128)S(1)}, f32[48,1152]{1,0:T(8,128)S(1)}, f32[144,1152]{1,0:T(8,128)S(1)}, f32[144,896]{1,0:T(8,128)S(1)}, f32[48,1152...) custom-call(bf16[4,2,144,3584]{3,2,1,0:T(8,128)(2,1)} %bitcast.287, ...), custom_call_target="tpu_custom_call" | custom-call | tf_op jit(solution)/shard_map/sum_gradients/pallas_call | solution.py:1091
  984.9 11.0 gather_rows.14
  995.9 57.6 %sum_shared.1 = (f32[32,128]{1,0:T(8,128)S(1)}, bf16[8,1088,128]{2,1,0:T(8,128)(2,1)S(1)}) custom-call(f32[4,4,2,32,128]{4,3,2,1,0:T(8,128)S(1)} %bitcast.279, bf16[8,1088,128]{2,1,0:T(8,128)(2,1)S(1)} %bitcast.272), custom_call_target="tpu_custom_call" | custom-call | tf_op jit(solution)/shard_map/sum_shared/pallas_call | solution.py:1091
  1058.4 9.6 push_totals.1
  1077.6 14.5 %gather_rows.15 = f32[7776,128]{1,0:T(8,128)} custom-call(s32[7776]{0:T(1024)S(1)} %copy-done.36, f32[8704,128]{1,0:T(8,128)S(1)} %bitcast_convert_fusion.1.x_ref), custom_call_target="tpu_custom_call" | custom-call | tf_op jit(solution)/shard_map/gather_rows/pallas_call | solution.py:662
  1098.9 11.1 fusion.174
  (535 shorter events, 186.5 us)
Async XLA Ops:
  7.2 520.1 %all-gather.2.cloned.1.call-start = ((), (), s32[]{:S(2)}) async-start(), calls=%async_computation.6 | async-start | bytes 10948608 | tf_op jit(solution)/shard_map/all_gather | solution.py:1727
  8.9 101.5 %copy-start.65 = (s32[7776]{0:T(1024)}, s32[7776]{0:T(1024)S(1)}, u32[]{:S(2)}) copy-start(s32[7776]{0:T(1024)S(1)} %get-tuple-element.935) | copy-start | bytes 93316
  8.9 101.5 %copy-start.67 = (s32[7776]{0:T(1024)}, s32[7776]{0:T(1024)S(1)}, u32[]{:S(2)}) copy-start(s32[7776]{0:T(1024)S(1)} %get-tuple-element.938) | copy-start | bytes 93316
  9.2 101.2 %copy-start.151 = (s32[8]{0:T(128)}, s32[8]{0:T(128)S(1)}, u32[]{:S(2)}) copy-start(s32[8]{0:T(128)S(1)} %convert_element_type.262) | copy-start | bytes 100
  10.5 120.8 %copy-start.101 = (bf16[36,2442]{1,0:T(8,128)(2,1)}, bf16[36,2442]{1,0:T(8,128)(2,1)S(1)}, u32[]{:S(2)}) copy-start(bf16[36,2442]{1,0:T(8,128)(2,1)S(1)} %reshape.961) | copy-start | bytes 527476
  16.3 94.1 %copy-start.62 = (s32[7776]{0:T(1024)}, s32[7776]{0:T(1024)S(1)}, u32[]{:S(2)}) copy-start(s32[7776]{0:T(1024)S(1)} %convert_element_type.264) | copy-start | bytes 93316
  94.7 36.6 %copy-start.147 = (s32[64]{0:T(128)}, s32[64]{0:T(128)S(1)}, u32[]{:S(2)}) copy-start(s32[64]{0:T(128)S(1)} %eq.269) | copy-start | bytes 772
  94.9 15.5 %copy-start.26 = (s32[8704]{0:T(1024)}, s32[8704]{0:T(1024)S(1)}, u32[]{:S(2)}) copy-start(s32[8704]{0:T(1024)S(1)} %reshape.972.tag_ref.index_ref) | copy-start | bytes 104452
  146.4 277.1 %copy-start.136 = (f32[2,1,128,16]{2,3,1,0:T(8,128)S(1)}, f32[2,1,128,16]{2,3,1,0:T(8,128)}, u32[]{:S(2)}) copy-start(f32[2,1,128,16]{2,3,1,0:T(8,128)} %param.40) | copy-start | bytes 49156
  417.7 51.6 %copy-start.7 = (bf16[4,4,2,48,1152]{4,3,2,1,0:T(8,128)(2,1)}, bf16[4,4,2,48,1152]{4,3,2,1,0:T(8,128)(2,1)S(1)}, u32[]{:S(2)}) copy-start(bf16[4,4,2,48,1152]{4,3,2,1,0:T(8,128)(2,1)S(1)} %get-tuple-element.514) | copy-start | bytes 10616836
  417.7 561.9 %reduce-scatter.5.cloned.1.call-start = ((), (), s32[]{:S(2)}) async-start(), calls=%async_computation.8 | async-start | bytes 10948608 | tf_op jit(solution)/shard_map/reduce_scatter | solution.py:1775
  471.8 14.5 %copy-start.55 = (f32[2,128,1152]{2,1,0:T(8,128)}, f32[2,128,1152]{2,1,0:T(8,128)S(1)}, u32[]{:S(2)}) copy-start(f32[2,128,1152]{2,1,0:T(8,128)S(1)} %get-tuple-element.633) | copy-start | bytes 3538948
  472.2 17.5 %slice-start.3 = ((s8[8257536]{0:T(1024)(128)(4,1)}), s8[4194304]{0:T(1024)(128)(4,1)S(1)}, s32[]{:S(2)}) async-start(s8[8257536]{0:T(1024)(128)(4,1)} %bitcast.366), calls=%async_computation.12 | async-start | bytes 8388608
  472.5 17.1 %slice-start.4 = ((s8[8257536]{0:T(1024)(128)(4,1)}), s8[4063232]{0:T(1024)(128)(4,1)S(1)}, s32[]{:S(2)}) async-start(s8[8257536]{0:T(1024)(128)(4,1)} %bitcast.366), calls=%async_computation.13 | async-start | bytes 8126464
  487.4 21.2 %copy-start.50 = (f32[2,256,1152]{2,1,0:T(8,128)}, f32[2,256,1152]{2,1,0:T(8,128)S(1)}, u32[]{:S(2)}) copy-start(f32[2,256,1152]{2,1,0:T(8,128)S(1)} %get-tuple-element.699) | copy-start | bytes 7077892
  494.8 13.7 %copy-start = (bf16[512,3584]{1,0:T(8,128)(2,1)}, bf16[512,3584]{1,0:T(8,128)(2,1)S(1)}, u32[]{:S(2)}) copy-start(bf16[512,3584]{1,0:T(8,128)(2,1)S(1)} %convolution_convert_fusion.8.packed_ref) | copy-start | bytes 11010052
  494.9 13.8 %copy-start.129 = (f32[1,2,1152]{2,1,0:T(2,128)S(1)}, f32[1,2,1152]{2,1,0:T(2,128)}, u32[]{:S(2)}) copy-start(f32[1,2,1152]{2,1,0:T(2,128)} %copy.284) | copy-start | bytes 27652
  494.9 13.8 %copy-start.149 = (bf16[4,4,2,48,1152]{4,3,2,1,0:T(8,128)(2,1)S(1)}, bf16[4,4,2,48,1152]{4,3,2,1,0:T(8,128)(2,1)}, u32[]{:S(2)}) copy-start(bf16[4,4,2,48,1152]{4,3,2,1,0:T(8,128)(2,1)} %get-tuple-element.518) | copy-start | bytes 10616836
  557.5 423.1 %reduce-scatter.3.cloned.1.call-start = ((), (), s32[]{:S(2)}) async-start(), calls=%async_computation.7 | async-start | bytes 10948608 | tf_op jit(solution)/shard_map/reduce_scatter | solution.py:1786
  561.2 16.0 %copy-start.54 = (f32[2,256,1152]{2,1,0:T(8,128)S(1)}, f32[2,256,1152]{2,1,0:T(8,128)}, u32[]{:S(2)}) copy-start(f32[2,256,1152]{2,1,0:T(8,128)} %copy-done.52) | copy-start | bytes 7077892
  598.2 17.9 %copy-start.51 = (f32[2,256,1152]{2,1,0:T(8,128)S(1)}, f32[2,256,1152]{2,1,0:T(8,128)}, u32[]{:S(2)}) copy-start(f32[2,256,1152]{2,1,0:T(8,128)} %copy-done.50) | copy-start | bytes 7077892
  995.9 58.1 %copy-start.139 = (bf16[64,128]{1,0:T(8,128)(2,1)S(1)}, bf16[64,128]{1,0:T(8,128)(2,1)}, u32[]{:S(2)}) copy-start(bf16[64,128]{1,0:T(8,128)(2,1)} %copy-done.137) | copy-start | bytes 49156
  995.9 58.1 %copy-start.142 = (bf16[64,128]{1,0:T(8,128)(2,1)S(1)}, bf16[64,128]{1,0:T(8,128)(2,1)}, u32[]{:S(2)}) copy-start(bf16[64,128]{1,0:T(8,128)(2,1)} %copy-done.140) | copy-start | bytes 49156
  995.9 58.1 %copy-start.153 = (f32[64,36]{0,1:T(8,128)S(1)}, f32[64,36]{0,1:T(8,128)}, u32[]{:S(2)}) copy-start(f32[64,36]{0,1:T(8,128)} %fusion.135) | copy-start | bytes 27652
  995.9 58.3 %copy-start.102 = (f32[36,1152]{1,0:T(8,128)S(1)}, f32[36,1152]{1,0:T(8,128)}, u32[]{:S(2)}) copy-start(f32[36,1152]{1,0:T(8,128)} %fusion.166) | copy-start | bytes 497668
  995.9 58.3 %copy-start.103 = (f32[36,1001]{1,0:T(8,128)S(1)}, f32[36,1001]{1,0:T(8,128)}, u32[]{:S(2)}) copy-start(f32[36,1001]{1,0:T(8,128)} %fusion.67) | copy-start | bytes 432436
  1077.5 14.5 %copy-start.108 = (f32[87912]{0:T(1024)S(1)}, f32[87912]{0:T(1024)}, u32[]{:S(2)}) copy-start(f32[87912]{0:T(1024)} %param.36) | copy-start | bytes 1054948
  1077.6 14.5 %copy-start.109 = (f32[87912]{0:T(1024)S(1)}, f32[87912]{0:T(1024)}, u32[]{:S(2)}) copy-start(f32[87912]{0:T(1024)} %param.38) | copy-start | bytes 1054948
  1077.6 14.5 %copy-start.110 = (f32[87912]{0:T(1024)S(1)}, f32[87912]{0:T(1024)}, u32[]{:S(2)}) copy-start(f32[87912]{0:T(1024)} %param.37) | copy-start | bytes 1054948
  1077.6 15.7 %copy-start.87 = (f32[580608]{0:T(1024)S(1)}, f32[580608]{0:T(1024)}, u32[]{:S(2)}) copy-start(f32[580608]{0:T(1024)} %param.32) | copy-start | bytes 6967300
  1077.6 15.7 %copy-start.88 = (f32[580608]{0:T(1024)S(1)}, f32[580608]{0:T(1024)}, u32[]{:S(2)}) copy-start(f32[580608]{0:T(1024)} %param.34) | copy-start | bytes 6967300
  1077.6 15.7 %copy-start.89 = (f32[580608]{0:T(1024)S(1)}, f32[580608]{0:T(1024)}, u32[]{:S(2)}) copy-start(f32[580608]{0:T(1024)} %param.33) | copy-start | bytes 6967300
  (130 other events, 550.1 us)
Sparse Core Ops, SparseCore 0:
  417.8 88.5 all-gather.1
  557.6 142.6 reduce-scatter.4
  706.4 187.3 reduce-scatter.2
